TPU v7x, 128 devices: a whole 4x4x4 slice. The times are simulated.
128 devices in a mesh: blk: 16 (over x_lo, y, core), grp: 8 (over z, x_hi).
Axes of the slice: x: 4 (x_hi: 2, x_lo: 2; x = x_hi * 2 + x_lo), y: 4, z: 4, core: 2. Of those that a mesh axis runs over, the one named last changes fastest.
Arguments:
- picture_vectors: bfloat16 [16384, 1152], P(('blk', 'grp')), may hold values from -6 to 6
- caption_vectors: bfloat16 [16384, 1152], P(('blk', 'grp')), may hold values from -6 to 6
- ln_inverse_warmth: float32 [], replicated, may hold values from 1.6 to 2.7
- score_offset: float32 [], replicated, may hold values from -2 to 0
- objective_multiplier: float32 [], replicated, may hold values from 32768 to 262144
Outputs:
- image_grad: bfloat16 [16384, 1152], P(('blk', 'grp'))
- text_grad: bfloat16 [16384, 1152], P(('blk', 'grp'))
All inputs are finite; a program needn't handle non-finite values.
Results may differ from a plain program's by a relative error of at most 0.017.
Values may be sent and summed in bfloat16 or wider, within the bound.
No kernel may reach another device: no remote copies, remote signals or barrier semaphores. Data moves between devices by JAX's collectives and lax.ppermute only.
A program may use at most 64 MiB of HBM per device.

v0:
```python
import jax
import jax.numpy as jnp
from jax import lax
from jax.sharding import PartitionSpec as P


def from_behind(value, axis, steps):
    count = lax.axis_size(axis)
    pairs = [(source, (source + steps) % count) for source in range(count)]
    return lax.ppermute(value, axis, pairs)


def unit_rows(raw):
    values = raw.astype(jnp.float32)
    inverse = lax.rsqrt(jnp.sum(values * values, axis=1, keepdims=True) + 1e-06)
    return (values * inverse, inverse)


def through_norm(unit, inverse, direct):
    along = jnp.sum(unit * direct, axis=1, keepdims=True)
    return (inverse * (direct - unit * along)).astype(jnp.bfloat16)


def send_text(payload):
    return from_behind(payload, "blk", 1)


def send_sums(payload):
    return from_behind(payload, "blk", 1)


def on_device(
    picture_vectors, caption_vectors, ln_inverse_warmth, score_offset, objective_multiplier
):
    row_count = picture_vectors.shape[0]
    feature = picture_vectors.shape[1]
    size_blk = lax.axis_size("blk")
    size_grp = lax.axis_size("grp")
    batch_total = row_count * size_blk * size_grp
    group_rows = row_count * size_grp
    index_blk = lax.axis_index("blk")
    index_grp = lax.axis_index("grp")
    image_unit, image_inv = unit_rows(picture_vectors)
    text_unit, text_inv = unit_rows(caption_vectors)
    image_half = image_unit.astype(jnp.bfloat16)
    caption_subset_entries = text_unit.astype(jnp.bfloat16)
    score_multiplier = jnp.exp(ln_inverse_warmth)
    sigmoid_coefficient = objective_multiplier / batch_total
    image_group = lax.all_gather(image_half, "grp", axis=0, tiled=True)
    image_ids = index_blk * group_rows + jnp.arange(group_rows, dtype=jnp.int32)

    def tile_terms(visiting, visit_ids):
        similarity_scores = (
            score_multiplier
            * lax.dot_general(
                image_group, visiting, (((1,), (1,)), ((), ())), preferred_element_type=jnp.float32
            )
            + score_offset
        )
        match_polarity = jnp.where(
            image_ids[:, None] == visit_ids[None, :], jnp.float32(1.0), jnp.float32(-1.0)
        )
        score_derivative = (
            -(sigmoid_coefficient * score_multiplier)
            * match_polarity
            * jax.nn.sigmoid(-match_polarity * similarity_scores)
        ).astype(jnp.bfloat16)
        image_term = jnp.dot(score_derivative, visiting, preferred_element_type=jnp.float32)
        text_term = lax.dot_general(
            score_derivative,
            image_group,
            (((0,), (0,)), ((), ())),
            preferred_element_type=jnp.float32,
        )
        text_round = lax.optimization_barrier(text_term.astype(jnp.bfloat16))
        return (image_term, text_round.astype(jnp.float32))

    row_ids = jnp.arange(row_count, dtype=jnp.int32)

    def source_ids(step_index):
        source = (index_blk - step_index) % size_blk
        return (source * size_grp + index_grp) * row_count + row_ids

    def one_visit(step_index, carried):
        visiting, text_acc, image_acc = carried
        image_term, text_term = tile_terms(visiting, source_ids(step_index))
        text_acc = send_sums(text_acc + text_term)
        visiting = send_text(visiting)
        return (visiting, text_acc, image_acc + image_term)

    start_state = (
        caption_subset_entries,
        jnp.zeros((row_count, feature), jnp.float32),
        jnp.zeros((group_rows, feature), jnp.float32),
    )
    visiting, text_acc, image_acc = lax.fori_loop(0, size_blk - 1, one_visit, start_state)
    image_term, text_term = tile_terms(visiting, source_ids(size_blk - 1))
    text_dir = send_sums(text_acc + text_term)
    image_part = image_acc + image_term
    image_dir = lax.psum_scatter(image_part, "grp", scatter_dimension=0, tiled=True)
    return (
        through_norm(image_unit, image_inv, image_dir),
        through_norm(text_unit, text_inv, text_dir),
    )


def solution(mesh):
    return jax.shard_map(
        on_device,
        mesh=mesh,
        in_specs=(P(("blk", "grp"), None), P(("blk", "grp"), None), P(), P(), P()),
        out_specs=(P(("blk", "grp"), None), P(("blk", "grp"), None)),
        check_vma=False,
    )
```

profile of v0, /device:TPU:1, one launch (start us, length us, event | category | flops | bytes accessed | tf_op | source)
XLA Modules:
  0.0 468.5 jit_solution(316643605418217194)
XLA Ops:
  15.2 54.9 %all-gather.2.cloned.1.call-done = bf16[1024,1152]{1,0:T(8,128)(2,1)} async-done(((bf16[128,1152]{1,0:T(8,128)(2,1)}), bf16[1024,1152]{1,0:T(8,128)(2,1)}) %all-gather.2.cloned.1.call-update) | async-done | bytes 2359312 | tf_op jit(solution)/shard_map/all_gather | solution.py:49
  70.2 283.8 %while.20 = (s32[]{:T(128)}, bf16[128,1152]{1,0:T(8,128)(2,1)}, f32[128,1152]{1,0:T(8,128)S(1)}, f32[1024,1152]{1,0:T(8,128)}, f32[]{:T(128)}, /*index=5*/s32[]{...) while((s32[]{:T(128)}, bf16[128,1152]{1,0:T(8,128)(2,1)}, ...), condition=%wide.region_3.4_spmd.clone, body=%wide.region_2.3_spmd.clone.sunk | while | flops 910345344 | bytes 30877120 | solution.py:96
  71.3 3.2 fusion.61
  80.3 7.0 %collective-permute-done = bf16[128,1152]{1,0:T(8,128)(2,1)} collective-permute-done((bf16[128,1152]{1,0:T(8,128)(2,1)S(1)}, bf16[128,1152]{1,0:T(8,128)(2,1)}, u32[]{:S(2)}, u32[]{:S(2)}) %collective-permute-start) | collective-permute-done | bytes 294944 | tf_op jit(solution)/shard_map/while/body/eval_jaxpr/ppermute | solution.py:10
  88.5 3.2 fusion.61
  95.0 5.2 %convolution_add_fusion.3 = f32[1024,1152]{1,0:T(8,128)} fusion(bf16[1024,128]{1,0:T(8,128)(2,1)S(1)} %fusion.61, bf16[128,1152]{1,0:T(8,128)(2,1)S(1)} %copy.12, f32[1024,1152]{1,0:T(8,128)} %get-tuple-element.448, pred[]{:T(512)S(6)} %compare.5), kind=kOutput, calls=%fused_computation.2.clone.1 | convolution fusion | flops 304349184 | bytes 9994241 | tf_op jit(solution)/shard_map/while/body/eval_jaxpr/dot_general | solution.py:68
  100.2 4.7 %collective-permute-done = bf16[128,1152]{1,0:T(8,128)(2,1)} collective-permute-done((bf16[128,1152]{1,0:T(8,128)(2,1)S(1)}, bf16[128,1152]{1,0:T(8,128)(2,1)}, u32[]{:S(2)}, u32[]{:S(2)}) %collective-permute-start) | collective-permute-done | bytes 294944 | tf_op jit(solution)/shard_map/while/body/eval_jaxpr/ppermute | solution.py:10
  106.1 3.2 fusion.61
  112.6 5.2 %convolution_add_fusion.3 = f32[1024,1152]{1,0:T(8,128)} fusion(bf16[1024,128]{1,0:T(8,128)(2,1)S(1)} %fusion.61, bf16[128,1152]{1,0:T(8,128)(2,1)S(1)} %copy.12, f32[1024,1152]{1,0:T(8,128)} %get-tuple-element.448, pred[]{:T(512)S(6)} %compare.5), kind=kOutput, calls=%fused_computation.2.clone.1 | convolution fusion | flops 304349184 | bytes 9994241 | tf_op jit(solution)/shard_map/while/body/eval_jaxpr/dot_general | solution.py:68
  117.8 4.7 %collective-permute-done = bf16[128,1152]{1,0:T(8,128)(2,1)} collective-permute-done((bf16[128,1152]{1,0:T(8,128)(2,1)S(1)}, bf16[128,1152]{1,0:T(8,128)(2,1)}, u32[]{:S(2)}, u32[]{:S(2)}) %collective-permute-start) | collective-permute-done | bytes 294944 | tf_op jit(solution)/shard_map/while/body/eval_jaxpr/ppermute | solution.py:10
  123.6 3.2 fusion.61
  130.2 5.2 %convolution_add_fusion.3 = f32[1024,1152]{1,0:T(8,128)} fusion(bf16[1024,128]{1,0:T(8,128)(2,1)S(1)} %fusion.61, bf16[128,1152]{1,0:T(8,128)(2,1)S(1)} %copy.12, f32[1024,1152]{1,0:T(8,128)} %get-tuple-element.448, pred[]{:T(512)S(6)} %compare.5), kind=kOutput, calls=%fused_computation.2.clone.1 | convolution fusion | flops 304349184 | bytes 9994241 | tf_op jit(solution)/shard_map/while/body/eval_jaxpr/dot_general | solution.py:68
  135.4 4.7 %collective-permute-done = bf16[128,1152]{1,0:T(8,128)(2,1)} collective-permute-done((bf16[128,1152]{1,0:T(8,128)(2,1)S(1)}, bf16[128,1152]{1,0:T(8,128)(2,1)}, u32[]{:S(2)}, u32[]{:S(2)}) %collective-permute-start) | collective-permute-done | bytes 294944 | tf_op jit(solution)/shard_map/while/body/eval_jaxpr/ppermute | solution.py:10
  141.2 3.2 fusion.61
  147.8 5.2 %convolution_add_fusion.3 = f32[1024,1152]{1,0:T(8,128)} fusion(bf16[1024,128]{1,0:T(8,128)(2,1)S(1)} %fusion.61, bf16[128,1152]{1,0:T(8,128)(2,1)S(1)} %copy.12, f32[1024,1152]{1,0:T(8,128)} %get-tuple-element.448, pred[]{:T(512)S(6)} %compare.5), kind=kOutput, calls=%fused_computation.2.clone.1 | convolution fusion | flops 304349184 | bytes 9994241 | tf_op jit(solution)/shard_map/while/body/eval_jaxpr/dot_general | solution.py:68
  153.0 4.7 %collective-permute-done = bf16[128,1152]{1,0:T(8,128)(2,1)} collective-permute-done((bf16[128,1152]{1,0:T(8,128)(2,1)S(1)}, bf16[128,1152]{1,0:T(8,128)(2,1)}, u32[]{:S(2)}, u32[]{:S(2)}) %collective-permute-start) | collective-permute-done | bytes 294944 | tf_op jit(solution)/shard_map/while/body/eval_jaxpr/ppermute | solution.py:10
  158.8 3.2 fusion.61
  165.3 5.2 %convolution_add_fusion.3 = f32[1024,1152]{1,0:T(8,128)} fusion(bf16[1024,128]{1,0:T(8,128)(2,1)S(1)} %fusion.61, bf16[128,1152]{1,0:T(8,128)(2,1)S(1)} %copy.12, f32[1024,1152]{1,0:T(8,128)} %get-tuple-element.448, pred[]{:T(512)S(6)} %compare.5), kind=kOutput, calls=%fused_computation.2.clone.1 | convolution fusion | flops 304349184 | bytes 9994241 | tf_op jit(solution)/shard_map/while/body/eval_jaxpr/dot_general | solution.py:68
  170.5 6.2 %collective-permute-done = bf16[128,1152]{1,0:T(8,128)(2,1)} collective-permute-done((bf16[128,1152]{1,0:T(8,128)(2,1)S(1)}, bf16[128,1152]{1,0:T(8,128)(2,1)}, u32[]{:S(2)}, u32[]{:S(2)}) %collective-permute-start) | collective-permute-done | bytes 294944 | tf_op jit(solution)/shard_map/while/body/eval_jaxpr/ppermute | solution.py:10
  177.9 3.2 fusion.61
  182.9 5.2 %convolution_add_fusion.3 = f32[1024,1152]{1,0:T(8,128)} fusion(bf16[1024,128]{1,0:T(8,128)(2,1)S(1)} %fusion.61, bf16[128,1152]{1,0:T(8,128)(2,1)S(1)} %copy.12, f32[1024,1152]{1,0:T(8,128)} %get-tuple-element.448, pred[]{:T(512)S(6)} %compare.5), kind=kOutput, calls=%fused_computation.2.clone.1 | convolution fusion | flops 304349184 | bytes 9994241 | tf_op jit(solution)/shard_map/while/body/eval_jaxpr/dot_general | solution.py:68
  188.1 8.3 %collective-permute-done = bf16[128,1152]{1,0:T(8,128)(2,1)} collective-permute-done((bf16[128,1152]{1,0:T(8,128)(2,1)S(1)}, bf16[128,1152]{1,0:T(8,128)(2,1)}, u32[]{:S(2)}, u32[]{:S(2)}) %collective-permute-start) | collective-permute-done | bytes 294944 | tf_op jit(solution)/shard_map/while/body/eval_jaxpr/ppermute | solution.py:10
  197.6 3.2 fusion.61
  201.6 5.2 %convolution_add_fusion.3 = f32[1024,1152]{1,0:T(8,128)} fusion(bf16[1024,128]{1,0:T(8,128)(2,1)S(1)} %fusion.61, bf16[128,1152]{1,0:T(8,128)(2,1)S(1)} %copy.12, f32[1024,1152]{1,0:T(8,128)} %get-tuple-element.448, pred[]{:T(512)S(6)} %compare.5), kind=kOutput, calls=%fused_computation.2.clone.1 | convolution fusion | flops 304349184 | bytes 9994241 | tf_op jit(solution)/shard_map/while/body/eval_jaxpr/dot_general | solution.py:68
  206.8 9.4 %collective-permute-done = bf16[128,1152]{1,0:T(8,128)(2,1)} collective-permute-done((bf16[128,1152]{1,0:T(8,128)(2,1)S(1)}, bf16[128,1152]{1,0:T(8,128)(2,1)}, u32[]{:S(2)}, u32[]{:S(2)}) %collective-permute-start) | collective-permute-done | bytes 294944 | tf_op jit(solution)/shard_map/while/body/eval_jaxpr/ppermute | solution.py:10
  217.3 3.2 fusion.61
  221.2 5.2 %convolution_add_fusion.3 = f32[1024,1152]{1,0:T(8,128)} fusion(bf16[1024,128]{1,0:T(8,128)(2,1)S(1)} %fusion.61, bf16[128,1152]{1,0:T(8,128)(2,1)S(1)} %copy.12, f32[1024,1152]{1,0:T(8,128)} %get-tuple-element.448, pred[]{:T(512)S(6)} %compare.5), kind=kOutput, calls=%fused_computation.2.clone.1 | convolution fusion | flops 304349184 | bytes 9994241 | tf_op jit(solution)/shard_map/while/body/eval_jaxpr/dot_general | solution.py:68
  226.5 9.4 %collective-permute-done = bf16[128,1152]{1,0:T(8,128)(2,1)} collective-permute-done((bf16[128,1152]{1,0:T(8,128)(2,1)S(1)}, bf16[128,1152]{1,0:T(8,128)(2,1)}, u32[]{:S(2)}, u32[]{:S(2)}) %collective-permute-start) | collective-permute-done | bytes 294944 | tf_op jit(solution)/shard_map/while/body/eval_jaxpr/ppermute | solution.py:10
  237.0 3.2 fusion.61
  240.9 5.2 %convolution_add_fusion.3 = f32[1024,1152]{1,0:T(8,128)} fusion(bf16[1024,128]{1,0:T(8,128)(2,1)S(1)} %fusion.61, bf16[128,1152]{1,0:T(8,128)(2,1)S(1)} %copy.12, f32[1024,1152]{1,0:T(8,128)} %get-tuple-element.448, pred[]{:T(512)S(6)} %compare.5), kind=kOutput, calls=%fused_computation.2.clone.1 | convolution fusion | flops 304349184 | bytes 9994241 | tf_op jit(solution)/shard_map/while/body/eval_jaxpr/dot_general | solution.py:68
  246.2 9.4 %collective-permute-done = bf16[128,1152]{1,0:T(8,128)(2,1)} collective-permute-done((bf16[128,1152]{1,0:T(8,128)(2,1)S(1)}, bf16[128,1152]{1,0:T(8,128)(2,1)}, u32[]{:S(2)}, u32[]{:S(2)}) %collective-permute-start) | collective-permute-done | bytes 294944 | tf_op jit(solution)/shard_map/while/body/eval_jaxpr/ppermute | solution.py:10
  260.6 5.2 %convolution_add_fusion.3 = f32[1024,1152]{1,0:T(8,128)} fusion(bf16[1024,128]{1,0:T(8,128)(2,1)S(1)} %fusion.61, bf16[128,1152]{1,0:T(8,128)(2,1)S(1)} %copy.12, f32[1024,1152]{1,0:T(8,128)} %get-tuple-element.448, pred[]{:T(512)S(6)} %compare.5), kind=kOutput, calls=%fused_computation.2.clone.1 | convolution fusion | flops 304349184 | bytes 9994241 | tf_op jit(solution)/shard_map/while/body/eval_jaxpr/dot_general | solution.py:68
  265.8 9.4 %collective-permute-done = bf16[128,1152]{1,0:T(8,128)(2,1)} collective-permute-done((bf16[128,1152]{1,0:T(8,128)(2,1)S(1)}, bf16[128,1152]{1,0:T(8,128)(2,1)}, u32[]{:S(2)}, u32[]{:S(2)}) %collective-permute-start) | collective-permute-done | bytes 294944 | tf_op jit(solution)/shard_map/while/body/eval_jaxpr/ppermute | solution.py:10
  276.3 3.2 fusion.61
  280.3 5.2 %convolution_add_fusion.3 = f32[1024,1152]{1,0:T(8,128)} fusion(bf16[1024,128]{1,0:T(8,128)(2,1)S(1)} %fusion.61, bf16[128,1152]{1,0:T(8,128)(2,1)S(1)} %copy.12, f32[1024,1152]{1,0:T(8,128)} %get-tuple-element.448, pred[]{:T(512)S(6)} %compare.5), kind=kOutput, calls=%fused_computation.2.clone.1 | convolution fusion | flops 304349184 | bytes 9994241 | tf_op jit(solution)/shard_map/while/body/eval_jaxpr/dot_general | solution.py:68
  285.5 9.4 %collective-permute-done = bf16[128,1152]{1,0:T(8,128)(2,1)} collective-permute-done((bf16[128,1152]{1,0:T(8,128)(2,1)S(1)}, bf16[128,1152]{1,0:T(8,128)(2,1)}, u32[]{:S(2)}, u32[]{:S(2)}) %collective-permute-start) | collective-permute-done | bytes 294944 | tf_op jit(solution)/shard_map/while/body/eval_jaxpr/ppermute | solution.py:10
  296.0 3.2 fusion.61
  300.0 5.2 %convolution_add_fusion.3 = f32[1024,1152]{1,0:T(8,128)} fusion(bf16[1024,128]{1,0:T(8,128)(2,1)S(1)} %fusion.61, bf16[128,1152]{1,0:T(8,128)(2,1)S(1)} %copy.12, f32[1024,1152]{1,0:T(8,128)} %get-tuple-element.448, pred[]{:T(512)S(6)} %compare.5), kind=kOutput, calls=%fused_computation.2.clone.1 | convolution fusion | flops 304349184 | bytes 9994241 | tf_op jit(solution)/shard_map/while/body/eval_jaxpr/dot_general | solution.py:68
  305.2 9.4 %collective-permute-done = bf16[128,1152]{1,0:T(8,128)(2,1)} collective-permute-done((bf16[128,1152]{1,0:T(8,128)(2,1)S(1)}, bf16[128,1152]{1,0:T(8,128)(2,1)}, u32[]{:S(2)}, u32[]{:S(2)}) %collective-permute-start) | collective-permute-done | bytes 294944 | tf_op jit(solution)/shard_map/while/body/eval_jaxpr/ppermute | solution.py:10
  315.7 3.2 fusion.61
  319.7 5.2 %convolution_add_fusion.3 = f32[1024,1152]{1,0:T(8,128)} fusion(bf16[1024,128]{1,0:T(8,128)(2,1)S(1)} %fusion.61, bf16[128,1152]{1,0:T(8,128)(2,1)S(1)} %copy.12, f32[1024,1152]{1,0:T(8,128)} %get-tuple-element.448, pred[]{:T(512)S(6)} %compare.5), kind=kOutput, calls=%fused_computation.2.clone.1 | convolution fusion | flops 304349184 | bytes 9994241 | tf_op jit(solution)/shard_map/while/body/eval_jaxpr/dot_general | solution.py:68
  324.9 9.4 %collective-permute-done = bf16[128,1152]{1,0:T(8,128)(2,1)} collective-permute-done((bf16[128,1152]{1,0:T(8,128)(2,1)S(1)}, bf16[128,1152]{1,0:T(8,128)(2,1)}, u32[]{:S(2)}, u32[]{:S(2)}) %collective-permute-start) | collective-permute-done | bytes 294944 | tf_op jit(solution)/shard_map/while/body/eval_jaxpr/ppermute | solution.py:10
  335.4 3.2 fusion.61
  339.4 5.2 %convolution_add_fusion.3 = f32[1024,1152]{1,0:T(8,128)} fusion(bf16[1024,128]{1,0:T(8,128)(2,1)S(1)} %fusion.61, bf16[128,1152]{1,0:T(8,128)(2,1)S(1)} %copy.12, f32[1024,1152]{1,0:T(8,128)} %get-tuple-element.448, pred[]{:T(512)S(6)} %compare.5), kind=kOutput, calls=%fused_computation.2.clone.1 | convolution fusion | flops 304349184 | bytes 9994241 | tf_op jit(solution)/shard_map/while/body/eval_jaxpr/dot_general | solution.py:68
  344.6 9.4 %collective-permute-done = bf16[128,1152]{1,0:T(8,128)(2,1)} collective-permute-done((bf16[128,1152]{1,0:T(8,128)(2,1)S(1)}, bf16[128,1152]{1,0:T(8,128)(2,1)}, u32[]{:S(2)}, u32[]{:S(2)}) %collective-permute-start) | collective-permute-done | bytes 294944 | tf_op jit(solution)/shard_map/while/body/eval_jaxpr/ppermute | solution.py:10
  357.4 3.8 convolution_add_fusion.1
  364.5 14.1 %collective-permute-done.2 = f32[128,1152]{1,0:T(8,128)S(1)} collective-permute-done((f32[128,1152]{1,0:T(8,128)S(1)}, f32[128,1152]{1,0:T(8,128)S(1)}, u32[]{:S(2)}, u32[]{:S(2)}) %collective-permute-start.2) | collective-permute-done | bytes 589856 | tf_op jit(solution)/shard_map/ppermute | solution.py:10
  379.8 78.5 %reduce-scatter.2.cloned.1.call-done = f32[128,1152]{1,0:T(8,128)} async-done(((f32[1024,1152]{1,0:T(8,128)}), f32[128,1152]{1,0:T(8,128)}) %reduce-scatter.2.cloned.1.call-update) | async-done | bytes 589840 | tf_op jit(solution)/shard_map/reduce_scatter | solution.py:100
  (184 shorter events, 67.4 us)
Async XLA Ops:
  7.2 62.9 %all-gather.2.cloned.1.call-start = ((), (), s32[]{:S(2)}) async-start(), calls=%async_computation.1 | async-start | bytes 2654208 | tf_op jit(solution)/shard_map/all_gather | solution.py:49
  10.1 448.2 %reduce-scatter.2.cloned.1.call-start = ((), (), s32[]{:S(2)}) async-start(), calls=%async_computation.2 | async-start | bytes 5308416 | tf_op jit(solution)/shard_map/reduce_scatter | solution.py:100
  70.2 4.3 copy-start.1
  75.1 12.2 %collective-permute-start.1 = (f32[128,1152]{1,0:T(8,128)S(1)}, f32[128,1152]{1,0:T(8,128)S(1)}, u32[]{:S(2)}, u32[]{:S(2)}) collective-permute-start(f32[128,1152]{1,0:T(8,128)S(1)} %convert_add_fusion.3), channel_id=1, source_target_pairs={{0,8},{8,16},{16,24},{24,32},{32,40},{40,48},{48,56},{56,64},{64,7... | collective-permute-start | bytes 1769480 | tf_op jit(solution)/shard_map/while/body/eval_jaxpr/ppermute | solution.py:10
  77.4 10.0 %collective-permute-start = (bf16[128,1152]{1,0:T(8,128)(2,1)S(1)}, bf16[128,1152]{1,0:T(8,128)(2,1)}, u32[]{:S(2)}, u32[]{:S(2)}) collective-permute-start(bf16[128,1152]{1,0:T(8,128)(2,1)S(1)} %copy.12), channel_id=1, source_target_pairs={{0,8},{8,16},{16,24},{24,32},{32,40},{40,48},{48,56},{56,64},{64,7... | collective-permute-start | bytes 884744 | tf_op jit(solution)/shard_map/while/body/eval_jaxpr/ppermute | solution.py:10
  87.4 4.3 copy-start.1
  92.3 12.6 %collective-permute-start.1 = (f32[128,1152]{1,0:T(8,128)S(1)}, f32[128,1152]{1,0:T(8,128)S(1)}, u32[]{:S(2)}, u32[]{:S(2)}) collective-permute-start(f32[128,1152]{1,0:T(8,128)S(1)} %convert_add_fusion.3), channel_id=1, source_target_pairs={{0,8},{8,16},{16,24},{24,32},{32,40},{40,48},{48,56},{56,64},{64,7... | collective-permute-start | bytes 1769480 | tf_op jit(solution)/shard_map/while/body/eval_jaxpr/ppermute | solution.py:10
  94.9 10.0 %collective-permute-start = (bf16[128,1152]{1,0:T(8,128)(2,1)S(1)}, bf16[128,1152]{1,0:T(8,128)(2,1)}, u32[]{:S(2)}, u32[]{:S(2)}) collective-permute-start(bf16[128,1152]{1,0:T(8,128)(2,1)S(1)} %copy.12), channel_id=1, source_target_pairs={{0,8},{8,16},{16,24},{24,32},{32,40},{40,48},{48,56},{56,64},{64,7... | collective-permute-start | bytes 884744 | tf_op jit(solution)/shard_map/while/body/eval_jaxpr/ppermute | solution.py:10
  104.9 4.3 copy-start.1
  109.9 12.6 %collective-permute-start.1 = (f32[128,1152]{1,0:T(8,128)S(1)}, f32[128,1152]{1,0:T(8,128)S(1)}, u32[]{:S(2)}, u32[]{:S(2)}) collective-permute-start(f32[128,1152]{1,0:T(8,128)S(1)} %convert_add_fusion.3), channel_id=1, source_target_pairs={{0,8},{8,16},{16,24},{24,32},{32,40},{40,48},{48,56},{56,64},{64,7... | collective-permute-start | bytes 1769480 | tf_op jit(solution)/shard_map/while/body/eval_jaxpr/ppermute | solution.py:10
  112.5 10.0 %collective-permute-start = (bf16[128,1152]{1,0:T(8,128)(2,1)S(1)}, bf16[128,1152]{1,0:T(8,128)(2,1)}, u32[]{:S(2)}, u32[]{:S(2)}) collective-permute-start(bf16[128,1152]{1,0:T(8,128)(2,1)S(1)} %copy.12), channel_id=1, source_target_pairs={{0,8},{8,16},{16,24},{24,32},{32,40},{40,48},{48,56},{56,64},{64,7... | collective-permute-start | bytes 884744 | tf_op jit(solution)/shard_map/while/body/eval_jaxpr/ppermute | solution.py:10
  122.5 4.3 copy-start.1
  127.4 12.6 %collective-permute-start.1 = (f32[128,1152]{1,0:T(8,128)S(1)}, f32[128,1152]{1,0:T(8,128)S(1)}, u32[]{:S(2)}, u32[]{:S(2)}) collective-permute-start(f32[128,1152]{1,0:T(8,128)S(1)} %convert_add_fusion.3), channel_id=1, source_target_pairs={{0,8},{8,16},{16,24},{24,32},{32,40},{40,48},{48,56},{56,64},{64,7... | collective-permute-start | bytes 1769480 | tf_op jit(solution)/shard_map/while/body/eval_jaxpr/ppermute | solution.py:10
  130.1 10.0 %collective-permute-start = (bf16[128,1152]{1,0:T(8,128)(2,1)S(1)}, bf16[128,1152]{1,0:T(8,128)(2,1)}, u32[]{:S(2)}, u32[]{:S(2)}) collective-permute-start(bf16[128,1152]{1,0:T(8,128)(2,1)S(1)} %copy.12), channel_id=1, source_target_pairs={{0,8},{8,16},{16,24},{24,32},{32,40},{40,48},{48,56},{56,64},{64,7... | collective-permute-start | bytes 884744 | tf_op jit(solution)/shard_map/while/body/eval_jaxpr/ppermute | solution.py:10
  140.1 4.3 copy-start.1
  145.0 12.6 %collective-permute-start.1 = (f32[128,1152]{1,0:T(8,128)S(1)}, f32[128,1152]{1,0:T(8,128)S(1)}, u32[]{:S(2)}, u32[]{:S(2)}) collective-permute-start(f32[128,1152]{1,0:T(8,128)S(1)} %convert_add_fusion.3), channel_id=1, source_target_pairs={{0,8},{8,16},{16,24},{24,32},{32,40},{40,48},{48,56},{56,64},{64,7... | collective-permute-start | bytes 1769480 | tf_op jit(solution)/shard_map/while/body/eval_jaxpr/ppermute | solution.py:10
  147.7 10.0 %collective-permute-start = (bf16[128,1152]{1,0:T(8,128)(2,1)S(1)}, bf16[128,1152]{1,0:T(8,128)(2,1)}, u32[]{:S(2)}, u32[]{:S(2)}) collective-permute-start(bf16[128,1152]{1,0:T(8,128)(2,1)S(1)} %copy.12), channel_id=1, source_target_pairs={{0,8},{8,16},{16,24},{24,32},{32,40},{40,48},{48,56},{56,64},{64,7... | collective-permute-start | bytes 884744 | tf_op jit(solution)/shard_map/while/body/eval_jaxpr/ppermute | solution.py:10
  157.7 4.3 copy-start.1
  162.6 14.2 %collective-permute-start.1 = (f32[128,1152]{1,0:T(8,128)S(1)}, f32[128,1152]{1,0:T(8,128)S(1)}, u32[]{:S(2)}, u32[]{:S(2)}) collective-permute-start(f32[128,1152]{1,0:T(8,128)S(1)} %convert_add_fusion.3), channel_id=1, source_target_pairs={{0,8},{8,16},{16,24},{24,32},{32,40},{40,48},{48,56},{56,64},{64,7... | collective-permute-start | bytes 1769480 | tf_op jit(solution)/shard_map/while/body/eval_jaxpr/ppermute | solution.py:10
  165.3 11.5 %collective-permute-start = (bf16[128,1152]{1,0:T(8,128)(2,1)S(1)}, bf16[128,1152]{1,0:T(8,128)(2,1)}, u32[]{:S(2)}, u32[]{:S(2)}) collective-permute-start(bf16[128,1152]{1,0:T(8,128)(2,1)S(1)} %copy.12), channel_id=1, source_target_pairs={{0,8},{8,16},{16,24},{24,32},{32,40},{40,48},{48,56},{56,64},{64,7... | collective-permute-start | bytes 884744 | tf_op jit(solution)/shard_map/while/body/eval_jaxpr/ppermute | solution.py:10
  176.8 4.3 copy-start.1
  181.7 14.8 %collective-permute-start.1 = (f32[128,1152]{1,0:T(8,128)S(1)}, f32[128,1152]{1,0:T(8,128)S(1)}, u32[]{:S(2)}, u32[]{:S(2)}) collective-permute-start(f32[128,1152]{1,0:T(8,128)S(1)} %convert_add_fusion.3), channel_id=1, source_target_pairs={{0,8},{8,16},{16,24},{24,32},{32,40},{40,48},{48,56},{56,64},{64,7... | collective-permute-start | bytes 1769480 | tf_op jit(solution)/shard_map/while/body/eval_jaxpr/ppermute | solution.py:10
  182.8 13.6 %collective-permute-start = (bf16[128,1152]{1,0:T(8,128)(2,1)S(1)}, bf16[128,1152]{1,0:T(8,128)(2,1)}, u32[]{:S(2)}, u32[]{:S(2)}) collective-permute-start(bf16[128,1152]{1,0:T(8,128)(2,1)S(1)} %copy.12), channel_id=1, source_target_pairs={{0,8},{8,16},{16,24},{24,32},{32,40},{40,48},{48,56},{56,64},{64,7... | collective-permute-start | bytes 884744 | tf_op jit(solution)/shard_map/while/body/eval_jaxpr/ppermute | solution.py:10
  196.5 4.3 copy-start.1
  201.4 14.8 %collective-permute-start.1 = (f32[128,1152]{1,0:T(8,128)S(1)}, f32[128,1152]{1,0:T(8,128)S(1)}, u32[]{:S(2)}, u32[]{:S(2)}) collective-permute-start(f32[128,1152]{1,0:T(8,128)S(1)} %convert_add_fusion.3), channel_id=1, source_target_pairs={{0,8},{8,16},{16,24},{24,32},{32,40},{40,48},{48,56},{56,64},{64,7... | collective-permute-start | bytes 1769480 | tf_op jit(solution)/shard_map/while/body/eval_jaxpr/ppermute | solution.py:10
  201.5 14.7 %collective-permute-start = (bf16[128,1152]{1,0:T(8,128)(2,1)S(1)}, bf16[128,1152]{1,0:T(8,128)(2,1)}, u32[]{:S(2)}, u32[]{:S(2)}) collective-permute-start(bf16[128,1152]{1,0:T(8,128)(2,1)S(1)} %copy.12), channel_id=1, source_target_pairs={{0,8},{8,16},{16,24},{24,32},{32,40},{40,48},{48,56},{56,64},{64,7... | collective-permute-start | bytes 884744 | tf_op jit(solution)/shard_map/while/body/eval_jaxpr/ppermute | solution.py:10
  221.1 14.8 %collective-permute-start.1 = (f32[128,1152]{1,0:T(8,128)S(1)}, f32[128,1152]{1,0:T(8,128)S(1)}, u32[]{:S(2)}, u32[]{:S(2)}) collective-permute-start(f32[128,1152]{1,0:T(8,128)S(1)} %convert_add_fusion.3), channel_id=1, source_target_pairs={{0,8},{8,16},{16,24},{24,32},{32,40},{40,48},{48,56},{56,64},{64,7... | collective-permute-start | bytes 1769480 | tf_op jit(solution)/shard_map/while/body/eval_jaxpr/ppermute | solution.py:10
  221.2 14.7 %collective-permute-start = (bf16[128,1152]{1,0:T(8,128)(2,1)S(1)}, bf16[128,1152]{1,0:T(8,128)(2,1)}, u32[]{:S(2)}, u32[]{:S(2)}) collective-permute-start(bf16[128,1152]{1,0:T(8,128)(2,1)S(1)} %copy.12), channel_id=1, source_target_pairs={{0,8},{8,16},{16,24},{24,32},{32,40},{40,48},{48,56},{56,64},{64,7... | collective-permute-start | bytes 884744 | tf_op jit(solution)/shard_map/while/body/eval_jaxpr/ppermute | solution.py:10
  235.8 4.3 copy-start.1
  240.8 14.8 %collective-permute-start.1 = (f32[128,1152]{1,0:T(8,128)S(1)}, f32[128,1152]{1,0:T(8,128)S(1)}, u32[]{:S(2)}, u32[]{:S(2)}) collective-permute-start(f32[128,1152]{1,0:T(8,128)S(1)} %convert_add_fusion.3), channel_id=1, source_target_pairs={{0,8},{8,16},{16,24},{24,32},{32,40},{40,48},{48,56},{56,64},{64,7... | collective-permute-start | bytes 1769480 | tf_op jit(solution)/shard_map/while/body/eval_jaxpr/ppermute | solution.py:10
  240.8 14.7 %collective-permute-start = (bf16[128,1152]{1,0:T(8,128)(2,1)S(1)}, bf16[128,1152]{1,0:T(8,128)(2,1)}, u32[]{:S(2)}, u32[]{:S(2)}) collective-permute-start(bf16[128,1152]{1,0:T(8,128)(2,1)S(1)} %copy.12), channel_id=1, source_target_pairs={{0,8},{8,16},{16,24},{24,32},{32,40},{40,48},{48,56},{56,64},{64,7... | collective-permute-start | bytes 884744 | tf_op jit(solution)/shard_map/while/body/eval_jaxpr/ppermute | solution.py:10
  260.5 14.8 %collective-permute-start.1 = (f32[128,1152]{1,0:T(8,128)S(1)}, f32[128,1152]{1,0:T(8,128)S(1)}, u32[]{:S(2)}, u32[]{:S(2)}) collective-permute-start(f32[128,1152]{1,0:T(8,128)S(1)} %convert_add_fusion.3), channel_id=1, source_target_pairs={{0,8},{8,16},{16,24},{24,32},{32,40},{40,48},{48,56},{56,64},{64,7... | collective-permute-start | bytes 1769480 | tf_op jit(solution)/shard_map/while/body/eval_jaxpr/ppermute | solution.py:10
  260.5 14.7 %collective-permute-start = (bf16[128,1152]{1,0:T(8,128)(2,1)S(1)}, bf16[128,1152]{1,0:T(8,128)(2,1)}, u32[]{:S(2)}, u32[]{:S(2)}) collective-permute-start(bf16[128,1152]{1,0:T(8,128)(2,1)S(1)} %copy.12), channel_id=1, source_target_pairs={{0,8},{8,16},{16,24},{24,32},{32,40},{40,48},{48,56},{56,64},{64,7... | collective-permute-start | bytes 884744 | tf_op jit(solution)/shard_map/while/body/eval_jaxpr/ppermute | solution.py:10
  275.2 4.3 copy-start.1
  280.1 14.8 %collective-permute-start.1 = (f32[128,1152]{1,0:T(8,128)S(1)}, f32[128,1152]{1,0:T(8,128)S(1)}, u32[]{:S(2)}, u32[]{:S(2)}) collective-permute-start(f32[128,1152]{1,0:T(8,128)S(1)} %convert_add_fusion.3), channel_id=1, source_target_pairs={{0,8},{8,16},{16,24},{24,32},{32,40},{40,48},{48,56},{56,64},{64,7... | collective-permute-start | bytes 1769480 | tf_op jit(solution)/shard_map/while/body/eval_jaxpr/ppermute | solution.py:10
  280.2 14.7 %collective-permute-start = (bf16[128,1152]{1,0:T(8,128)(2,1)S(1)}, bf16[128,1152]{1,0:T(8,128)(2,1)}, u32[]{:S(2)}, u32[]{:S(2)}) collective-permute-start(bf16[128,1152]{1,0:T(8,128)(2,1)S(1)} %copy.12), channel_id=1, source_target_pairs={{0,8},{8,16},{16,24},{24,32},{32,40},{40,48},{48,56},{56,64},{64,7... | collective-permute-start | bytes 884744 | tf_op jit(solution)/shard_map/while/body/eval_jaxpr/ppermute | solution.py:10
  294.9 4.3 copy-start.1
  299.8 14.8 %collective-permute-start.1 = (f32[128,1152]{1,0:T(8,128)S(1)}, f32[128,1152]{1,0:T(8,128)S(1)}, u32[]{:S(2)}, u32[]{:S(2)}) collective-permute-start(f32[128,1152]{1,0:T(8,128)S(1)} %convert_add_fusion.3), channel_id=1, source_target_pairs={{0,8},{8,16},{16,24},{24,32},{32,40},{40,48},{48,56},{56,64},{64,7... | collective-permute-start | bytes 1769480 | tf_op jit(solution)/shard_map/while/body/eval_jaxpr/ppermute | solution.py:10
  299.9 14.7 %collective-permute-start = (bf16[128,1152]{1,0:T(8,128)(2,1)S(1)}, bf16[128,1152]{1,0:T(8,128)(2,1)}, u32[]{:S(2)}, u32[]{:S(2)}) collective-permute-start(bf16[128,1152]{1,0:T(8,128)(2,1)S(1)} %copy.12), channel_id=1, source_target_pairs={{0,8},{8,16},{16,24},{24,32},{32,40},{40,48},{48,56},{56,64},{64,7... | collective-permute-start | bytes 884744 | tf_op jit(solution)/shard_map/while/body/eval_jaxpr/ppermute | solution.py:10
  314.6 4.3 copy-start.1
  319.5 14.8 %collective-permute-start.1 = (f32[128,1152]{1,0:T(8,128)S(1)}, f32[128,1152]{1,0:T(8,128)S(1)}, u32[]{:S(2)}, u32[]{:S(2)}) collective-permute-start(f32[128,1152]{1,0:T(8,128)S(1)} %convert_add_fusion.3), channel_id=1, source_target_pairs={{0,8},{8,16},{16,24},{24,32},{32,40},{40,48},{48,56},{56,64},{64,7... | collective-permute-start | bytes 1769480 | tf_op jit(solution)/shard_map/while/body/eval_jaxpr/ppermute | solution.py:10
  319.6 14.7 %collective-permute-start = (bf16[128,1152]{1,0:T(8,128)(2,1)S(1)}, bf16[128,1152]{1,0:T(8,128)(2,1)}, u32[]{:S(2)}, u32[]{:S(2)}) collective-permute-start(bf16[128,1152]{1,0:T(8,128)(2,1)S(1)} %copy.12), channel_id=1, source_target_pairs={{0,8},{8,16},{16,24},{24,32},{32,40},{40,48},{48,56},{56,64},{64,7... | collective-permute-start | bytes 884744 | tf_op jit(solution)/shard_map/while/body/eval_jaxpr/ppermute | solution.py:10
  334.3 4.3 copy-start.1
  339.2 14.8 %collective-permute-start.1 = (f32[128,1152]{1,0:T(8,128)S(1)}, f32[128,1152]{1,0:T(8,128)S(1)}, u32[]{:S(2)}, u32[]{:S(2)}) collective-permute-start(f32[128,1152]{1,0:T(8,128)S(1)} %convert_add_fusion.3), channel_id=1, source_target_pairs={{0,8},{8,16},{16,24},{24,32},{32,40},{40,48},{48,56},{56,64},{64,7... | collective-permute-start | bytes 1769480 | tf_op jit(solution)/shard_map/while/body/eval_jaxpr/ppermute | solution.py:10
  339.3 14.7 %collective-permute-start = (bf16[128,1152]{1,0:T(8,128)(2,1)S(1)}, bf16[128,1152]{1,0:T(8,128)(2,1)}, u32[]{:S(2)}, u32[]{:S(2)}) collective-permute-start(bf16[128,1152]{1,0:T(8,128)(2,1)S(1)} %copy.12), channel_id=1, source_target_pairs={{0,8},{8,16},{16,24},{24,32},{32,40},{40,48},{48,56},{56,64},{64,7... | collective-permute-start | bytes 884744 | tf_op jit(solution)/shard_map/while/body/eval_jaxpr/ppermute | solution.py:10
  361.2 17.4 %copy-start.3 = (bf16[128,1152]{1,0:T(8,128)(2,1)S(1)}, bf16[128,1152]{1,0:T(8,128)(2,1)}, u32[]{:S(2)}) copy-start(bf16[128,1152]{1,0:T(8,128)(2,1)} %param.8) | copy-start | bytes 884740
  361.2 97.1 %copy-start.4 = (bf16[128,1152]{1,0:T(8,128)(2,1)S(1)}, bf16[128,1152]{1,0:T(8,128)(2,1)}, u32[]{:S(2)}) copy-start(bf16[128,1152]{1,0:T(8,128)(2,1)} %param.7) | copy-start | bytes 884740
  364.4 14.2 %collective-permute-start.2 = (f32[128,1152]{1,0:T(8,128)S(1)}, f32[128,1152]{1,0:T(8,128)S(1)}, u32[]{:S(2)}, u32[]{:S(2)}) collective-permute-start(f32[128,1152]{1,0:T(8,128)S(1)} %convert_add_fusion.1), channel_id=1, source_target_pairs={{0,8},{8,16},{16,24},{24,32},{32,40},{40,48},{48,56},{56,64},{64,7... | collective-permute-start | bytes 1769480 | tf_op jit(solution)/shard_map/ppermute | solution.py:10
  (5 other events, 14.4 us)
Sparse Core Ops, SparseCore 0:
  10.9 59.1 all-gather.1
  361.4 96.9 reduce-scatter.1
where the time goes:
time: 471 us; the launch traced here: 468 us
  waiting for transfers between devices  263 us (56%)
  matrix products  140 us (30%)
  local copies, waits for them, and re-layouts  19.1 us (4%)
  starting transfers between devices  18.6 us (4%)
  between operations  16.1 us (3%)
  other arithmetic  11.2 us (2%)
    ppermute x31, waiting for transfers between devices, from_behind(): return lax.ppermute(value, axis, pairs)  129 us
    dot_general x16, matrix products, tile_terms(): jnp.dot(score_derivative, visiting, preferred_element_type=jnp.float32)  79.7 us
    reduce_scatter x1, waiting for transfers between devices, on_device(): lax.psum_scatter(image_part, 'grp', scatter_dimension=0, tiled=True)  78.5 us
    all_gather x1, waiting for transfers between devices, on_device(): image_group = lax.all_gather(image_half, 'grp', axis=0, tiled=True)  54.9 us
    dot_general x16, matrix products, tile_terms(): lax.dot_general(image_group, visiting, (((1,), (1,)), ((), ())), preferre...  50.5 us
    ppermute x31, starting transfers between devices, from_behind(): return lax.ppermute(value, axis, pairs)  18.5 us
    while x45, local copies, waits for them, and re-layouts  16.8 us
    dot_general x16, matrix products, tile_terms(): lax.dot_general(score_derivative, image_group, (((0,), (0,)), ((), ())),...  9.59 us
  transfers between devices with their start and end apart: 33, of which 18 were waited for; matrix products, arithmetic and copies ran while one was open for 17% of the time, Pallas kernels for 0%

commit v1 on v0

v1 whole, which is shorter than its diff:
```python
from functools import partial

import jax
import jax.numpy as jnp
from jax import lax
from jax.experimental import pallas as pl
from jax.experimental.pallas import tpu as pltpu
from jax.sharding import PartitionSpec as P

RING = 4
CORES = 2
TILE = 256
COPY_ROWS = 32
VMEM_BYTES = 24 * 1024 * 1024


def place(x, y, z, core):
    blk = ((x % 2) * RING + y) * CORES + core
    return blk * 8 + z * 2 + x // 2


def sender(move):
    pairs = [
        (place(x, y, z, core), place(*move(x, y, z, core)))
        for x in range(RING)
        for y in range(RING)
        for z in range(RING)
        for core in range(CORES)
    ]
    return lambda value: lax.ppermute(value, ("blk", "grp"), pairs)


def ring(steps):
    return sender(
        lambda x, y, z, c: (x, y, (z + steps) % RING, c) if c else (x, (y + steps) % RING, z, c)
    )


to_core = sender(lambda x, y, z, c: (x, y, z, 1 - c))
cross = sender(lambda x, y, z, c: (3 - x if c else x ^ 1, y, z, c))
up, down = ring(1), ring(RING - 1)


def call(name, body, out_shape, operands, flops, scalars=(), after=(), scratch=()):
    moved = sum(2 * value.size for value in operands) + sum(2 * shape.size for shape in out_shape)
    out = pl.pallas_call(
        lambda *refs: body(*refs[len(after) :]),
        name=name,
        out_shape=out_shape,
        in_specs=[pl.BlockSpec(memory_space=pl.ANY)] * len(after)
        + [pl.BlockSpec(memory_space=pltpu.SMEM)] * len(scalars)
        + [pl.BlockSpec(memory_space=pltpu.VMEM)] * len(operands),
        scratch_shapes=list(scratch),
        compiler_params=pltpu.CompilerParams(vmem_limit_bytes=VMEM_BYTES),
        cost_estimate=pl.CostEstimate(flops=flops // 64, bytes_accessed=moved // 64, transcendentals=0),
    )(*after, *scalars, *operands)
    return list(out)


def array(rows, columns):
    return jax.ShapeDtypeStruct((rows, columns), jnp.bfloat16)


def total_of(terms):
    total = terms[0].astype(jnp.float32)
    for term in terms[1:]:
        total = total + term.astype(jnp.float32)
    return total


def add(*terms, flops=0, after=()):
    def body(*refs):
        refs[-1][...] = total_of([ref[...] for ref in refs[:-1]]).astype(jnp.bfloat16)

    return call("add", body, [array(*terms[0].shape)], terms, flops, after=after)[0]


def unit_of(values):
    inverse = lax.rsqrt(jnp.sum(values * values, axis=1, keepdims=True) + 1e-06)
    return values * inverse, inverse


def unit_halves(core, parameters, batch_total, picture, caption):
    def body(core, warmth, score_offset, multiplier, picture_ref, caption_ref, *refs):
        keep, give, constants, image, text, sems = refs
        copies = []
        for source, target in ((picture_ref, image), (caption_ref, text)):
            for first in range(0, source.shape[0], COPY_ROWS):
                here = pl.ds(first, COPY_ROWS)
                copies.append(
                    pltpu.make_async_copy(
                        source.at[here, :], target.at[here, :], sems.at[len(copies)]
                    )
                )
        for copy in copies:
            copy.start()
        scale = jnp.exp(jnp.full((1, TILE), warmth[0], jnp.float32))
        constants[0:1, :] = 0.5 * scale
        constants[1:2, :] = jnp.full((1, TILE), 0.5 * score_offset[0], jnp.float32)
        constants[2:3, :] = 0.5 * (multiplier[0] / batch_total * scale)
        for copy in copies:
            copy.wait()

        @pl.when(core[0] == 0)
        def _():
            give[...] = unit_of(image[...].astype(jnp.float32))[0].astype(jnp.bfloat16)
            keep[...] = unit_of(text[...].astype(jnp.float32))[0].astype(jnp.bfloat16)

        @pl.when(core[0] != 0)
        def _():
            give[...] = unit_of(text[...].astype(jnp.float32))[0].astype(jnp.bfloat16)
            keep[...] = unit_of(image[...].astype(jnp.float32))[0].astype(jnp.bfloat16)

    return pl.pallas_call(
        body,
        name="units",
        out_shape=[array(*picture.shape)] * 2 + [jax.ShapeDtypeStruct((8, TILE), jnp.float32)],
        in_specs=[pl.BlockSpec(memory_space=pltpu.SMEM)] * 4
        + [pl.BlockSpec(memory_space=pltpu.HBM)] * 2,
        scratch_shapes=[
            pltpu.VMEM(picture.shape, jnp.bfloat16),
            pltpu.VMEM(picture.shape, jnp.bfloat16),
            pltpu.SemaphoreType.DMA((2 * picture.shape[0] // COPY_ROWS,)),
        ],
        compiler_params=pltpu.CompilerParams(vmem_limit_bytes=VMEM_BYTES),
    )(core, *parameters, picture, caption)


def pack(*blocks):
    rows, feature = blocks[0].shape

    def body(*refs):
        for at, ref in enumerate(refs[:-1]):
            refs[-1][pl.ds(at * rows, rows), :] = ref[...]

    return call("pack", body, [array(len(blocks) * rows, feature)], blocks, rows * feature)[0]


def stacked(refs):
    return jnp.concatenate([ref[...] for ref in refs], axis=0)


def sums(name, constants, left, right, held=None, own=False, rows_out=None, after=()):
    feature = left[0].shape[1]
    count, others = sum(ref.shape[0] for ref in left), sum(ref.shape[0] for ref in right)
    blocks = 1 if rows_out is None else count // rows_out

    def body(constants, *refs):
        left_refs, right_refs = refs[: len(left)], refs[len(left) :][: len(right)]
        refs = refs[len(left) + len(right) :]
        out, grads = refs[-1 - blocks : -1], refs[-1]
        slope, shift, factor = constants[0:1, :], constants[1:2, :], constants[2:3, :]
        tiles = [
            (ref, first)
            for ref, block in zip(right_refs, right)
            for first in range(0, block.shape[0], TILE)
        ]

        def scores(tile):
            ref, first = tile
            return lax.dot_general(
                stacked(left_refs),
                ref[pl.ds(first, TILE), :],
                (((1,), (1,)), ((), ())),
                preferred_element_type=jnp.float32,
            )

        upcoming = scores(tiles[0])
        for index in range(len(tiles)):
            current = upcoming
            if index + 1 < len(tiles):
                upcoming = scores(tiles[index + 1])
            bent = jnp.tanh(current * slope + shift) * factor
            offset = factor
            if own and index == 0:
                row = lax.broadcasted_iota(jnp.int32, bent.shape, 0)
                column = lax.broadcasted_iota(jnp.int32, bent.shape, 1)
                half = TILE // 2
                partner = jnp.where(row < half, row + half, row - half)
                paired = jnp.logical_and(column == partner, row < TILE)
                offset = jnp.where(paired, -factor, factor)
            grads[:, pl.ds(index * TILE, TILE)] = (bent + offset).astype(jnp.bfloat16)
        total = jnp.dot(grads[...], stacked(right_refs), preferred_element_type=jnp.float32)
        if held is not None:
            total = total + refs[0][...]
        if rows_out is None:
            out[0][...] = total
        else:
            for at, ref in enumerate(out):
                ref[...] = total[at * rows_out : (at + 1) * rows_out].astype(jnp.bfloat16)

    shapes = (
        [jax.ShapeDtypeStruct((count, feature), jnp.float32)]
        if rows_out is None
        else [array(rows_out, feature)] * blocks
    )
    return call(
        name,
        body,
        shapes,
        [constants, *left, *right] + ([] if held is None else [held]),
        4 * count * others * feature,
        (),
        after,
        [pltpu.VMEM((count, others), jnp.bfloat16)],
    )


def add_half(whole, part, half, flops=0, after=()):
    rows = part.shape[0]

    def body(whole, part, out):
        out[pl.ds((1 - half) * rows, rows), :] = whole[pl.ds((1 - half) * rows, rows), :]
        here = pl.ds(half * rows, rows)
        out[here, :] = total_of([whole[here, :], part[...]]).astype(jnp.bfloat16)

    return call("add_half", body, [array(*whole.shape)], [whole, part], flops, after=after)[0]


def through_norms(core, picture, caption, terms):
    rows, feature = picture.shape

    def give_body(*refs):
        total = total_of([ref[pl.ds(rows, rows), :] for ref in refs[:-1]])
        refs[-1][...] = total.astype(jnp.bfloat16)

    got = to_core(call("give", give_body, [array(rows, feature)], terms, 4 * rows * feature)[0])

    def body(core, picture, caption, got, *refs):
        kept, (image_out, text_out) = refs[:-2], refs[-2:]

        def finish(raw, direct, out):
            unit, inverse = unit_of(raw[...].astype(jnp.float32))
            along = jnp.sum(unit * direct, axis=1, keepdims=True)
            out[...] = (inverse * (direct - unit * along)).astype(jnp.bfloat16)

        def direct_kept():
            return total_of([ref[pl.ds(0, rows), :] for ref in kept])

        @pl.when(core[0] == 0)
        def _():
            finish(picture, got[...].astype(jnp.float32), image_out)
            finish(caption, direct_kept(), text_out)

        @pl.when(core[0] != 0)
        def _():
            finish(picture, direct_kept(), image_out)
            finish(caption, got[...].astype(jnp.float32), text_out)

    return call(
        "final",
        body,
        [array(rows, feature)] * 2,
        [picture, caption, got, *terms],
        20 * rows * feature,
        [core],
    )


def on_device(
    picture_vectors, caption_vectors, ln_inverse_warmth, score_offset, objective_multiplier
):
    batch_total = picture_vectors.shape[0] * lax.axis_size(("blk", "grp"))
    parameters = [
        value.reshape(1) for value in (ln_inverse_warmth, score_offset, objective_multiplier)
    ]
    core = (lax.axis_index("blk") & (CORES - 1)).reshape(1)
    rows = picture_vectors.shape[0]
    keep, give, constants = unit_halves(
        core, parameters, batch_total, picture_vectors, caption_vectors
    )
    own = jnp.concatenate([keep, to_core(give)], axis=0)
    partner, below, above = cross(own), up(own), down(own)
    partner_above, partner_below, far = cross(above), up(partner), down(above)
    near = [own, partner, above, below]
    near_other = [to_core(block) for block in near]
    near_held = sums("near", constants, near, near_other, own=True)[0]
    partner_below, near_held = lax.optimization_barrier((partner_below, near_held))
    far, near_held = lax.optimization_barrier((far, near_held))
    last = cross(far[:rows]), up(partner_below[rows:])
    middle = [partner_above, partner_below, far]
    middle_other = [to_core(block) for block in middle]
    middle_held = sums("middle", constants, middle, near_other)[0]
    *last, middle_held = lax.optimization_barrier((*last, middle_held))
    last = pack(*last)
    last_other = to_core(last)
    last_held = sums("last", constants, [last], [*near_other, *middle_other])[0]

    last_0, last_1 = sums("last_rest", constants, [last], [last_other], last_held, rows_out=rows)
    to_far, to_below = cross(last_0), down(last_1)
    rest = [*middle_other, last_other]
    partner_above, partner_below, far = sums(
        "middle_rest", constants, middle, rest, middle_held, rows_out=2 * rows, after=[last_0]
    )
    far, partner_below = add_half(far, to_far, 0), add_half(partner_below, to_below, 1)
    to_above, to_partner, to_above_too = up(far), down(partner_below), cross(partner_above)
    own, partner, above, below = sums(
        "near_rest",
        constants,
        near,
        rest,
        near_held,
        rows_out=2 * rows,
        after=[far, partner_below],
    )
    above, partner = add(above, to_above, to_above_too), add(partner, to_partner)
    terms = [own, up(above), down(below), cross(partner)]
    image_grad, text_grad = through_norms(core, picture_vectors, caption_vectors, terms)
    return image_grad, text_grad


def solution(mesh):
    return jax.shard_map(
        on_device,
        mesh=mesh,
        in_specs=(P(("blk", "grp"), None), P(("blk", "grp"), None), P(), P(), P()),
        out_specs=(P(("blk", "grp"), None), P(("blk", "grp"), None)),
        check_vma=False,
    )
```

time: 471 us -> 82.7 us (0.18)
  waiting for transfers between devices: 263 us -> 19.4 us
  matrix products: 140 us -> 0 us
  Pallas kernels: 0 us -> 27.1 us
  local copies, waits for them, and re-layouts: 19.1 us -> 2.03 us
  between operations: 16.1 us -> 2.76 us
  starting transfers between devices: 18.6 us -> 31.2 us
  other arithmetic: 11.2 us -> 0 us
    dot_general x48 -> x0, matrix products: 140 us -> none  [the longest x16 79.7 us: tile_terms(): jnp.dot(score_derivative, visiting, preferred_element_type=jnp.float32)]
    ppermute x31 -> x26, waiting for transfers between devices: 129 us -> 19.4 us  [sender(): return lambda value: lax.ppermute(value, ('blk', 'grp'), pairs)]
    reduce_scatter x1 -> x0, waiting for transfers between devices: 78.5 us -> none  [on_device(): lax.psum_scatter(image_part, 'grp', scatter_dimension=0, tiled=True)]
    all_gather x1 -> x0, waiting for transfers between devices: 54.9 us -> none  [on_device(): image_group = lax.all_gather(image_half, 'grp', axis=0, tiled=True)]
    pallas_call x0 -> x14, Pallas kernels: none -> 27.1 us  [the longest x13 26.1 us: call(): pl.pallas_call(lambda *refs: body(*refs[len(after):]), name=name, out_sha...]
    while x45 -> x0, local copies, waits for them, and re-layouts: 16.8 us -> none
    ppermute x31 -> x26, starting transfers between devices: 18.5 us -> 31.2 us  [sender(): return lambda value: lax.ppermute(value, ('blk', 'grp'), pairs)]
    convert_element_type x4 -> x0, other arithmetic: 6.56 us -> none  [the longest x2 2.93 us: through_norm(): return (inverse * (direct - unit * along)).astype(jnp.bfloat16)]
  transfers between devices with their start and end apart: 33 -> 26, of which waited for: 18 -> 10; matrix products, arithmetic and copies ran while one was open for 17% -> 0% of each run, Pallas kernels for 0% -> 29%
where the time goes in v1:
time: 82.7 us; the launch traced here: 82.5 us
  starting transfers between devices  31.2 us (38%)
  Pallas kernels  27.1 us (33%)
  waiting for transfers between devices  19.4 us (23%)
  between operations  2.76 us (3%)
  local copies, waits for them, and re-layouts  2.03 us (2%)
    ppermute x26, starting transfers between devices, sender(): return lambda value: lax.ppermute(value, ('blk', 'grp'), pairs)  31.2 us
    pallas_call x13, Pallas kernels, call(): pl.pallas_call(lambda *refs: body(*refs[len(after):]), name=name, out_sha...  26.1 us
    ppermute x26, waiting for transfers between devices, sender(): return lambda value: lax.ppermute(value, ('blk', 'grp'), pairs)  19.4 us
    unnamed x9, local copies, waits for them, and re-layouts  1.95 us
  transfers between devices with their start and end apart: 26, of which 10 were waited for; matrix products, arithmetic and copies ran while one was open for 0% of the time, Pallas kernels for 29%

profile of v1, /device:TPU:1, one launch (start us, length us, event | category | flops | bytes accessed | tf_op | source)
XLA Modules:
  0.0 82.5 jit_solution(12142471757112096658)
XLA Ops:
  2.6 1.0 %copy-done = bf16[128,1152]{1,0:T(8,128)(2,1)S(1)} copy-done((bf16[128,1152]{1,0:T(8,128)(2,1)S(1)}, bf16[128,1152]{1,0:T(8,128)(2,1)}, u32[]{:S(2)}) %copy-start) | copy-done | bytes 294936
  3.5 1.0 %copy-done.2 = bf16[128,1152]{1,0:T(8,128)(2,1)S(1)} copy-done((bf16[128,1152]{1,0:T(8,128)(2,1)S(1)}, bf16[128,1152]{1,0:T(8,128)(2,1)}, u32[]{:S(2)}) %copy-start.2) | copy-done | bytes 294936
  4.5 1.0 %units.1 = (bf16[128,1152]{1,0:T(8,128)(2,1)S(1)}, bf16[128,1152]{1,0:T(8,128)(2,1)S(1)}, f32[8,256]{1,0:T(8,128)S(1)}) custom-call(s32[1]{0:T(128)} %bitcast.core.refs_0_, f32[1]{0:T(128)} %bitcast.4.warmth, f32[1]{0:T(128)} %bitcast.5.score_offset, f32[1]{0:T(128)} %bitcast.6.multiplier, bf16[128,1152]{1,0:T(8,128)(2,1)S(1)} %copy-done, ...), custom_call_target="tpu_custom_call" | custom-call | tf_op jit(solution)/shard_map/units/pallas_call | solution.py:114
  5.5 1.5 %collective-permute-start = (bf16[128,1152]{1,0:T(8,128)(2,1)S(1)}, bf16[128,1152]{1,0:T(8,128)(2,1)S(1)}, u32[]{:S(2)}, u32[]{:S(2)}) collective-permute-start(bf16[128,1152]{1,0:T(8,128)(2,1)S(1)} %get-tuple-element.23), channel_id=1, source_target_pairs={{0,8},{8,0},{2,10},{10,2},{4,12},{12,4},{6,14},{14,6},{16,24},{24,... | collective-permute-start | bytes 884744 | tf_op jit(solution)/shard_map/ppermute | solution.py:30
  7.1 1.2 %collective-permute-done = bf16[128,1152]{1,0:T(8,128)(2,1)S(1)} collective-permute-done((bf16[128,1152]{1,0:T(8,128)(2,1)S(1)}, bf16[128,1152]{1,0:T(8,128)(2,1)S(1)}, u32[]{:S(2)}, u32[]{:S(2)}) %collective-permute-start) | collective-permute-done | bytes 294944 | tf_op jit(solution)/shard_map/ppermute | solution.py:30
  8.3 1.8 %collective-permute-start.5 = (bf16[256,1152]{1,0:T(8,128)(2,1)S(1)}, bf16[256,1152]{1,0:T(8,128)(2,1)S(1)}, u32[]{:S(2)}, u32[]{:S(2)}) collective-permute-start(bf16[256,1152]{1,0:T(8,128)(2,1)S(1)} %constant_dynamic-update-slice_fusion.refs_1_.refs_3_), channel_id=1, source_target_pairs={{0,16},{8,10},{2,18},{10,12},{4,20},{12,14},{6,22},{14,8},{16,32},... | collective-permute-start | bytes 1769480 | tf_op jit(solution)/shard_map/ppermute | solution.py:30
  10.1 2.5 %collective-permute-start.3 = (bf16[256,1152]{1,0:T(8,128)(2,1)S(1)}, bf16[256,1152]{1,0:T(8,128)(2,1)S(1)}, u32[]{:S(2)}, u32[]{:S(2)}) collective-permute-start(bf16[256,1152]{1,0:T(8,128)(2,1)S(1)} %constant_dynamic-update-slice_fusion.refs_1_.refs_3_), channel_id=1, source_target_pairs={{0,64},{8,73},{2,66},{10,75},{4,68},{12,77},{6,70},{14,79},{16,80}... | collective-permute-start | bytes 1769480 | tf_op jit(solution)/shard_map/ppermute | solution.py:30
  12.5 2.2 %collective-permute-start.1 = (bf16[256,1152]{1,0:T(8,128)(2,1)S(1)}, bf16[256,1152]{1,0:T(8,128)(2,1)S(1)}, u32[]{:S(2)}, u32[]{:S(2)}) collective-permute-start(bf16[256,1152]{1,0:T(8,128)(2,1)S(1)} %constant_dynamic-update-slice_fusion.refs_1_.refs_3_), channel_id=1, source_target_pairs={{0,48},{8,14},{2,50},{10,8},{4,52},{12,10},{6,54},{14,12},{16,0},{... | collective-permute-start | bytes 1769480 | tf_op jit(solution)/shard_map/ppermute | solution.py:30
  14.8 4.7 %collective-permute-done.5.refs_4_.refs_6_ = bf16[256,1152]{1,0:T(8,128)(2,1)S(1)} collective-permute-done((bf16[256,1152]{1,0:T(8,128)(2,1)S(1)}, bf16[256,1152]{1,0:T(8,128)(2,1)S(1)}, u32[]{:S(2)}, u32[]{:S(2)}) %collective-permute-start.5) | collective-permute-done | bytes 589856 | tf_op jit(solution)/shard_map/ppermute | solution.py:30
  19.5 0.4 collective-permute-start.9
  19.8 0.2 collective-permute-done.3.refs_2_.refs_4_
  20.0 0.3 collective-permute-start.7
  20.3 1.3 %collective-permute-done.1.refs_3_.refs_5_ = bf16[256,1152]{1,0:T(8,128)(2,1)S(1)} collective-permute-done((bf16[256,1152]{1,0:T(8,128)(2,1)S(1)}, bf16[256,1152]{1,0:T(8,128)(2,1)S(1)}, u32[]{:S(2)}, u32[]{:S(2)}) %collective-permute-start.1) | collective-permute-done | bytes 589856 | tf_op jit(solution)/shard_map/ppermute | solution.py:30
  21.6 0.2 collective-permute-start.8
  21.8 1.6 %collective-permute-start.4 = (bf16[256,1152]{1,0:T(8,128)(2,1)S(1)}, bf16[256,1152]{1,0:T(8,128)(2,1)S(1)}, u32[]{:S(2)}, u32[]{:S(2)}) collective-permute-start(bf16[256,1152]{1,0:T(8,128)(2,1)S(1)} %collective-permute-done.3.refs_2_.refs_4_), channel_id=1, source_target_pairs={{0,16},{8,10},{2,18},{10,12},{4,20},{12,14},{6,22},{14,8},{16,32},... | collective-permute-start | bytes 1769480 | tf_op jit(solution)/shard_map/ppermute | solution.py:30
  23.4 2.1 %collective-permute-start.2 = (bf16[256,1152]{1,0:T(8,128)(2,1)S(1)}, bf16[256,1152]{1,0:T(8,128)(2,1)S(1)}, u32[]{:S(2)}, u32[]{:S(2)}) collective-permute-start(bf16[256,1152]{1,0:T(8,128)(2,1)S(1)} %collective-permute-done.1.refs_3_.refs_5_), channel_id=1, source_target_pairs={{0,48},{8,14},{2,50},{10,8},{4,52},{12,10},{6,54},{14,12},{16,0},{... | collective-permute-start | bytes 1769480 | tf_op jit(solution)/shard_map/ppermute | solution.py:30
  25.5 1.8 %collective-permute-start.12 = (bf16[256,1152]{1,0:T(8,128)(2,1)S(1)}, bf16[256,1152]{1,0:T(8,128)(2,1)S(1)}, u32[]{:S(2)}, u32[]{:S(2)}) collective-permute-start(bf16[256,1152]{1,0:T(8,128)(2,1)S(1)} %collective-permute-done.1.refs_3_.refs_5_), channel_id=1, source_target_pairs={{0,64},{8,73},{2,66},{10,75},{4,68},{12,77},{6,70},{14,79},{16,80}... | collective-permute-start | bytes 1769480 | tf_op jit(solution)/shard_map/ppermute | solution.py:30
  27.3 5.8 %near.1.refs_11_ = f32[1024,1152]{1,0:T(8,128)S(1)} custom-call(f32[8,256]{1,0:T(8,128)S(1)} %get-tuple-element.21.refs_0_.refs_1_.refs_2_, bf16[256,1152]{1,0:T(8,128)(2,1)S(1)} %constant_dynamic-update-slice_fusion.refs_1_.refs_3_, bf16[256,1152]{1,0:T(8,128)(2,1)S(1)} %collective-permute-done.3.refs_2_.refs_4_, ...), custom_call_target="tpu_custom_call" | custom-call | flops 75497472 | bytes 110656 | tf_op jit(solution)/shard_map/near/pallas_call | solution.py:46
  33.2 1.0 %collective-permute-start.11 = (bf16[128,1152]{1,0:T(8,128)(2,1)S(1)}, bf16[128,1152]{1,0:T(8,128)(2,1)S(1)}, u32[]{:S(2)}, u32[]{:S(2)}) collective-permute-start(bf16[128,1152]{1,0:T(8,128)(2,1)S(1)} %slice.7), channel_id=1, source_target_pairs={{0,16},{8,10},{2,18},{10,12},{4,20},{12,14},{6,22},{14,8},{16,32},... | collective-permute-start | bytes 884744 | tf_op jit(solution)/shard_map/ppermute | solution.py:30
  34.2 1.8 %collective-permute-start.10 = (bf16[128,1152]{1,0:T(8,128)(2,1)S(1)}, bf16[128,1152]{1,0:T(8,128)(2,1)S(1)}, u32[]{:S(2)}, u32[]{:S(2)}) collective-permute-start(bf16[128,1152]{1,0:T(8,128)(2,1)S(1)} %slice.6), channel_id=1, source_target_pairs={{0,64},{8,73},{2,66},{10,75},{4,68},{12,77},{6,70},{14,79},{16,80}... | collective-permute-start | bytes 884744 | tf_op jit(solution)/shard_map/ppermute | solution.py:30
  36.0 0.5 collective-permute-start.15
  36.5 4.4 %middle.1.refs_9_ = f32[768,1152]{1,0:T(8,128)S(1)} custom-call(f32[8,256]{1,0:T(8,128)S(1)} %get-tuple-element.21.refs_0_.refs_1_.refs_2_, bf16[256,1152]{1,0:T(8,128)(2,1)S(1)} %collective-permute-done.12.refs_1_.refs_2_, bf16[256,1152]{1,0:T(8,128)(2,1)S(1)} %collective-permute-done.4.refs_2_.refs_3_, ...), custom_call_target="tpu_custom_call" | custom-call | flops 56623104 | bytes 92224 | tf_op jit(solution)/shard_map/middle/pallas_call | solution.py:46
  40.9 0.3 collective-permute-done.10.refs_0_
  41.3 0.8 %collective-permute-start.13 = (bf16[256,1152]{1,0:T(8,128)(2,1)S(1)}, bf16[256,1152]{1,0:T(8,128)(2,1)S(1)}, u32[]{:S(2)}, u32[]{:S(2)}) collective-permute-start(bf16[256,1152]{1,0:T(8,128)(2,1)S(1)} %pack.1.refs_1_), channel_id=1, source_target_pairs={{0,8},{8,0},{2,10},{10,2},{4,12},{12,4},{6,14},{14,6},{16,24},{24,... | collective-permute-start | bytes 1769480 | tf_op jit(solution)/shard_map/ppermute | solution.py:30
  42.1 2.6 %last.1.refs_3_ = f32[256,1152]{1,0:T(8,128)S(1)} custom-call(f32[8,256]{1,0:T(8,128)S(1)} %get-tuple-element.21.refs_0_.refs_1_.refs_2_, bf16[256,1152]{1,0:T(8,128)(2,1)S(1)} %pack.1.refs_1_, bf16[256,1152]{1,0:T(8,128)(2,1)S(1)} %collective-permute-done.6.refs_5_.refs_4_.refs_2_, bf16[256,1152]{1,0:T(8,128)(2,1)S(1)} %collective-permute-done.7.refs_6_.refs_5_.refs_3_, ...), custom_call_target="tpu_custom_call" | custom-call | flops 33030144 | bytes 83008 | tf_op jit(solution)/shard_map/last/pallas_call | solution.py:46
  44.8 0.9 %last_rest.1 = (bf16[128,1152]{1,0:T(8,128)(2,1)S(1)}, bf16[128,1152]{1,0:T(8,128)(2,1)S(1)}) custom-call(f32[8,256]{1,0:T(8,128)S(1)} %get-tuple-element.21.refs_0_.refs_1_.refs_2_, bf16[256,1152]{1,0:T(8,128)(2,1)S(1)} %pack.1.refs_1_, bf16[256,1152]{1,0:T(8,128)(2,1)S(1)} %collective-permute-done.13.refs_2_.refs_8_.refs_10_, f32[256,1152]{1,0:T(8,128)S(1)} %last.1.refs_3_), custom_call_target="tpu_custom_call" | custom-call | flops 4718592 | bytes 36928 | tf_op jit(solution)/shard_map/last_rest/pallas_call | solution.py:46
  45.7 3.2 %collective-permute-start.18 = (bf16[128,1152]{1,0:T(8,128)(2,1)S(1)}, bf16[128,1152]{1,0:T(8,128)(2,1)S(1)}, u32[]{:S(2)}, u32[]{:S(2)}) collective-permute-start(bf16[128,1152]{1,0:T(8,128)(2,1)S(1)} %get-tuple-element.33), channel_id=1, source_target_pairs={{0,48},{8,14},{2,50},{10,8},{4,52},{12,10},{6,54},{14,12},{16,0},{... | collective-permute-start | bytes 884744 | tf_op jit(solution)/shard_map/ppermute | solution.py:30
  48.9 1.8 %collective-permute-start.17 = (bf16[128,1152]{1,0:T(8,128)(2,1)S(1)}, bf16[128,1152]{1,0:T(8,128)(2,1)S(1)}, u32[]{:S(2)}, u32[]{:S(2)}) collective-permute-start(bf16[128,1152]{1,0:T(8,128)(2,1)S(1)} %get-tuple-element.29.refs_0_), channel_id=1, source_target_pairs={{0,64},{8,73},{2,66},{10,75},{4,68},{12,77},{6,70},{14,79},{16,80}... | collective-permute-start | bytes 884744 | tf_op jit(solution)/shard_map/ppermute | solution.py:30
  50.7 4.4 %middle_rest.1 = (bf16[256,1152]{1,0:T(8,128)(2,1)S(1)}, bf16[256,1152]{1,0:T(8,128)(2,1)S(1)}, bf16[256,1152]{1,0:T(8,128)(2,1)S(1)}) custom-call(bf16[128,1152]{1,0:T(8,128)(2,1)S(1)} %get-tuple-element.29.refs_0_, f32[8,256]{1,0:T(8,128)S(1)} %get-tuple-element.21.refs_0_.refs_1_.refs_2_, bf16[256,1152]{1,0:T(8,128)(2,1)S(1)} %collective-permute-done.12.refs_1_.refs_2_, ...), custom_call_target="tpu_custom_call" | custom-call | flops 56623104 | bytes 119872 | tf_op jit(solution)/shard_map/middle_rest/pallas_call | solution.py:46
  55.2 0.1 add_half.3.refs_1_
  55.3 0.6 collective-permute-start.23
  55.8 1.8 %collective-permute-start.20 = (bf16[256,1152]{1,0:T(8,128)(2,1)S(1)}, bf16[256,1152]{1,0:T(8,128)(2,1)S(1)}, u32[]{:S(2)}, u32[]{:S(2)}) collective-permute-start(bf16[256,1152]{1,0:T(8,128)(2,1)S(1)} %get-tuple-element.37), channel_id=1, source_target_pairs={{0,64},{8,73},{2,66},{10,75},{4,68},{12,77},{6,70},{14,79},{16,80}... | collective-permute-start | bytes 1769480 | tf_op jit(solution)/shard_map/ppermute | solution.py:30
  57.7 0.1 add_half.2.refs_0_
  57.8 0.3 collective-permute-start.19
  58.1 5.8 %near_rest.1 = (bf16[256,1152]{1,0:T(8,128)(2,1)S(1)}, bf16[256,1152]{1,0:T(8,128)(2,1)S(1)}, bf16[256,1152]{1,0:T(8,128)(2,1)S(1)}, bf16[256,1152]{1,0:T(8,128)(2,1)S(1)}) custom-call(bf16[256,1152]{1,0:T(8,128)(2,1)S(1)} %add_half.2.refs_0_, bf16[256,1152]{1,0:T(8,128)(2,1)S(1)} %add_half.3.refs_1_, ...), custom_call_target="tpu_custom_call" | custom-call | flops 75497472 | bytes 147520 | tf_op jit(solution)/shard_map/near_rest/pallas_call | solution.py:46
  63.9 2.7 %collective-permute-start.22 = (bf16[256,1152]{1,0:T(8,128)(2,1)S(1)}, bf16[256,1152]{1,0:T(8,128)(2,1)S(1)}, u32[]{:S(2)}, u32[]{:S(2)}) collective-permute-start(bf16[256,1152]{1,0:T(8,128)(2,1)S(1)} %get-tuple-element.38), channel_id=1, source_target_pairs={{0,48},{8,14},{2,50},{10,8},{4,52},{12,10},{6,54},{14,12},{16,0},{... | collective-permute-start | bytes 1769480 | tf_op jit(solution)/shard_map/ppermute | solution.py:30
  66.7 0.1 add.3
  66.8 0.9 %collective-permute-start.24 = (bf16[256,1152]{1,0:T(8,128)(2,1)S(1)}, bf16[256,1152]{1,0:T(8,128)(2,1)S(1)}, u32[]{:S(2)}, u32[]{:S(2)}) collective-permute-start(bf16[256,1152]{1,0:T(8,128)(2,1)S(1)} %add.3), channel_id=1, source_target_pairs={{0,64},{8,73},{2,66},{10,75},{4,68},{12,77},{6,70},{14,79},{16,80}... | collective-permute-start | bytes 1769480 | tf_op jit(solution)/shard_map/ppermute | solution.py:30
  67.7 0.3 collective-permute-done.19.refs_1_
  68.0 0.2 add.2
  68.2 0.1 collective-permute-start.21
  68.3 5.2 %collective-permute-done.22.refs_2_.refs_6_ = bf16[256,1152]{1,0:T(8,128)(2,1)S(1)} collective-permute-done((bf16[256,1152]{1,0:T(8,128)(2,1)S(1)}, bf16[256,1152]{1,0:T(8,128)(2,1)S(1)}, u32[]{:S(2)}, u32[]{:S(2)}) %collective-permute-start.22) | collective-permute-done | bytes 589856 | tf_op jit(solution)/shard_map/ppermute | solution.py:30
  73.5 3.6 %collective-permute-done.24.refs_3_.refs_7_ = bf16[256,1152]{1,0:T(8,128)(2,1)S(1)} collective-permute-done((bf16[256,1152]{1,0:T(8,128)(2,1)S(1)}, bf16[256,1152]{1,0:T(8,128)(2,1)S(1)}, u32[]{:S(2)}, u32[]{:S(2)}) %collective-permute-start.24) | collective-permute-done | bytes 589856 | tf_op jit(solution)/shard_map/ppermute | solution.py:30
  77.1 1.4 %collective-permute-done.21.refs_1_.refs_5_ = bf16[256,1152]{1,0:T(8,128)(2,1)S(1)} collective-permute-done((bf16[256,1152]{1,0:T(8,128)(2,1)S(1)}, bf16[256,1152]{1,0:T(8,128)(2,1)S(1)}, u32[]{:S(2)}, u32[]{:S(2)}) %collective-permute-start.21) | collective-permute-done | bytes 589856 | tf_op jit(solution)/shard_map/ppermute | solution.py:30
  78.5 0.1 give.1
  78.7 1.3 %collective-permute-start.25 = (bf16[128,1152]{1,0:T(8,128)(2,1)S(1)}, bf16[128,1152]{1,0:T(8,128)(2,1)S(1)}, u32[]{:S(2)}, u32[]{:S(2)}) collective-permute-start(bf16[128,1152]{1,0:T(8,128)(2,1)S(1)} %give.1), channel_id=1, source_target_pairs={{0,8},{8,0},{2,10},{10,2},{4,12},{12,4},{6,14},{14,6},{16,24},{24,... | collective-permute-start | bytes 884744 | tf_op jit(solution)/shard_map/ppermute | solution.py:30
  79.9 1.2 %collective-permute-done.25.refs_3_ = bf16[128,1152]{1,0:T(8,128)(2,1)S(1)} collective-permute-done((bf16[128,1152]{1,0:T(8,128)(2,1)S(1)}, bf16[128,1152]{1,0:T(8,128)(2,1)S(1)}, u32[]{:S(2)}, u32[]{:S(2)}) %collective-permute-start.25) | collective-permute-done | bytes 294944 | tf_op jit(solution)/shard_map/ppermute | solution.py:30
  81.2 1.4 %final.1 = (bf16[128,1152]{1,0:T(8,128)(2,1)}, bf16[128,1152]{1,0:T(8,128)(2,1)}) custom-call(s32[1]{0:T(128)} %bitcast.core.refs_0_, bf16[128,1152]{1,0:T(8,128)(2,1)S(1)} %copy-done.1, bf16[128,1152]{1,0:T(8,128)(2,1)S(1)} %copy-done.3, bf16[128,1152]{1,0:T(8,128)(2,1)S(1)} %collective-permute-done.25.refs_3_, ...), custom_call_target="tpu_custom_call" | custom-call | flops 46080 | bytes 59904 | tf_op jit(solution)/shard_map/final/pallas_call | solution.py:46
  (30 shorter events, 0.2 us)
Async XLA Ops:
  2.6 1.0 %copy-start = (bf16[128,1152]{1,0:T(8,128)(2,1)S(1)}, bf16[128,1152]{1,0:T(8,128)(2,1)}, u32[]{:S(2)}) copy-start(bf16[128,1152]{1,0:T(8,128)(2,1)} %refs_1_.1) | copy-start | bytes 884740
  3.5 1.0 %copy-start.2 = (bf16[128,1152]{1,0:T(8,128)(2,1)S(1)}, bf16[128,1152]{1,0:T(8,128)(2,1)}, u32[]{:S(2)}) copy-start(bf16[128,1152]{1,0:T(8,128)(2,1)} %refs_2_.1) | copy-start | bytes 884740
  5.5 2.7 %collective-permute-start = (bf16[128,1152]{1,0:T(8,128)(2,1)S(1)}, bf16[128,1152]{1,0:T(8,128)(2,1)S(1)}, u32[]{:S(2)}, u32[]{:S(2)}) collective-permute-start(bf16[128,1152]{1,0:T(8,128)(2,1)S(1)} %get-tuple-element.23), channel_id=1, source_target_pairs={{0,8},{8,0},{2,10},{10,2},{4,12},{12,4},{6,14},{14,6},{16,24},{24,... | collective-permute-start | bytes 884744 | tf_op jit(solution)/shard_map/ppermute | solution.py:30
  8.3 11.2 %collective-permute-start.5 = (bf16[256,1152]{1,0:T(8,128)(2,1)S(1)}, bf16[256,1152]{1,0:T(8,128)(2,1)S(1)}, u32[]{:S(2)}, u32[]{:S(2)}) collective-permute-start(bf16[256,1152]{1,0:T(8,128)(2,1)S(1)} %constant_dynamic-update-slice_fusion.refs_1_.refs_3_), channel_id=1, source_target_pairs={{0,16},{8,10},{2,18},{10,12},{4,20},{12,14},{6,22},{14,8},{16,32},... | collective-permute-start | bytes 1769480 | tf_op jit(solution)/shard_map/ppermute | solution.py:30
  10.1 9.9 %collective-permute-start.3 = (bf16[256,1152]{1,0:T(8,128)(2,1)S(1)}, bf16[256,1152]{1,0:T(8,128)(2,1)S(1)}, u32[]{:S(2)}, u32[]{:S(2)}) collective-permute-start(bf16[256,1152]{1,0:T(8,128)(2,1)S(1)} %constant_dynamic-update-slice_fusion.refs_1_.refs_3_), channel_id=1, source_target_pairs={{0,64},{8,73},{2,66},{10,75},{4,68},{12,77},{6,70},{14,79},{16,80}... | collective-permute-start | bytes 1769480 | tf_op jit(solution)/shard_map/ppermute | solution.py:30
  12.5 9.0 %collective-permute-start.1 = (bf16[256,1152]{1,0:T(8,128)(2,1)S(1)}, bf16[256,1152]{1,0:T(8,128)(2,1)S(1)}, u32[]{:S(2)}, u32[]{:S(2)}) collective-permute-start(bf16[256,1152]{1,0:T(8,128)(2,1)S(1)} %constant_dynamic-update-slice_fusion.refs_1_.refs_3_), channel_id=1, source_target_pairs={{0,48},{8,14},{2,50},{10,8},{4,52},{12,10},{6,54},{14,12},{16,0},{... | collective-permute-start | bytes 1769480 | tf_op jit(solution)/shard_map/ppermute | solution.py:30
  14.8 8.6 %collective-permute-start.6 = (bf16[256,1152]{1,0:T(8,128)(2,1)S(1)}, bf16[256,1152]{1,0:T(8,128)(2,1)S(1)}, u32[]{:S(2)}, u32[]{:S(2)}) collective-permute-start(bf16[256,1152]{1,0:T(8,128)(2,1)S(1)} %constant_dynamic-update-slice_fusion.refs_1_.refs_3_), channel_id=1, source_target_pairs={{0,8},{8,0},{2,10},{10,2},{4,12},{12,4},{6,14},{14,6},{16,24},{24,... | collective-permute-start | bytes 1769480 | tf_op jit(solution)/shard_map/ppermute | solution.py:30
  19.5 6.1 %collective-permute-start.9 = (bf16[256,1152]{1,0:T(8,128)(2,1)S(1)}, bf16[256,1152]{1,0:T(8,128)(2,1)S(1)}, u32[]{:S(2)}, u32[]{:S(2)}) collective-permute-start(bf16[256,1152]{1,0:T(8,128)(2,1)S(1)} %collective-permute-done.5.refs_4_.refs_6_), channel_id=1, source_target_pairs={{0,8},{8,0},{2,10},{10,2},{4,12},{12,4},{6,14},{14,6},{16,24},{24,... | collective-permute-start | bytes 1769480 | tf_op jit(solution)/shard_map/ppermute | solution.py:30
  20.0 7.3 %collective-permute-start.7 = (bf16[256,1152]{1,0:T(8,128)(2,1)S(1)}, bf16[256,1152]{1,0:T(8,128)(2,1)S(1)}, u32[]{:S(2)}, u32[]{:S(2)}) collective-permute-start(bf16[256,1152]{1,0:T(8,128)(2,1)S(1)} %collective-permute-done.3.refs_2_.refs_4_), channel_id=1, source_target_pairs={{0,8},{8,0},{2,10},{10,2},{4,12},{12,4},{6,14},{14,6},{16,24},{24,... | collective-permute-start | bytes 1769480 | tf_op jit(solution)/shard_map/ppermute | solution.py:30
  21.6 5.8 %collective-permute-start.8 = (bf16[256,1152]{1,0:T(8,128)(2,1)S(1)}, bf16[256,1152]{1,0:T(8,128)(2,1)S(1)}, u32[]{:S(2)}, u32[]{:S(2)}) collective-permute-start(bf16[256,1152]{1,0:T(8,128)(2,1)S(1)} %collective-permute-done.1.refs_3_.refs_5_), channel_id=1, source_target_pairs={{0,8},{8,0},{2,10},{10,2},{4,12},{12,4},{6,14},{14,6},{16,24},{24,... | collective-permute-start | bytes 1769480 | tf_op jit(solution)/shard_map/ppermute | solution.py:30
  21.8 11.4 %collective-permute-start.4 = (bf16[256,1152]{1,0:T(8,128)(2,1)S(1)}, bf16[256,1152]{1,0:T(8,128)(2,1)S(1)}, u32[]{:S(2)}, u32[]{:S(2)}) collective-permute-start(bf16[256,1152]{1,0:T(8,128)(2,1)S(1)} %collective-permute-done.3.refs_2_.refs_4_), channel_id=1, source_target_pairs={{0,16},{8,10},{2,18},{10,12},{4,20},{12,14},{6,22},{14,8},{16,32},... | collective-permute-start | bytes 1769480 | tf_op jit(solution)/shard_map/ppermute | solution.py:30
  23.4 9.7 %collective-permute-start.2 = (bf16[256,1152]{1,0:T(8,128)(2,1)S(1)}, bf16[256,1152]{1,0:T(8,128)(2,1)S(1)}, u32[]{:S(2)}, u32[]{:S(2)}) collective-permute-start(bf16[256,1152]{1,0:T(8,128)(2,1)S(1)} %collective-permute-done.1.refs_3_.refs_5_), channel_id=1, source_target_pairs={{0,48},{8,14},{2,50},{10,8},{4,52},{12,10},{6,54},{14,12},{16,0},{... | collective-permute-start | bytes 1769480 | tf_op jit(solution)/shard_map/ppermute | solution.py:30
  25.5 11.0 %collective-permute-start.12 = (bf16[256,1152]{1,0:T(8,128)(2,1)S(1)}, bf16[256,1152]{1,0:T(8,128)(2,1)S(1)}, u32[]{:S(2)}, u32[]{:S(2)}) collective-permute-start(bf16[256,1152]{1,0:T(8,128)(2,1)S(1)} %collective-permute-done.1.refs_3_.refs_5_), channel_id=1, source_target_pairs={{0,64},{8,73},{2,66},{10,75},{4,68},{12,77},{6,70},{14,79},{16,80}... | collective-permute-start | bytes 1769480 | tf_op jit(solution)/shard_map/ppermute | solution.py:30
  33.2 7.7 %collective-permute-start.11 = (bf16[128,1152]{1,0:T(8,128)(2,1)S(1)}, bf16[128,1152]{1,0:T(8,128)(2,1)S(1)}, u32[]{:S(2)}, u32[]{:S(2)}) collective-permute-start(bf16[128,1152]{1,0:T(8,128)(2,1)S(1)} %slice.7), channel_id=1, source_target_pairs={{0,16},{8,10},{2,18},{10,12},{4,20},{12,14},{6,22},{14,8},{16,32},... | collective-permute-start | bytes 884744 | tf_op jit(solution)/shard_map/ppermute | solution.py:30
  34.2 7.0 %collective-permute-start.10 = (bf16[128,1152]{1,0:T(8,128)(2,1)S(1)}, bf16[128,1152]{1,0:T(8,128)(2,1)S(1)}, u32[]{:S(2)}, u32[]{:S(2)}) collective-permute-start(bf16[128,1152]{1,0:T(8,128)(2,1)S(1)} %slice.6), channel_id=1, source_target_pairs={{0,64},{8,73},{2,66},{10,75},{4,68},{12,77},{6,70},{14,79},{16,80}... | collective-permute-start | bytes 884744 | tf_op jit(solution)/shard_map/ppermute | solution.py:30
  36.0 6.1 %collective-permute-start.16 = (bf16[256,1152]{1,0:T(8,128)(2,1)S(1)}, bf16[256,1152]{1,0:T(8,128)(2,1)S(1)}, u32[]{:S(2)}, u32[]{:S(2)}) collective-permute-start(bf16[256,1152]{1,0:T(8,128)(2,1)S(1)} %collective-permute-done.2.refs_3_.refs_4_), channel_id=1, source_target_pairs={{0,8},{8,0},{2,10},{10,2},{4,12},{12,4},{6,14},{14,6},{16,24},{24,... | collective-permute-start | bytes 1769480 | tf_op jit(solution)/shard_map/ppermute | solution.py:30
  36.0 6.1 %collective-permute-start.15 = (bf16[256,1152]{1,0:T(8,128)(2,1)S(1)}, bf16[256,1152]{1,0:T(8,128)(2,1)S(1)}, u32[]{:S(2)}, u32[]{:S(2)}) collective-permute-start(bf16[256,1152]{1,0:T(8,128)(2,1)S(1)} %collective-permute-done.4.refs_2_.refs_3_), channel_id=1, source_target_pairs={{0,8},{8,0},{2,10},{10,2},{4,12},{12,4},{6,14},{14,6},{16,24},{24,... | collective-permute-start | bytes 1769480 | tf_op jit(solution)/shard_map/ppermute | solution.py:30
  36.5 5.6 %collective-permute-start.14 = (bf16[256,1152]{1,0:T(8,128)(2,1)S(1)}, bf16[256,1152]{1,0:T(8,128)(2,1)S(1)}, u32[]{:S(2)}, u32[]{:S(2)}) collective-permute-start(bf16[256,1152]{1,0:T(8,128)(2,1)S(1)} %collective-permute-done.12.refs_1_.refs_2_), channel_id=1, source_target_pairs={{0,8},{8,0},{2,10},{10,2},{4,12},{12,4},{6,14},{14,6},{16,24},{24,... | collective-permute-start | bytes 1769480 | tf_op jit(solution)/shard_map/ppermute | solution.py:30
  41.3 3.5 %collective-permute-start.13 = (bf16[256,1152]{1,0:T(8,128)(2,1)S(1)}, bf16[256,1152]{1,0:T(8,128)(2,1)S(1)}, u32[]{:S(2)}, u32[]{:S(2)}) collective-permute-start(bf16[256,1152]{1,0:T(8,128)(2,1)S(1)} %pack.1.refs_1_), channel_id=1, source_target_pairs={{0,8},{8,0},{2,10},{10,2},{4,12},{12,4},{6,14},{14,6},{16,24},{24,... | collective-permute-start | bytes 1769480 | tf_op jit(solution)/shard_map/ppermute | solution.py:30
  45.7 9.5 %collective-permute-start.18 = (bf16[128,1152]{1,0:T(8,128)(2,1)S(1)}, bf16[128,1152]{1,0:T(8,128)(2,1)S(1)}, u32[]{:S(2)}, u32[]{:S(2)}) collective-permute-start(bf16[128,1152]{1,0:T(8,128)(2,1)S(1)} %get-tuple-element.33), channel_id=1, source_target_pairs={{0,48},{8,14},{2,50},{10,8},{4,52},{12,10},{6,54},{14,12},{16,0},{... | collective-permute-start | bytes 884744 | tf_op jit(solution)/shard_map/ppermute | solution.py:30
  48.9 8.8 %collective-permute-start.17 = (bf16[128,1152]{1,0:T(8,128)(2,1)S(1)}, bf16[128,1152]{1,0:T(8,128)(2,1)S(1)}, u32[]{:S(2)}, u32[]{:S(2)}) collective-permute-start(bf16[128,1152]{1,0:T(8,128)(2,1)S(1)} %get-tuple-element.29.refs_0_), channel_id=1, source_target_pairs={{0,64},{8,73},{2,66},{10,75},{4,68},{12,77},{6,70},{14,79},{16,80}... | collective-permute-start | bytes 884744 | tf_op jit(solution)/shard_map/ppermute | solution.py:30
  55.3 11.4 %collective-permute-start.23 = (bf16[256,1152]{1,0:T(8,128)(2,1)S(1)}, bf16[256,1152]{1,0:T(8,128)(2,1)S(1)}, u32[]{:S(2)}, u32[]{:S(2)}) collective-permute-start(bf16[256,1152]{1,0:T(8,128)(2,1)S(1)} %add_half.3.refs_1_), channel_id=1, source_target_pairs={{0,48},{8,14},{2,50},{10,8},{4,52},{12,10},{6,54},{14,12},{16,0},{... | collective-permute-start | bytes 1769480 | tf_op jit(solution)/shard_map/ppermute | solution.py:30
  55.8 11.9 %collective-permute-start.20 = (bf16[256,1152]{1,0:T(8,128)(2,1)S(1)}, bf16[256,1152]{1,0:T(8,128)(2,1)S(1)}, u32[]{:S(2)}, u32[]{:S(2)}) collective-permute-start(bf16[256,1152]{1,0:T(8,128)(2,1)S(1)} %get-tuple-element.37), channel_id=1, source_target_pairs={{0,64},{8,73},{2,66},{10,75},{4,68},{12,77},{6,70},{14,79},{16,80}... | collective-permute-start | bytes 1769480 | tf_op jit(solution)/shard_map/ppermute | solution.py:30
  57.8 10.2 %collective-permute-start.19 = (bf16[256,1152]{1,0:T(8,128)(2,1)S(1)}, bf16[256,1152]{1,0:T(8,128)(2,1)S(1)}, u32[]{:S(2)}, u32[]{:S(2)}) collective-permute-start(bf16[256,1152]{1,0:T(8,128)(2,1)S(1)} %add_half.2.refs_0_), channel_id=1, source_target_pairs={{0,16},{8,10},{2,18},{10,12},{4,20},{12,14},{6,22},{14,8},{16,32},... | collective-permute-start | bytes 1769480 | tf_op jit(solution)/shard_map/ppermute | solution.py:30
  63.9 17.3 %copy-start.1 = (bf16[128,1152]{1,0:T(8,128)(2,1)S(1)}, bf16[128,1152]{1,0:T(8,128)(2,1)}, u32[]{:S(2)}) copy-start(bf16[128,1152]{1,0:T(8,128)(2,1)} %refs_1_.1) | copy-start | bytes 884740
  63.9 17.3 %copy-start.3 = (bf16[128,1152]{1,0:T(8,128)(2,1)S(1)}, bf16[128,1152]{1,0:T(8,128)(2,1)}, u32[]{:S(2)}) copy-start(bf16[128,1152]{1,0:T(8,128)(2,1)} %refs_2_.1) | copy-start | bytes 884740
  63.9 9.6 %collective-permute-start.22 = (bf16[256,1152]{1,0:T(8,128)(2,1)S(1)}, bf16[256,1152]{1,0:T(8,128)(2,1)S(1)}, u32[]{:S(2)}, u32[]{:S(2)}) collective-permute-start(bf16[256,1152]{1,0:T(8,128)(2,1)S(1)} %get-tuple-element.38), channel_id=1, source_target_pairs={{0,48},{8,14},{2,50},{10,8},{4,52},{12,10},{6,54},{14,12},{16,0},{... | collective-permute-start | bytes 1769480 | tf_op jit(solution)/shard_map/ppermute | solution.py:30
  66.8 10.3 %collective-permute-start.24 = (bf16[256,1152]{1,0:T(8,128)(2,1)S(1)}, bf16[256,1152]{1,0:T(8,128)(2,1)S(1)}, u32[]{:S(2)}, u32[]{:S(2)}) collective-permute-start(bf16[256,1152]{1,0:T(8,128)(2,1)S(1)} %add.3), channel_id=1, source_target_pairs={{0,64},{8,73},{2,66},{10,75},{4,68},{12,77},{6,70},{14,79},{16,80}... | collective-permute-start | bytes 1769480 | tf_op jit(solution)/shard_map/ppermute | solution.py:30
  68.2 10.3 %collective-permute-start.21 = (bf16[256,1152]{1,0:T(8,128)(2,1)S(1)}, bf16[256,1152]{1,0:T(8,128)(2,1)S(1)}, u32[]{:S(2)}, u32[]{:S(2)}) collective-permute-start(bf16[256,1152]{1,0:T(8,128)(2,1)S(1)} %add.2), channel_id=1, source_target_pairs={{0,16},{8,10},{2,18},{10,12},{4,20},{12,14},{6,22},{14,8},{16,32},... | collective-permute-start | bytes 1769480 | tf_op jit(solution)/shard_map/ppermute | solution.py:30
  78.7 2.5 %collective-permute-start.25 = (bf16[128,1152]{1,0:T(8,128)(2,1)S(1)}, bf16[128,1152]{1,0:T(8,128)(2,1)S(1)}, u32[]{:S(2)}, u32[]{:S(2)}) collective-permute-start(bf16[128,1152]{1,0:T(8,128)(2,1)S(1)} %give.1), channel_id=1, source_target_pairs={{0,8},{8,0},{2,10},{10,2},{4,12},{12,4},{6,14},{14,6},{16,24},{24,... | collective-permute-start | bytes 884744 | tf_op jit(solution)/shard_map/ppermute | solution.py:30

commit v2 on v1

--- a/solution.py
+++ b/solution.py
@@ -10,7 +10,6 @@
 RING = 4
 CORES = 2
 TILE = 256
-COPY_ROWS = 32
 VMEM_BYTES = 24 * 1024 * 1024
 
 
@@ -30,15 +29,19 @@
     return lambda value: lax.ppermute(value, ("blk", "grp"), pairs)
 
 
+def sender_pair(move):
+    return sender(move), sender(lambda *at: (*move(*at)[:3], 1 - at[3]))
+
+
 def ring(steps):
-    return sender(
+    return sender_pair(
         lambda x, y, z, c: (x, y, (z + steps) % RING, c) if c else (x, (y + steps) % RING, z, c)
     )
 
 
 to_core = sender(lambda x, y, z, c: (x, y, z, 1 - c))
-cross = sender(lambda x, y, z, c: (3 - x if c else x ^ 1, y, z, c))
-up, down = ring(1), ring(RING - 1)
+cross, cross_over = sender_pair(lambda x, y, z, c: (3 - x if c else x ^ 1, y, z, c))
+(up, up_over), (down, down_over) = ring(1), ring(RING - 1)
 
 
 def call(name, body, out_shape, operands, flops, scalars=(), after=(), scratch=()):
@@ -81,49 +84,26 @@
 
 
 def unit_halves(core, parameters, batch_total, picture, caption):
-    def body(core, warmth, score_offset, multiplier, picture_ref, caption_ref, *refs):
-        keep, give, constants, image, text, sems = refs
-        copies = []
-        for source, target in ((picture_ref, image), (caption_ref, text)):
-            for first in range(0, source.shape[0], COPY_ROWS):
-                here = pl.ds(first, COPY_ROWS)
-                copies.append(
-                    pltpu.make_async_copy(
-                        source.at[here, :], target.at[here, :], sems.at[len(copies)]
-                    )
-                )
-        for copy in copies:
-            copy.start()
+    def body(core, warmth, score_offset, multiplier, picture, caption, keep, give, constants):
         scale = jnp.exp(jnp.full((1, TILE), warmth[0], jnp.float32))
         constants[0:1, :] = 0.5 * scale
         constants[1:2, :] = jnp.full((1, TILE), 0.5 * score_offset[0], jnp.float32)
         constants[2:3, :] = 0.5 * (multiplier[0] / batch_total * scale)
-        for copy in copies:
-            copy.wait()
+
+        def fill(carried, handed):
+            keep[...] = unit_of(carried[...].astype(jnp.float32))[0].astype(jnp.bfloat16)
+            give[...] = unit_of(handed[...].astype(jnp.float32))[0].astype(jnp.bfloat16)
 
         @pl.when(core[0] == 0)
         def _():
-            give[...] = unit_of(image[...].astype(jnp.float32))[0].astype(jnp.bfloat16)
-            keep[...] = unit_of(text[...].astype(jnp.float32))[0].astype(jnp.bfloat16)
+            fill(caption, picture)
 
         @pl.when(core[0] != 0)
         def _():
-            give[...] = unit_of(text[...].astype(jnp.float32))[0].astype(jnp.bfloat16)
-            keep[...] = unit_of(image[...].astype(jnp.float32))[0].astype(jnp.bfloat16)
-
-    return pl.pallas_call(
-        body,
-        name="units",
-        out_shape=[array(*picture.shape)] * 2 + [jax.ShapeDtypeStruct((8, TILE), jnp.float32)],
-        in_specs=[pl.BlockSpec(memory_space=pltpu.SMEM)] * 4
-        + [pl.BlockSpec(memory_space=pltpu.HBM)] * 2,
-        scratch_shapes=[
-            pltpu.VMEM(picture.shape, jnp.bfloat16),
-            pltpu.VMEM(picture.shape, jnp.bfloat16),
-            pltpu.SemaphoreType.DMA((2 * picture.shape[0] // COPY_ROWS,)),
-        ],
-        compiler_params=pltpu.CompilerParams(vmem_limit_bytes=VMEM_BYTES),
-    )(core, *parameters, picture, caption)
+            fill(picture, caption)
+
+    shapes = [array(*picture.shape)] * 2 + [jax.ShapeDtypeStruct((8, TILE), jnp.float32)]
+    return call("units", body, shapes, [picture, caption], 6 * picture.size, [core, *parameters])
 
 
 def pack(*blocks):
@@ -217,41 +197,46 @@
     return call("add_half", body, [array(*whole.shape)], [whole, part], flops, after=after)[0]
 
 
-def through_norms(core, picture, caption, terms):
+def add_halves(halves, *terms):
+    rows = halves[0].shape[0]
+
+    def body(*refs):
+        for half in range(2):
+            parts = [refs[half][...]]
+            parts += [ref[pl.ds(half * rows, rows), :] for ref in refs[2:-2]]
+            refs[half - 2][...] = total_of(parts).astype(jnp.bfloat16)
+
+    return call("add_halves", body, [array(*halves[0].shape)] * 2, [*halves, *terms], 0)
+
+
+def through_norms(core, picture, caption, carried, handed):
     rows, feature = picture.shape
-
-    def give_body(*refs):
-        total = total_of([ref[pl.ds(rows, rows), :] for ref in refs[:-1]])
-        refs[-1][...] = total.astype(jnp.bfloat16)
-
-    got = to_core(call("give", give_body, [array(rows, feature)], terms, 4 * rows * feature)[0])
-
-    def body(core, picture, caption, got, *refs):
-        kept, (image_out, text_out) = refs[:-2], refs[-2:]
-
-        def finish(raw, direct, out):
+    count = len(carried)
+
+    def body(core, picture, caption, *refs):
+        carried, handed, (image_out, text_out) = refs[:count], refs[count:-2], refs[-2:]
+
+        def finish(raw, terms, out):
+            direct = total_of([ref[...] for ref in terms])
             unit, inverse = unit_of(raw[...].astype(jnp.float32))
             along = jnp.sum(unit * direct, axis=1, keepdims=True)
             out[...] = (inverse * (direct - unit * along)).astype(jnp.bfloat16)
 
-        def direct_kept():
-            return total_of([ref[pl.ds(0, rows), :] for ref in kept])
-
         @pl.when(core[0] == 0)
         def _():
-            finish(picture, got[...].astype(jnp.float32), image_out)
-            finish(caption, direct_kept(), text_out)
+            finish(picture, handed, image_out)
+            finish(caption, carried, text_out)
 
         @pl.when(core[0] != 0)
         def _():
-            finish(picture, direct_kept(), image_out)
-            finish(caption, got[...].astype(jnp.float32), text_out)
+            finish(picture, carried, image_out)
+            finish(caption, handed, text_out)
 
     return call(
         "final",
         body,
         [array(rows, feature)] * 2,
-        [picture, caption, got, *terms],
+        [picture, caption, *carried, *handed],
         20 * rows * feature,
         [core],
     )
@@ -294,18 +279,21 @@
     )
     far, partner_below = add_half(far, to_far, 0), add_half(partner_below, to_below, 1)
     to_above, to_partner, to_above_too = up(far), down(partner_below), cross(partner_above)
-    own, partner, above, below = sums(
+    near_parts = sums(
         "near_rest",
         constants,
         near,
         rest,
         near_held,
-        rows_out=2 * rows,
+        rows_out=rows,
         after=[far, partner_below],
     )
-    above, partner = add(above, to_above, to_above_too), add(partner, to_partner)
-    terms = [own, up(above), down(below), cross(partner)]
-    image_grad, text_grad = through_norms(core, picture_vectors, caption_vectors, terms)
+    own, partner, above, below = [near_parts[at : at + 2] for at in range(0, len(near_parts), 2)]
+    partner = add_halves(partner, to_partner)
+    above = add_halves(above, to_above, to_above_too)
+    carried = [own[0], down(below[0]), cross(partner[0]), up(above[0])]
+    handed = [to_core(own[1]), down_over(below[1]), cross_over(partner[1]), up_over(above[1])]
+    image_grad, text_grad = through_norms(core, picture_vectors, caption_vectors, carried, handed)
     return image_grad, text_grad
 
 

time: 82.7 us -> 83.6 us (1.011)
  starting transfers between devices: 31.2 us -> 33.9 us
  waiting for transfers between devices: 19.4 us -> 18.4 us
    ppermute x26 -> x29, starting transfers between devices: 31.2 us -> 33.9 us  [sender(): return lambda value: lax.ppermute(value, ('blk', 'grp'), pairs)]
    ppermute x26 -> x29, waiting for transfers between devices: 19.4 us -> 18.4 us  [sender(): return lambda value: lax.ppermute(value, ('blk', 'grp'), pairs)]
    pallas_call x1 -> x0, Pallas kernels: 1.03 us -> none  [unit_halves(): pl.pallas_call(body, name='units', out_shape=[array(*picture.shape)] * 2...]
  transfers between devices with their start and end apart: 26 -> 29, of which waited for: 10 -> 10; matrix products, arithmetic and copies ran while one was open for 0% -> 0% of each run, Pallas kernels for 29% -> 28%
where the time goes in v2:
time: 83.6 us; the launch traced here: 83.4 us
  starting transfers between devices  33.9 us (41%)
  Pallas kernels  26.3 us (31%)
  waiting for transfers between devices  18.4 us (22%)
  between operations  2.8 us (3%)
  local copies, waits for them, and re-layouts  2.03 us (2%)
    ppermute x29, starting transfers between devices, sender(): return lambda value: lax.ppermute(value, ('blk', 'grp'), pairs)  33.9 us
    pallas_call x13, Pallas kernels, call(): pl.pallas_call(lambda *refs: body(*refs[len(after):]), name=name, out_sha...  26.3 us
    ppermute x29, waiting for transfers between devices, sender(): return lambda value: lax.ppermute(value, ('blk', 'grp'), pairs)  18.4 us
    unnamed x9, local copies, waits for them, and re-layouts  1.95 us
  transfers between devices with their start and end apart: 29, of which 10 were waited for; matrix products, arithmetic and copies ran while one was open for 0% of the time, Pallas kernels for 28%

profile of v2, /device:TPU:1, one launch (start us, length us, event | category | flops | bytes accessed | tf_op | source)
XLA Modules:
  0.0 83.4 jit_solution(11063392256420444265)
XLA Ops:
  2.6 1.0 %copy-done = bf16[128,1152]{1,0:T(8,128)(2,1)S(1)} copy-done((bf16[128,1152]{1,0:T(8,128)(2,1)S(1)}, bf16[128,1152]{1,0:T(8,128)(2,1)}, u32[]{:S(2)}) %copy-start) | copy-done | bytes 294936
  3.5 1.0 %copy-done.2 = bf16[128,1152]{1,0:T(8,128)(2,1)S(1)} copy-done((bf16[128,1152]{1,0:T(8,128)(2,1)S(1)}, bf16[128,1152]{1,0:T(8,128)(2,1)}, u32[]{:S(2)}) %copy-start.2) | copy-done | bytes 294936
  4.5 0.2 units.1
  4.7 1.5 %collective-permute-start = (bf16[128,1152]{1,0:T(8,128)(2,1)S(1)}, bf16[128,1152]{1,0:T(8,128)(2,1)S(1)}, u32[]{:S(2)}, u32[]{:S(2)}) collective-permute-start(bf16[128,1152]{1,0:T(8,128)(2,1)S(1)} %get-tuple-element.31), channel_id=1, source_target_pairs={{0,8},{8,0},{2,10},{10,2},{4,12},{12,4},{6,14},{14,6},{16,24},{24,... | collective-permute-start | bytes 884744 | tf_op jit(solution)/shard_map/ppermute | solution.py:29
  6.2 1.2 %collective-permute-done = bf16[128,1152]{1,0:T(8,128)(2,1)S(1)} collective-permute-done((bf16[128,1152]{1,0:T(8,128)(2,1)S(1)}, bf16[128,1152]{1,0:T(8,128)(2,1)S(1)}, u32[]{:S(2)}, u32[]{:S(2)}) %collective-permute-start) | collective-permute-done | bytes 294944 | tf_op jit(solution)/shard_map/ppermute | solution.py:29
  7.5 1.8 %collective-permute-start.5 = (bf16[256,1152]{1,0:T(8,128)(2,1)S(1)}, bf16[256,1152]{1,0:T(8,128)(2,1)S(1)}, u32[]{:S(2)}, u32[]{:S(2)}) collective-permute-start(bf16[256,1152]{1,0:T(8,128)(2,1)S(1)} %constant_dynamic-update-slice_fusion.refs_1_.refs_3_), channel_id=1, source_target_pairs={{0,16},{8,10},{2,18},{10,12},{4,20},{12,14},{6,22},{14,8},{16,32},... | collective-permute-start | bytes 1769480 | tf_op jit(solution)/shard_map/ppermute | solution.py:29
  9.3 2.5 %collective-permute-start.3 = (bf16[256,1152]{1,0:T(8,128)(2,1)S(1)}, bf16[256,1152]{1,0:T(8,128)(2,1)S(1)}, u32[]{:S(2)}, u32[]{:S(2)}) collective-permute-start(bf16[256,1152]{1,0:T(8,128)(2,1)S(1)} %constant_dynamic-update-slice_fusion.refs_1_.refs_3_), channel_id=1, source_target_pairs={{0,64},{8,73},{2,66},{10,75},{4,68},{12,77},{6,70},{14,79},{16,80}... | collective-permute-start | bytes 1769480 | tf_op jit(solution)/shard_map/ppermute | solution.py:29
  11.7 2.2 %collective-permute-start.1 = (bf16[256,1152]{1,0:T(8,128)(2,1)S(1)}, bf16[256,1152]{1,0:T(8,128)(2,1)S(1)}, u32[]{:S(2)}, u32[]{:S(2)}) collective-permute-start(bf16[256,1152]{1,0:T(8,128)(2,1)S(1)} %constant_dynamic-update-slice_fusion.refs_1_.refs_3_), channel_id=1, source_target_pairs={{0,48},{8,14},{2,50},{10,8},{4,52},{12,10},{6,54},{14,12},{16,0},{... | collective-permute-start | bytes 1769480 | tf_op jit(solution)/shard_map/ppermute | solution.py:29
  14.0 4.7 %collective-permute-done.5.refs_4_.refs_6_ = bf16[256,1152]{1,0:T(8,128)(2,1)S(1)} collective-permute-done((bf16[256,1152]{1,0:T(8,128)(2,1)S(1)}, bf16[256,1152]{1,0:T(8,128)(2,1)S(1)}, u32[]{:S(2)}, u32[]{:S(2)}) %collective-permute-start.5) | collective-permute-done | bytes 589856 | tf_op jit(solution)/shard_map/ppermute | solution.py:29
  18.6 0.4 collective-permute-start.9
  19.0 0.2 collective-permute-done.3.refs_2_.refs_4_
  19.2 0.3 collective-permute-start.7
  19.5 1.3 %collective-permute-done.1.refs_3_.refs_5_ = bf16[256,1152]{1,0:T(8,128)(2,1)S(1)} collective-permute-done((bf16[256,1152]{1,0:T(8,128)(2,1)S(1)}, bf16[256,1152]{1,0:T(8,128)(2,1)S(1)}, u32[]{:S(2)}, u32[]{:S(2)}) %collective-permute-start.1) | collective-permute-done | bytes 589856 | tf_op jit(solution)/shard_map/ppermute | solution.py:29
  20.8 0.2 collective-permute-start.8
  20.9 1.6 %collective-permute-start.4 = (bf16[256,1152]{1,0:T(8,128)(2,1)S(1)}, bf16[256,1152]{1,0:T(8,128)(2,1)S(1)}, u32[]{:S(2)}, u32[]{:S(2)}) collective-permute-start(bf16[256,1152]{1,0:T(8,128)(2,1)S(1)} %collective-permute-done.3.refs_2_.refs_4_), channel_id=1, source_target_pairs={{0,16},{8,10},{2,18},{10,12},{4,20},{12,14},{6,22},{14,8},{16,32},... | collective-permute-start | bytes 1769480 | tf_op jit(solution)/shard_map/ppermute | solution.py:29
  22.6 2.1 %collective-permute-start.2 = (bf16[256,1152]{1,0:T(8,128)(2,1)S(1)}, bf16[256,1152]{1,0:T(8,128)(2,1)S(1)}, u32[]{:S(2)}, u32[]{:S(2)}) collective-permute-start(bf16[256,1152]{1,0:T(8,128)(2,1)S(1)} %collective-permute-done.1.refs_3_.refs_5_), channel_id=1, source_target_pairs={{0,48},{8,14},{2,50},{10,8},{4,52},{12,10},{6,54},{14,12},{16,0},{... | collective-permute-start | bytes 1769480 | tf_op jit(solution)/shard_map/ppermute | solution.py:29
  24.7 1.8 %collective-permute-start.12 = (bf16[256,1152]{1,0:T(8,128)(2,1)S(1)}, bf16[256,1152]{1,0:T(8,128)(2,1)S(1)}, u32[]{:S(2)}, u32[]{:S(2)}) collective-permute-start(bf16[256,1152]{1,0:T(8,128)(2,1)S(1)} %collective-permute-done.1.refs_3_.refs_5_), channel_id=1, source_target_pairs={{0,64},{8,73},{2,66},{10,75},{4,68},{12,77},{6,70},{14,79},{16,80}... | collective-permute-start | bytes 1769480 | tf_op jit(solution)/shard_map/ppermute | solution.py:29
  26.5 5.8 %near.1.refs_11_ = f32[1024,1152]{1,0:T(8,128)S(1)} custom-call(f32[8,256]{1,0:T(8,128)S(1)} %get-tuple-element.29.refs_0_.refs_1_.refs_2_, bf16[256,1152]{1,0:T(8,128)(2,1)S(1)} %constant_dynamic-update-slice_fusion.refs_1_.refs_3_, bf16[256,1152]{1,0:T(8,128)(2,1)S(1)} %collective-permute-done.3.refs_2_.refs_4_, ...), custom_call_target="tpu_custom_call" | custom-call | flops 75497472 | bytes 110656 | tf_op jit(solution)/shard_map/near/pallas_call | solution.py:49
  32.4 1.0 %collective-permute-start.11 = (bf16[128,1152]{1,0:T(8,128)(2,1)S(1)}, bf16[128,1152]{1,0:T(8,128)(2,1)S(1)}, u32[]{:S(2)}, u32[]{:S(2)}) collective-permute-start(bf16[128,1152]{1,0:T(8,128)(2,1)S(1)} %slice.7), channel_id=1, source_target_pairs={{0,16},{8,10},{2,18},{10,12},{4,20},{12,14},{6,22},{14,8},{16,32},... | collective-permute-start | bytes 884744 | tf_op jit(solution)/shard_map/ppermute | solution.py:29
  33.4 1.8 %collective-permute-start.10 = (bf16[128,1152]{1,0:T(8,128)(2,1)S(1)}, bf16[128,1152]{1,0:T(8,128)(2,1)S(1)}, u32[]{:S(2)}, u32[]{:S(2)}) collective-permute-start(bf16[128,1152]{1,0:T(8,128)(2,1)S(1)} %slice.6), channel_id=1, source_target_pairs={{0,64},{8,73},{2,66},{10,75},{4,68},{12,77},{6,70},{14,79},{16,80}... | collective-permute-start | bytes 884744 | tf_op jit(solution)/shard_map/ppermute | solution.py:29
  35.2 0.5 collective-permute-start.15
  35.7 4.4 %middle.1.refs_9_ = f32[768,1152]{1,0:T(8,128)S(1)} custom-call(f32[8,256]{1,0:T(8,128)S(1)} %get-tuple-element.29.refs_0_.refs_1_.refs_2_, bf16[256,1152]{1,0:T(8,128)(2,1)S(1)} %collective-permute-done.12.refs_1_.refs_2_, bf16[256,1152]{1,0:T(8,128)(2,1)S(1)} %collective-permute-done.4.refs_2_.refs_3_, ...), custom_call_target="tpu_custom_call" | custom-call | flops 56623104 | bytes 92224 | tf_op jit(solution)/shard_map/middle/pallas_call | solution.py:49
  40.1 0.3 collective-permute-done.10.refs_0_
  40.5 0.8 %collective-permute-start.13 = (bf16[256,1152]{1,0:T(8,128)(2,1)S(1)}, bf16[256,1152]{1,0:T(8,128)(2,1)S(1)}, u32[]{:S(2)}, u32[]{:S(2)}) collective-permute-start(bf16[256,1152]{1,0:T(8,128)(2,1)S(1)} %pack.1.refs_1_), channel_id=1, source_target_pairs={{0,8},{8,0},{2,10},{10,2},{4,12},{12,4},{6,14},{14,6},{16,24},{24,... | collective-permute-start | bytes 1769480 | tf_op jit(solution)/shard_map/ppermute | solution.py:29
  41.3 2.6 %last.1.refs_3_ = f32[256,1152]{1,0:T(8,128)S(1)} custom-call(f32[8,256]{1,0:T(8,128)S(1)} %get-tuple-element.29.refs_0_.refs_1_.refs_2_, bf16[256,1152]{1,0:T(8,128)(2,1)S(1)} %pack.1.refs_1_, bf16[256,1152]{1,0:T(8,128)(2,1)S(1)} %collective-permute-done.6.refs_5_.refs_4_.refs_2_, bf16[256,1152]{1,0:T(8,128)(2,1)S(1)} %collective-permute-done.7.refs_6_.refs_5_.refs_3_, ...), custom_call_target="tpu_custom_call" | custom-call | flops 33030144 | bytes 83008 | tf_op jit(solution)/shard_map/last/pallas_call | solution.py:49
  44.0 0.9 %last_rest.1 = (bf16[128,1152]{1,0:T(8,128)(2,1)S(1)}, bf16[128,1152]{1,0:T(8,128)(2,1)S(1)}) custom-call(f32[8,256]{1,0:T(8,128)S(1)} %get-tuple-element.29.refs_0_.refs_1_.refs_2_, bf16[256,1152]{1,0:T(8,128)(2,1)S(1)} %pack.1.refs_1_, bf16[256,1152]{1,0:T(8,128)(2,1)S(1)} %collective-permute-done.13.refs_2_.refs_8_.refs_10_, f32[256,1152]{1,0:T(8,128)S(1)} %last.1.refs_3_), custom_call_target="tpu_custom_call" | custom-call | flops 4718592 | bytes 36928 | tf_op jit(solution)/shard_map/last_rest/pallas_call | solution.py:49
  44.9 3.2 %collective-permute-start.18 = (bf16[128,1152]{1,0:T(8,128)(2,1)S(1)}, bf16[128,1152]{1,0:T(8,128)(2,1)S(1)}, u32[]{:S(2)}, u32[]{:S(2)}) collective-permute-start(bf16[128,1152]{1,0:T(8,128)(2,1)S(1)} %get-tuple-element.41), channel_id=1, source_target_pairs={{0,48},{8,14},{2,50},{10,8},{4,52},{12,10},{6,54},{14,12},{16,0},{... | collective-permute-start | bytes 884744 | tf_op jit(solution)/shard_map/ppermute | solution.py:29
  48.1 1.8 %collective-permute-start.17 = (bf16[128,1152]{1,0:T(8,128)(2,1)S(1)}, bf16[128,1152]{1,0:T(8,128)(2,1)S(1)}, u32[]{:S(2)}, u32[]{:S(2)}) collective-permute-start(bf16[128,1152]{1,0:T(8,128)(2,1)S(1)} %get-tuple-element.37.refs_0_), channel_id=1, source_target_pairs={{0,64},{8,73},{2,66},{10,75},{4,68},{12,77},{6,70},{14,79},{16,80}... | collective-permute-start | bytes 884744 | tf_op jit(solution)/shard_map/ppermute | solution.py:29
  49.9 4.4 %middle_rest.1 = (bf16[256,1152]{1,0:T(8,128)(2,1)S(1)}, bf16[256,1152]{1,0:T(8,128)(2,1)S(1)}, bf16[256,1152]{1,0:T(8,128)(2,1)S(1)}) custom-call(bf16[128,1152]{1,0:T(8,128)(2,1)S(1)} %get-tuple-element.37.refs_0_, f32[8,256]{1,0:T(8,128)S(1)} %get-tuple-element.29.refs_0_.refs_1_.refs_2_, bf16[256,1152]{1,0:T(8,128)(2,1)S(1)} %collective-permute-done.12.refs_1_.refs_2_, ...), custom_call_target="tpu_custom_call" | custom-call | flops 56623104 | bytes 119872 | tf_op jit(solution)/shard_map/middle_rest/pallas_call | solution.py:49
  54.4 0.1 add_half.3.refs_1_
  54.5 0.6 collective-permute-start.20
  55.0 1.8 %collective-permute-start.23 = (bf16[256,1152]{1,0:T(8,128)(2,1)S(1)}, bf16[256,1152]{1,0:T(8,128)(2,1)S(1)}, u32[]{:S(2)}, u32[]{:S(2)}) collective-permute-start(bf16[256,1152]{1,0:T(8,128)(2,1)S(1)} %get-tuple-element.50), channel_id=1, source_target_pairs={{0,64},{8,73},{2,66},{10,75},{4,68},{12,77},{6,70},{14,79},{16,80}... | collective-permute-start | bytes 1769480 | tf_op jit(solution)/shard_map/ppermute | solution.py:29
  56.9 0.1 add_half.2.refs_0_
  57.0 0.3 collective-permute-start.22
  57.3 5.8 %near_rest.1 = (bf16[128,1152]{1,0:T(8,128)(2,1)S(1)}, bf16[128,1152]{1,0:T(8,128)(2,1)S(1)}, bf16[128,1152]{1,0:T(8,128)(2,1)S(1)}, bf16[128,1152]{1,0:T(8,128)...) custom-call(bf16[256,1152]{1,0:T(8,128)(2,1)S(1)} %add_half.2.refs_0, ...), custom_call_target="tpu_custom_call" | custom-call | flops 75497472 | bytes 147520 | tf_op jit(solution)/shard_map/near_rest/pallas_call | solution.py:49
  63.1 2.7 %collective-permute-start.19 = (bf16[128,1152]{1,0:T(8,128)(2,1)S(1)}, bf16[128,1152]{1,0:T(8,128)(2,1)S(1)}, u32[]{:S(2)}, u32[]{:S(2)}) collective-permute-start(bf16[128,1152]{1,0:T(8,128)(2,1)S(1)} %get-tuple-element.44), channel_id=1, source_target_pairs={{0,48},{8,14},{2,50},{10,8},{4,52},{12,10},{6,54},{14,12},{16,0},{... | collective-permute-start | bytes 884744 | tf_op jit(solution)/shard_map/ppermute | solution.py:29
  65.8 2.5 %collective-permute-start.26 = (bf16[128,1152]{1,0:T(8,128)(2,1)S(1)}, bf16[128,1152]{1,0:T(8,128)(2,1)S(1)}, u32[]{:S(2)}, u32[]{:S(2)}) collective-permute-start(bf16[128,1152]{1,0:T(8,128)(2,1)S(1)} %get-tuple-element.53), channel_id=1, source_target_pairs={{0,56},{8,6},{2,58},{10,0},{4,60},{12,2},{6,62},{14,4},{16,8},{24,... | collective-permute-start | bytes 884744 | tf_op jit(solution)/shard_map/ppermute | solution.py:29
  68.3 0.1 add_halves.2
  68.5 2.4 %collective-permute-start.21 = (bf16[128,1152]{1,0:T(8,128)(2,1)S(1)}, bf16[128,1152]{1,0:T(8,128)(2,1)S(1)}, u32[]{:S(2)}, u32[]{:S(2)}) collective-permute-start(bf16[128,1152]{1,0:T(8,128)(2,1)S(1)} %get-tuple-element.47), channel_id=1, source_target_pairs={{0,64},{8,73},{2,66},{10,75},{4,68},{12,77},{6,70},{14,79},{16,80}... | collective-permute-start | bytes 884744 | tf_op jit(solution)/shard_map/ppermute | solution.py:29
  70.9 0.2 add_halves.3
  71.1 0.1 collective-permute-start.24
  71.2 0.1 collective-permute-start.28
  71.3 1.4 %collective-permute-done.26.refs_8_ = bf16[128,1152]{1,0:T(8,128)(2,1)S(1)} collective-permute-done((bf16[128,1152]{1,0:T(8,128)(2,1)S(1)}, bf16[128,1152]{1,0:T(8,128)(2,1)S(1)}, u32[]{:S(2)}, u32[]{:S(2)}) %collective-permute-start.26) | collective-permute-done | bytes 294944 | tf_op jit(solution)/shard_map/ppermute | solution.py:29
  72.7 2.7 %collective-permute-done.21.refs_5_ = bf16[128,1152]{1,0:T(8,128)(2,1)S(1)} collective-permute-done((bf16[128,1152]{1,0:T(8,128)(2,1)S(1)}, bf16[128,1152]{1,0:T(8,128)(2,1)S(1)}, u32[]{:S(2)}, u32[]{:S(2)}) %collective-permute-start.21) | collective-permute-done | bytes 294944 | tf_op jit(solution)/shard_map/ppermute | solution.py:29
  75.4 2.6 %collective-permute-done.27.refs_9_ = bf16[128,1152]{1,0:T(8,128)(2,1)S(1)} collective-permute-done((bf16[128,1152]{1,0:T(8,128)(2,1)S(1)}, bf16[128,1152]{1,0:T(8,128)(2,1)S(1)}, u32[]{:S(2)}, u32[]{:S(2)}) %collective-permute-start.27) | collective-permute-done | bytes 294944 | tf_op jit(solution)/shard_map/ppermute | solution.py:29
  77.9 0.3 collective-permute-done.24.refs_6_
  78.2 3.7 %collective-permute-done.28.refs_10_ = bf16[128,1152]{1,0:T(8,128)(2,1)S(1)} collective-permute-done((bf16[128,1152]{1,0:T(8,128)(2,1)S(1)}, bf16[128,1152]{1,0:T(8,128)(2,1)S(1)}, u32[]{:S(2)}, u32[]{:S(2)}) %collective-permute-start.28) | collective-permute-done | bytes 294944 | tf_op jit(solution)/shard_map/ppermute | solution.py:29
  81.9 1.5 %final.1 = (bf16[128,1152]{1,0:T(8,128)(2,1)}, bf16[128,1152]{1,0:T(8,128)(2,1)}) custom-call(s32[1]{0:T(128)} %bitcast.refs_0_, bf16[128,1152]{1,0:T(8,128)(2,1)S(1)} %copy-done.1, bf16[128,1152]{1,0:T(8,128)(2,1)S(1)} %copy-done.3, bf16[128,1152]{1,0:T(8,128)(2,1)S(1)} %get-tuple-element.43.refs_3_, bf16[128,1152]{1,0:T(8,128)(2,1)S(1)} %collective-permute-done.19.refs_4_, ...), custom_call_target="tpu_custom_call" | custom-call | flops 46080 | bytes 55296 | tf_op jit(solution)/shard_map/final/pallas_call | solution.py:49
  (35 shorter events, 0.2 us)
Async XLA Ops:
  2.6 1.0 %copy-start = (bf16[128,1152]{1,0:T(8,128)(2,1)S(1)}, bf16[128,1152]{1,0:T(8,128)(2,1)}, u32[]{:S(2)}) copy-start(bf16[128,1152]{1,0:T(8,128)(2,1)} %refs_1_.1) | copy-start | bytes 884740
  3.5 1.0 %copy-start.2 = (bf16[128,1152]{1,0:T(8,128)(2,1)S(1)}, bf16[128,1152]{1,0:T(8,128)(2,1)}, u32[]{:S(2)}) copy-start(bf16[128,1152]{1,0:T(8,128)(2,1)} %refs_2_.1) | copy-start | bytes 884740
  4.7 2.7 %collective-permute-start = (bf16[128,1152]{1,0:T(8,128)(2,1)S(1)}, bf16[128,1152]{1,0:T(8,128)(2,1)S(1)}, u32[]{:S(2)}, u32[]{:S(2)}) collective-permute-start(bf16[128,1152]{1,0:T(8,128)(2,1)S(1)} %get-tuple-element.31), channel_id=1, source_target_pairs={{0,8},{8,0},{2,10},{10,2},{4,12},{12,4},{6,14},{14,6},{16,24},{24,... | collective-permute-start | bytes 884744 | tf_op jit(solution)/shard_map/ppermute | solution.py:29
  7.5 11.2 %collective-permute-start.5 = (bf16[256,1152]{1,0:T(8,128)(2,1)S(1)}, bf16[256,1152]{1,0:T(8,128)(2,1)S(1)}, u32[]{:S(2)}, u32[]{:S(2)}) collective-permute-start(bf16[256,1152]{1,0:T(8,128)(2,1)S(1)} %constant_dynamic-update-slice_fusion.refs_1_.refs_3_), channel_id=1, source_target_pairs={{0,16},{8,10},{2,18},{10,12},{4,20},{12,14},{6,22},{14,8},{16,32},... | collective-permute-start | bytes 1769480 | tf_op jit(solution)/shard_map/ppermute | solution.py:29
  9.3 9.9 %collective-permute-start.3 = (bf16[256,1152]{1,0:T(8,128)(2,1)S(1)}, bf16[256,1152]{1,0:T(8,128)(2,1)S(1)}, u32[]{:S(2)}, u32[]{:S(2)}) collective-permute-start(bf16[256,1152]{1,0:T(8,128)(2,1)S(1)} %constant_dynamic-update-slice_fusion.refs_1_.refs_3_), channel_id=1, source_target_pairs={{0,64},{8,73},{2,66},{10,75},{4,68},{12,77},{6,70},{14,79},{16,80}... | collective-permute-start | bytes 1769480 | tf_op jit(solution)/shard_map/ppermute | solution.py:29
  11.7 9.0 %collective-permute-start.1 = (bf16[256,1152]{1,0:T(8,128)(2,1)S(1)}, bf16[256,1152]{1,0:T(8,128)(2,1)S(1)}, u32[]{:S(2)}, u32[]{:S(2)}) collective-permute-start(bf16[256,1152]{1,0:T(8,128)(2,1)S(1)} %constant_dynamic-update-slice_fusion.refs_1_.refs_3_), channel_id=1, source_target_pairs={{0,48},{8,14},{2,50},{10,8},{4,52},{12,10},{6,54},{14,12},{16,0},{... | collective-permute-start | bytes 1769480 | tf_op jit(solution)/shard_map/ppermute | solution.py:29
  13.9 8.6 %collective-permute-start.6 = (bf16[256,1152]{1,0:T(8,128)(2,1)S(1)}, bf16[256,1152]{1,0:T(8,128)(2,1)S(1)}, u32[]{:S(2)}, u32[]{:S(2)}) collective-permute-start(bf16[256,1152]{1,0:T(8,128)(2,1)S(1)} %constant_dynamic-update-slice_fusion.refs_1_.refs_3_), channel_id=1, source_target_pairs={{0,8},{8,0},{2,10},{10,2},{4,12},{12,4},{6,14},{14,6},{16,24},{24,... | collective-permute-start | bytes 1769480 | tf_op jit(solution)/shard_map/ppermute | solution.py:29
  18.6 6.1 %collective-permute-start.9 = (bf16[256,1152]{1,0:T(8,128)(2,1)S(1)}, bf16[256,1152]{1,0:T(8,128)(2,1)S(1)}, u32[]{:S(2)}, u32[]{:S(2)}) collective-permute-start(bf16[256,1152]{1,0:T(8,128)(2,1)S(1)} %collective-permute-done.5.refs_4_.refs_6_), channel_id=1, source_target_pairs={{0,8},{8,0},{2,10},{10,2},{4,12},{12,4},{6,14},{14,6},{16,24},{24,... | collective-permute-start | bytes 1769480 | tf_op jit(solution)/shard_map/ppermute | solution.py:29
  19.2 7.3 %collective-permute-start.7 = (bf16[256,1152]{1,0:T(8,128)(2,1)S(1)}, bf16[256,1152]{1,0:T(8,128)(2,1)S(1)}, u32[]{:S(2)}, u32[]{:S(2)}) collective-permute-start(bf16[256,1152]{1,0:T(8,128)(2,1)S(1)} %collective-permute-done.3.refs_2_.refs_4_), channel_id=1, source_target_pairs={{0,8},{8,0},{2,10},{10,2},{4,12},{12,4},{6,14},{14,6},{16,24},{24,... | collective-permute-start | bytes 1769480 | tf_op jit(solution)/shard_map/ppermute | solution.py:29
  20.8 5.8 %collective-permute-start.8 = (bf16[256,1152]{1,0:T(8,128)(2,1)S(1)}, bf16[256,1152]{1,0:T(8,128)(2,1)S(1)}, u32[]{:S(2)}, u32[]{:S(2)}) collective-permute-start(bf16[256,1152]{1,0:T(8,128)(2,1)S(1)} %collective-permute-done.1.refs_3_.refs_5_), channel_id=1, source_target_pairs={{0,8},{8,0},{2,10},{10,2},{4,12},{12,4},{6,14},{14,6},{16,24},{24,... | collective-permute-start | bytes 1769480 | tf_op jit(solution)/shard_map/ppermute | solution.py:29
  20.9 11.4 %collective-permute-start.4 = (bf16[256,1152]{1,0:T(8,128)(2,1)S(1)}, bf16[256,1152]{1,0:T(8,128)(2,1)S(1)}, u32[]{:S(2)}, u32[]{:S(2)}) collective-permute-start(bf16[256,1152]{1,0:T(8,128)(2,1)S(1)} %collective-permute-done.3.refs_2_.refs_4_), channel_id=1, source_target_pairs={{0,16},{8,10},{2,18},{10,12},{4,20},{12,14},{6,22},{14,8},{16,32},... | collective-permute-start | bytes 1769480 | tf_op jit(solution)/shard_map/ppermute | solution.py:29
  22.6 9.7 %collective-permute-start.2 = (bf16[256,1152]{1,0:T(8,128)(2,1)S(1)}, bf16[256,1152]{1,0:T(8,128)(2,1)S(1)}, u32[]{:S(2)}, u32[]{:S(2)}) collective-permute-start(bf16[256,1152]{1,0:T(8,128)(2,1)S(1)} %collective-permute-done.1.refs_3_.refs_5_), channel_id=1, source_target_pairs={{0,48},{8,14},{2,50},{10,8},{4,52},{12,10},{6,54},{14,12},{16,0},{... | collective-permute-start | bytes 1769480 | tf_op jit(solution)/shard_map/ppermute | solution.py:29
  24.7 11.0 %collective-permute-start.12 = (bf16[256,1152]{1,0:T(8,128)(2,1)S(1)}, bf16[256,1152]{1,0:T(8,128)(2,1)S(1)}, u32[]{:S(2)}, u32[]{:S(2)}) collective-permute-start(bf16[256,1152]{1,0:T(8,128)(2,1)S(1)} %collective-permute-done.1.refs_3_.refs_5_), channel_id=1, source_target_pairs={{0,64},{8,73},{2,66},{10,75},{4,68},{12,77},{6,70},{14,79},{16,80}... | collective-permute-start | bytes 1769480 | tf_op jit(solution)/shard_map/ppermute | solution.py:29
  32.4 7.7 %collective-permute-start.11 = (bf16[128,1152]{1,0:T(8,128)(2,1)S(1)}, bf16[128,1152]{1,0:T(8,128)(2,1)S(1)}, u32[]{:S(2)}, u32[]{:S(2)}) collective-permute-start(bf16[128,1152]{1,0:T(8,128)(2,1)S(1)} %slice.7), channel_id=1, source_target_pairs={{0,16},{8,10},{2,18},{10,12},{4,20},{12,14},{6,22},{14,8},{16,32},... | collective-permute-start | bytes 884744 | tf_op jit(solution)/shard_map/ppermute | solution.py:29
  33.4 7.0 %collective-permute-start.10 = (bf16[128,1152]{1,0:T(8,128)(2,1)S(1)}, bf16[128,1152]{1,0:T(8,128)(2,1)S(1)}, u32[]{:S(2)}, u32[]{:S(2)}) collective-permute-start(bf16[128,1152]{1,0:T(8,128)(2,1)S(1)} %slice.6), channel_id=1, source_target_pairs={{0,64},{8,73},{2,66},{10,75},{4,68},{12,77},{6,70},{14,79},{16,80}... | collective-permute-start | bytes 884744 | tf_op jit(solution)/shard_map/ppermute | solution.py:29
  35.2 6.1 %collective-permute-start.16 = (bf16[256,1152]{1,0:T(8,128)(2,1)S(1)}, bf16[256,1152]{1,0:T(8,128)(2,1)S(1)}, u32[]{:S(2)}, u32[]{:S(2)}) collective-permute-start(bf16[256,1152]{1,0:T(8,128)(2,1)S(1)} %collective-permute-done.2.refs_3_.refs_4_), channel_id=1, source_target_pairs={{0,8},{8,0},{2,10},{10,2},{4,12},{12,4},{6,14},{14,6},{16,24},{24,... | collective-permute-start | bytes 1769480 | tf_op jit(solution)/shard_map/ppermute | solution.py:29
  35.2 6.1 %collective-permute-start.15 = (bf16[256,1152]{1,0:T(8,128)(2,1)S(1)}, bf16[256,1152]{1,0:T(8,128)(2,1)S(1)}, u32[]{:S(2)}, u32[]{:S(2)}) collective-permute-start(bf16[256,1152]{1,0:T(8,128)(2,1)S(1)} %collective-permute-done.4.refs_2_.refs_3_), channel_id=1, source_target_pairs={{0,8},{8,0},{2,10},{10,2},{4,12},{12,4},{6,14},{14,6},{16,24},{24,... | collective-permute-start | bytes 1769480 | tf_op jit(solution)/shard_map/ppermute | solution.py:29
  35.7 5.6 %collective-permute-start.14 = (bf16[256,1152]{1,0:T(8,128)(2,1)S(1)}, bf16[256,1152]{1,0:T(8,128)(2,1)S(1)}, u32[]{:S(2)}, u32[]{:S(2)}) collective-permute-start(bf16[256,1152]{1,0:T(8,128)(2,1)S(1)} %collective-permute-done.12.refs_1_.refs_2_), channel_id=1, source_target_pairs={{0,8},{8,0},{2,10},{10,2},{4,12},{12,4},{6,14},{14,6},{16,24},{24,... | collective-permute-start | bytes 1769480 | tf_op jit(solution)/shard_map/ppermute | solution.py:29
  40.5 3.5 %collective-permute-start.13 = (bf16[256,1152]{1,0:T(8,128)(2,1)S(1)}, bf16[256,1152]{1,0:T(8,128)(2,1)S(1)}, u32[]{:S(2)}, u32[]{:S(2)}) collective-permute-start(bf16[256,1152]{1,0:T(8,128)(2,1)S(1)} %pack.1.refs_1_), channel_id=1, source_target_pairs={{0,8},{8,0},{2,10},{10,2},{4,12},{12,4},{6,14},{14,6},{16,24},{24,... | collective-permute-start | bytes 1769480 | tf_op jit(solution)/shard_map/ppermute | solution.py:29
  44.9 9.5 %collective-permute-start.18 = (bf16[128,1152]{1,0:T(8,128)(2,1)S(1)}, bf16[128,1152]{1,0:T(8,128)(2,1)S(1)}, u32[]{:S(2)}, u32[]{:S(2)}) collective-permute-start(bf16[128,1152]{1,0:T(8,128)(2,1)S(1)} %get-tuple-element.41), channel_id=1, source_target_pairs={{0,48},{8,14},{2,50},{10,8},{4,52},{12,10},{6,54},{14,12},{16,0},{... | collective-permute-start | bytes 884744 | tf_op jit(solution)/shard_map/ppermute | solution.py:29
  48.1 8.8 %collective-permute-start.17 = (bf16[128,1152]{1,0:T(8,128)(2,1)S(1)}, bf16[128,1152]{1,0:T(8,128)(2,1)S(1)}, u32[]{:S(2)}, u32[]{:S(2)}) collective-permute-start(bf16[128,1152]{1,0:T(8,128)(2,1)S(1)} %get-tuple-element.37.refs_0_), channel_id=1, source_target_pairs={{0,64},{8,73},{2,66},{10,75},{4,68},{12,77},{6,70},{14,79},{16,80}... | collective-permute-start | bytes 884744 | tf_op jit(solution)/shard_map/ppermute | solution.py:29
  54.5 11.4 %collective-permute-start.20 = (bf16[256,1152]{1,0:T(8,128)(2,1)S(1)}, bf16[256,1152]{1,0:T(8,128)(2,1)S(1)}, u32[]{:S(2)}, u32[]{:S(2)}) collective-permute-start(bf16[256,1152]{1,0:T(8,128)(2,1)S(1)} %add_half.3.refs_1_), channel_id=1, source_target_pairs={{0,48},{8,14},{2,50},{10,8},{4,52},{12,10},{6,54},{14,12},{16,0},{... | collective-permute-start | bytes 1769480 | tf_op jit(solution)/shard_map/ppermute | solution.py:29
  55.0 13.5 %collective-permute-start.23 = (bf16[256,1152]{1,0:T(8,128)(2,1)S(1)}, bf16[256,1152]{1,0:T(8,128)(2,1)S(1)}, u32[]{:S(2)}, u32[]{:S(2)}) collective-permute-start(bf16[256,1152]{1,0:T(8,128)(2,1)S(1)} %get-tuple-element.50), channel_id=1, source_target_pairs={{0,64},{8,73},{2,66},{10,75},{4,68},{12,77},{6,70},{14,79},{16,80}... | collective-permute-start | bytes 1769480 | tf_op jit(solution)/shard_map/ppermute | solution.py:29
  57.0 24.9 %copy-start.1 = (bf16[128,1152]{1,0:T(8,128)(2,1)S(1)}, bf16[128,1152]{1,0:T(8,128)(2,1)}, u32[]{:S(2)}) copy-start(bf16[128,1152]{1,0:T(8,128)(2,1)} %refs_1_.1) | copy-start | bytes 884740
  57.0 24.9 %copy-start.3 = (bf16[128,1152]{1,0:T(8,128)(2,1)S(1)}, bf16[128,1152]{1,0:T(8,128)(2,1)}, u32[]{:S(2)}) copy-start(bf16[128,1152]{1,0:T(8,128)(2,1)} %refs_2_.1) | copy-start | bytes 884740
  57.0 13.9 %collective-permute-start.22 = (bf16[256,1152]{1,0:T(8,128)(2,1)S(1)}, bf16[256,1152]{1,0:T(8,128)(2,1)S(1)}, u32[]{:S(2)}, u32[]{:S(2)}) collective-permute-start(bf16[256,1152]{1,0:T(8,128)(2,1)S(1)} %add_half.2.refs_0_), channel_id=1, source_target_pairs={{0,16},{8,10},{2,18},{10,12},{4,20},{12,14},{6,22},{14,8},{16,32},... | collective-permute-start | bytes 1769480 | tf_op jit(solution)/shard_map/ppermute | solution.py:29
  63.1 8.0 %collective-permute-start.19 = (bf16[128,1152]{1,0:T(8,128)(2,1)S(1)}, bf16[128,1152]{1,0:T(8,128)(2,1)S(1)}, u32[]{:S(2)}, u32[]{:S(2)}) collective-permute-start(bf16[128,1152]{1,0:T(8,128)(2,1)S(1)} %get-tuple-element.44), channel_id=1, source_target_pairs={{0,48},{8,14},{2,50},{10,8},{4,52},{12,10},{6,54},{14,12},{16,0},{... | collective-permute-start | bytes 884744 | tf_op jit(solution)/shard_map/ppermute | solution.py:29
  65.8 5.3 %collective-permute-start.25 = (bf16[128,1152]{1,0:T(8,128)(2,1)S(1)}, bf16[128,1152]{1,0:T(8,128)(2,1)S(1)}, u32[]{:S(2)}, u32[]{:S(2)}) collective-permute-start(bf16[128,1152]{1,0:T(8,128)(2,1)S(1)} %get-tuple-element.52), channel_id=1, source_target_pairs={{0,8},{8,0},{2,10},{10,2},{4,12},{12,4},{6,14},{14,6},{16,24},{24,... | collective-permute-start | bytes 884744 | tf_op jit(solution)/shard_map/ppermute | solution.py:29
  65.8 6.8 %collective-permute-start.26 = (bf16[128,1152]{1,0:T(8,128)(2,1)S(1)}, bf16[128,1152]{1,0:T(8,128)(2,1)S(1)}, u32[]{:S(2)}, u32[]{:S(2)}) collective-permute-start(bf16[128,1152]{1,0:T(8,128)(2,1)S(1)} %get-tuple-element.53), channel_id=1, source_target_pairs={{0,56},{8,6},{2,58},{10,0},{4,60},{12,2},{6,62},{14,4},{16,8},{24,... | collective-permute-start | bytes 884744 | tf_op jit(solution)/shard_map/ppermute | solution.py:29
  68.5 6.9 %collective-permute-start.21 = (bf16[128,1152]{1,0:T(8,128)(2,1)S(1)}, bf16[128,1152]{1,0:T(8,128)(2,1)S(1)}, u32[]{:S(2)}, u32[]{:S(2)}) collective-permute-start(bf16[128,1152]{1,0:T(8,128)(2,1)S(1)} %get-tuple-element.47), channel_id=1, source_target_pairs={{0,64},{8,73},{2,66},{10,75},{4,68},{12,77},{6,70},{14,79},{16,80}... | collective-permute-start | bytes 884744 | tf_op jit(solution)/shard_map/ppermute | solution.py:29
  70.9 7.1 %collective-permute-start.27 = (bf16[128,1152]{1,0:T(8,128)(2,1)S(1)}, bf16[128,1152]{1,0:T(8,128)(2,1)S(1)}, u32[]{:S(2)}, u32[]{:S(2)}) collective-permute-start(bf16[128,1152]{1,0:T(8,128)(2,1)S(1)} %get-tuple-element.54), channel_id=1, source_target_pairs={{0,72},{8,65},{2,74},{10,67},{4,76},{12,69},{6,78},{14,71},{16,88}... | collective-permute-start | bytes 884744 | tf_op jit(solution)/shard_map/ppermute | solution.py:29
  71.1 7.1 %collective-permute-start.24 = (bf16[128,1152]{1,0:T(8,128)(2,1)S(1)}, bf16[128,1152]{1,0:T(8,128)(2,1)S(1)}, u32[]{:S(2)}, u32[]{:S(2)}) collective-permute-start(bf16[128,1152]{1,0:T(8,128)(2,1)S(1)} %get-tuple-element.51), channel_id=1, source_target_pairs={{0,16},{8,10},{2,18},{10,12},{4,20},{12,14},{6,22},{14,8},{16,32},... | collective-permute-start | bytes 884744 | tf_op jit(solution)/shard_map/ppermute | solution.py:29
  71.2 10.7 %collective-permute-start.28 = (bf16[128,1152]{1,0:T(8,128)(2,1)S(1)}, bf16[128,1152]{1,0:T(8,128)(2,1)S(1)}, u32[]{:S(2)}, u32[]{:S(2)}) collective-permute-start(bf16[128,1152]{1,0:T(8,128)(2,1)S(1)} %get-tuple-element.55), channel_id=1, source_target_pairs={{0,24},{8,2},{2,26},{10,4},{4,28},{12,6},{6,30},{14,0},{16,40},{24... | collective-permute-start | bytes 884744 | tf_op jit(solution)/shard_map/ppermute | solution.py:29

commit v3 on v1

--- a/solution.py
+++ b/solution.py
@@ -10,7 +10,6 @@
 RING = 4
 CORES = 2
 TILE = 256
-COPY_ROWS = 32
 VMEM_BYTES = 24 * 1024 * 1024
 
 
@@ -81,49 +80,26 @@
 
 
 def unit_halves(core, parameters, batch_total, picture, caption):
-    def body(core, warmth, score_offset, multiplier, picture_ref, caption_ref, *refs):
-        keep, give, constants, image, text, sems = refs
-        copies = []
-        for source, target in ((picture_ref, image), (caption_ref, text)):
-            for first in range(0, source.shape[0], COPY_ROWS):
-                here = pl.ds(first, COPY_ROWS)
-                copies.append(
-                    pltpu.make_async_copy(
-                        source.at[here, :], target.at[here, :], sems.at[len(copies)]
-                    )
-                )
-        for copy in copies:
-            copy.start()
+    def body(core, warmth, score_offset, multiplier, picture, caption, keep, give, constants):
         scale = jnp.exp(jnp.full((1, TILE), warmth[0], jnp.float32))
         constants[0:1, :] = 0.5 * scale
         constants[1:2, :] = jnp.full((1, TILE), 0.5 * score_offset[0], jnp.float32)
         constants[2:3, :] = 0.5 * (multiplier[0] / batch_total * scale)
-        for copy in copies:
-            copy.wait()
+
+        def fill(carried, handed):
+            keep[...] = unit_of(carried[...].astype(jnp.float32))[0].astype(jnp.bfloat16)
+            give[...] = unit_of(handed[...].astype(jnp.float32))[0].astype(jnp.bfloat16)
 
         @pl.when(core[0] == 0)
         def _():
-            give[...] = unit_of(image[...].astype(jnp.float32))[0].astype(jnp.bfloat16)
-            keep[...] = unit_of(text[...].astype(jnp.float32))[0].astype(jnp.bfloat16)
+            fill(caption, picture)
 
         @pl.when(core[0] != 0)
         def _():
-            give[...] = unit_of(text[...].astype(jnp.float32))[0].astype(jnp.bfloat16)
-            keep[...] = unit_of(image[...].astype(jnp.float32))[0].astype(jnp.bfloat16)
-
-    return pl.pallas_call(
-        body,
-        name="units",
-        out_shape=[array(*picture.shape)] * 2 + [jax.ShapeDtypeStruct((8, TILE), jnp.float32)],
-        in_specs=[pl.BlockSpec(memory_space=pltpu.SMEM)] * 4
-        + [pl.BlockSpec(memory_space=pltpu.HBM)] * 2,
-        scratch_shapes=[
-            pltpu.VMEM(picture.shape, jnp.bfloat16),
-            pltpu.VMEM(picture.shape, jnp.bfloat16),
-            pltpu.SemaphoreType.DMA((2 * picture.shape[0] // COPY_ROWS,)),
-        ],
-        compiler_params=pltpu.CompilerParams(vmem_limit_bytes=VMEM_BYTES),
-    )(core, *parameters, picture, caption)
+            fill(picture, caption)
+
+    shapes = [array(*picture.shape)] * 2 + [jax.ShapeDtypeStruct((8, TILE), jnp.float32)]
+    return call("units", body, shapes, [picture, caption], 6 * picture.size, [core, *parameters])
 
 
 def pack(*blocks):

time: 82.7 us -> 81.9 us (level)
    pallas_call x1 -> x0, Pallas kernels: 1.03 us -> none  [unit_halves(): pl.pallas_call(body, name='units', out_shape=[array(*picture.shape)] * 2...]
    pallas_call x13 -> x14, Pallas kernels: 26.1 us -> 26.3 us  [call(): pl.pallas_call(lambda *refs: body(*refs[len(after):]), name=name, out_sha...]
where the time goes in v3:
time: 81.9 us; the launch traced here: 81.7 us
  starting transfers between devices  31.2 us (38%)
  Pallas kernels  26.3 us (32%)
  waiting for transfers between devices  19.4 us (24%)
  between operations  2.77 us (3%)
  local copies, waits for them, and re-layouts  2.03 us (2%)
    ppermute x26, starting transfers between devices, sender(): return lambda value: lax.ppermute(value, ('blk', 'grp'), pairs)  31.2 us
    pallas_call x14, Pallas kernels, call(): pl.pallas_call(lambda *refs: body(*refs[len(after):]), name=name, out_sha...  26.3 us
    ppermute x26, waiting for transfers between devices, sender(): return lambda value: lax.ppermute(value, ('blk', 'grp'), pairs)  19.4 us
    unnamed x9, local copies, waits for them, and re-layouts  1.95 us
  transfers between devices with their start and end apart: 26, of which 10 were waited for; matrix products, arithmetic and copies ran while one was open for 0% of the time, Pallas kernels for 29%

profile of v3, /device:TPU:1, one launch (start us, length us, event | category | flops | bytes accessed | tf_op | source)
XLA Modules:
  0.0 81.7 jit_solution(16017623592249164498)
XLA Ops:
  2.6 1.0 %copy-done = bf16[128,1152]{1,0:T(8,128)(2,1)S(1)} copy-done((bf16[128,1152]{1,0:T(8,128)(2,1)S(1)}, bf16[128,1152]{1,0:T(8,128)(2,1)}, u32[]{:S(2)}) %copy-start) | copy-done | bytes 294936
  3.5 1.0 %copy-done.2 = bf16[128,1152]{1,0:T(8,128)(2,1)S(1)} copy-done((bf16[128,1152]{1,0:T(8,128)(2,1)S(1)}, bf16[128,1152]{1,0:T(8,128)(2,1)}, u32[]{:S(2)}) %copy-start.2) | copy-done | bytes 294936
  4.5 0.2 units.1
  4.7 1.5 %collective-permute-start = (bf16[128,1152]{1,0:T(8,128)(2,1)S(1)}, bf16[128,1152]{1,0:T(8,128)(2,1)S(1)}, u32[]{:S(2)}, u32[]{:S(2)}) collective-permute-start(bf16[128,1152]{1,0:T(8,128)(2,1)S(1)} %get-tuple-element.23), channel_id=1, source_target_pairs={{0,8},{8,0},{2,10},{10,2},{4,12},{12,4},{6,14},{14,6},{16,24},{24,... | collective-permute-start | bytes 884744 | tf_op jit(solution)/shard_map/ppermute | solution.py:29
  6.2 1.2 %collective-permute-done = bf16[128,1152]{1,0:T(8,128)(2,1)S(1)} collective-permute-done((bf16[128,1152]{1,0:T(8,128)(2,1)S(1)}, bf16[128,1152]{1,0:T(8,128)(2,1)S(1)}, u32[]{:S(2)}, u32[]{:S(2)}) %collective-permute-start) | collective-permute-done | bytes 294944 | tf_op jit(solution)/shard_map/ppermute | solution.py:29
  7.5 1.8 %collective-permute-start.5 = (bf16[256,1152]{1,0:T(8,128)(2,1)S(1)}, bf16[256,1152]{1,0:T(8,128)(2,1)S(1)}, u32[]{:S(2)}, u32[]{:S(2)}) collective-permute-start(bf16[256,1152]{1,0:T(8,128)(2,1)S(1)} %constant_dynamic-update-slice_fusion.refs_1_.refs_3_), channel_id=1, source_target_pairs={{0,16},{8,10},{2,18},{10,12},{4,20},{12,14},{6,22},{14,8},{16,32},... | collective-permute-start | bytes 1769480 | tf_op jit(solution)/shard_map/ppermute | solution.py:29
  9.3 2.5 %collective-permute-start.3 = (bf16[256,1152]{1,0:T(8,128)(2,1)S(1)}, bf16[256,1152]{1,0:T(8,128)(2,1)S(1)}, u32[]{:S(2)}, u32[]{:S(2)}) collective-permute-start(bf16[256,1152]{1,0:T(8,128)(2,1)S(1)} %constant_dynamic-update-slice_fusion.refs_1_.refs_3_), channel_id=1, source_target_pairs={{0,64},{8,73},{2,66},{10,75},{4,68},{12,77},{6,70},{14,79},{16,80}... | collective-permute-start | bytes 1769480 | tf_op jit(solution)/shard_map/ppermute | solution.py:29
  11.7 2.2 %collective-permute-start.1 = (bf16[256,1152]{1,0:T(8,128)(2,1)S(1)}, bf16[256,1152]{1,0:T(8,128)(2,1)S(1)}, u32[]{:S(2)}, u32[]{:S(2)}) collective-permute-start(bf16[256,1152]{1,0:T(8,128)(2,1)S(1)} %constant_dynamic-update-slice_fusion.refs_1_.refs_3_), channel_id=1, source_target_pairs={{0,48},{8,14},{2,50},{10,8},{4,52},{12,10},{6,54},{14,12},{16,0},{... | collective-permute-start | bytes 1769480 | tf_op jit(solution)/shard_map/ppermute | solution.py:29
  14.0 4.7 %collective-permute-done.5.refs_4_.refs_6_ = bf16[256,1152]{1,0:T(8,128)(2,1)S(1)} collective-permute-done((bf16[256,1152]{1,0:T(8,128)(2,1)S(1)}, bf16[256,1152]{1,0:T(8,128)(2,1)S(1)}, u32[]{:S(2)}, u32[]{:S(2)}) %collective-permute-start.5) | collective-permute-done | bytes 589856 | tf_op jit(solution)/shard_map/ppermute | solution.py:29
  18.6 0.4 collective-permute-start.9
  19.0 0.2 collective-permute-done.3.refs_2_.refs_4_
  19.2 0.3 collective-permute-start.7
  19.5 1.3 %collective-permute-done.1.refs_3_.refs_5_ = bf16[256,1152]{1,0:T(8,128)(2,1)S(1)} collective-permute-done((bf16[256,1152]{1,0:T(8,128)(2,1)S(1)}, bf16[256,1152]{1,0:T(8,128)(2,1)S(1)}, u32[]{:S(2)}, u32[]{:S(2)}) %collective-permute-start.1) | collective-permute-done | bytes 589856 | tf_op jit(solution)/shard_map/ppermute | solution.py:29
  20.8 0.2 collective-permute-start.8
  20.9 1.6 %collective-permute-start.4 = (bf16[256,1152]{1,0:T(8,128)(2,1)S(1)}, bf16[256,1152]{1,0:T(8,128)(2,1)S(1)}, u32[]{:S(2)}, u32[]{:S(2)}) collective-permute-start(bf16[256,1152]{1,0:T(8,128)(2,1)S(1)} %collective-permute-done.3.refs_2_.refs_4_), channel_id=1, source_target_pairs={{0,16},{8,10},{2,18},{10,12},{4,20},{12,14},{6,22},{14,8},{16,32},... | collective-permute-start | bytes 1769480 | tf_op jit(solution)/shard_map/ppermute | solution.py:29
  22.6 2.1 %collective-permute-start.2 = (bf16[256,1152]{1,0:T(8,128)(2,1)S(1)}, bf16[256,1152]{1,0:T(8,128)(2,1)S(1)}, u32[]{:S(2)}, u32[]{:S(2)}) collective-permute-start(bf16[256,1152]{1,0:T(8,128)(2,1)S(1)} %collective-permute-done.1.refs_3_.refs_5_), channel_id=1, source_target_pairs={{0,48},{8,14},{2,50},{10,8},{4,52},{12,10},{6,54},{14,12},{16,0},{... | collective-permute-start | bytes 1769480 | tf_op jit(solution)/shard_map/ppermute | solution.py:29
  24.7 1.8 %collective-permute-start.12 = (bf16[256,1152]{1,0:T(8,128)(2,1)S(1)}, bf16[256,1152]{1,0:T(8,128)(2,1)S(1)}, u32[]{:S(2)}, u32[]{:S(2)}) collective-permute-start(bf16[256,1152]{1,0:T(8,128)(2,1)S(1)} %collective-permute-done.1.refs_3_.refs_5_), channel_id=1, source_target_pairs={{0,64},{8,73},{2,66},{10,75},{4,68},{12,77},{6,70},{14,79},{16,80}... | collective-permute-start | bytes 1769480 | tf_op jit(solution)/shard_map/ppermute | solution.py:29
  26.5 5.8 %near.1.refs_11_ = f32[1024,1152]{1,0:T(8,128)S(1)} custom-call(f32[8,256]{1,0:T(8,128)S(1)} %get-tuple-element.21.refs_0_.refs_1_.refs_2_, bf16[256,1152]{1,0:T(8,128)(2,1)S(1)} %constant_dynamic-update-slice_fusion.refs_1_.refs_3_, bf16[256,1152]{1,0:T(8,128)(2,1)S(1)} %collective-permute-done.3.refs_2_.refs_4_, ...), custom_call_target="tpu_custom_call" | custom-call | flops 75497472 | bytes 110656 | tf_op jit(solution)/shard_map/near/pallas_call | solution.py:45
  32.4 1.0 %collective-permute-start.11 = (bf16[128,1152]{1,0:T(8,128)(2,1)S(1)}, bf16[128,1152]{1,0:T(8,128)(2,1)S(1)}, u32[]{:S(2)}, u32[]{:S(2)}) collective-permute-start(bf16[128,1152]{1,0:T(8,128)(2,1)S(1)} %slice.7), channel_id=1, source_target_pairs={{0,16},{8,10},{2,18},{10,12},{4,20},{12,14},{6,22},{14,8},{16,32},... | collective-permute-start | bytes 884744 | tf_op jit(solution)/shard_map/ppermute | solution.py:29
  33.4 1.8 %collective-permute-start.10 = (bf16[128,1152]{1,0:T(8,128)(2,1)S(1)}, bf16[128,1152]{1,0:T(8,128)(2,1)S(1)}, u32[]{:S(2)}, u32[]{:S(2)}) collective-permute-start(bf16[128,1152]{1,0:T(8,128)(2,1)S(1)} %slice.6), channel_id=1, source_target_pairs={{0,64},{8,73},{2,66},{10,75},{4,68},{12,77},{6,70},{14,79},{16,80}... | collective-permute-start | bytes 884744 | tf_op jit(solution)/shard_map/ppermute | solution.py:29
  35.2 0.5 collective-permute-start.15
  35.7 4.4 %middle.1.refs_9_ = f32[768,1152]{1,0:T(8,128)S(1)} custom-call(f32[8,256]{1,0:T(8,128)S(1)} %get-tuple-element.21.refs_0_.refs_1_.refs_2_, bf16[256,1152]{1,0:T(8,128)(2,1)S(1)} %collective-permute-done.12.refs_1_.refs_2_, bf16[256,1152]{1,0:T(8,128)(2,1)S(1)} %collective-permute-done.4.refs_2_.refs_3_, ...), custom_call_target="tpu_custom_call" | custom-call | flops 56623104 | bytes 92224 | tf_op jit(solution)/shard_map/middle/pallas_call | solution.py:45
  40.1 0.3 collective-permute-done.10.refs_0_
  40.5 0.8 %collective-permute-start.13 = (bf16[256,1152]{1,0:T(8,128)(2,1)S(1)}, bf16[256,1152]{1,0:T(8,128)(2,1)S(1)}, u32[]{:S(2)}, u32[]{:S(2)}) collective-permute-start(bf16[256,1152]{1,0:T(8,128)(2,1)S(1)} %pack.1.refs_1_), channel_id=1, source_target_pairs={{0,8},{8,0},{2,10},{10,2},{4,12},{12,4},{6,14},{14,6},{16,24},{24,... | collective-permute-start | bytes 1769480 | tf_op jit(solution)/shard_map/ppermute | solution.py:29
  41.3 2.6 %last.1.refs_3_ = f32[256,1152]{1,0:T(8,128)S(1)} custom-call(f32[8,256]{1,0:T(8,128)S(1)} %get-tuple-element.21.refs_0_.refs_1_.refs_2_, bf16[256,1152]{1,0:T(8,128)(2,1)S(1)} %pack.1.refs_1_, bf16[256,1152]{1,0:T(8,128)(2,1)S(1)} %collective-permute-done.6.refs_5_.refs_4_.refs_2_, bf16[256,1152]{1,0:T(8,128)(2,1)S(1)} %collective-permute-done.7.refs_6_.refs_5_.refs_3_, ...), custom_call_target="tpu_custom_call" | custom-call | flops 33030144 | bytes 83008 | tf_op jit(solution)/shard_map/last/pallas_call | solution.py:45
  44.0 0.9 %last_rest.1 = (bf16[128,1152]{1,0:T(8,128)(2,1)S(1)}, bf16[128,1152]{1,0:T(8,128)(2,1)S(1)}) custom-call(f32[8,256]{1,0:T(8,128)S(1)} %get-tuple-element.21.refs_0_.refs_1_.refs_2_, bf16[256,1152]{1,0:T(8,128)(2,1)S(1)} %pack.1.refs_1_, bf16[256,1152]{1,0:T(8,128)(2,1)S(1)} %collective-permute-done.13.refs_2_.refs_8_.refs_10_, f32[256,1152]{1,0:T(8,128)S(1)} %last.1.refs_3_), custom_call_target="tpu_custom_call" | custom-call | flops 4718592 | bytes 36928 | tf_op jit(solution)/shard_map/last_rest/pallas_call | solution.py:45
  44.9 3.2 %collective-permute-start.18 = (bf16[128,1152]{1,0:T(8,128)(2,1)S(1)}, bf16[128,1152]{1,0:T(8,128)(2,1)S(1)}, u32[]{:S(2)}, u32[]{:S(2)}) collective-permute-start(bf16[128,1152]{1,0:T(8,128)(2,1)S(1)} %get-tuple-element.33), channel_id=1, source_target_pairs={{0,48},{8,14},{2,50},{10,8},{4,52},{12,10},{6,54},{14,12},{16,0},{... | collective-permute-start | bytes 884744 | tf_op jit(solution)/shard_map/ppermute | solution.py:29
  48.1 1.8 %collective-permute-start.17 = (bf16[128,1152]{1,0:T(8,128)(2,1)S(1)}, bf16[128,1152]{1,0:T(8,128)(2,1)S(1)}, u32[]{:S(2)}, u32[]{:S(2)}) collective-permute-start(bf16[128,1152]{1,0:T(8,128)(2,1)S(1)} %get-tuple-element.29.refs_0_), channel_id=1, source_target_pairs={{0,64},{8,73},{2,66},{10,75},{4,68},{12,77},{6,70},{14,79},{16,80}... | collective-permute-start | bytes 884744 | tf_op jit(solution)/shard_map/ppermute | solution.py:29
  49.9 4.4 %middle_rest.1 = (bf16[256,1152]{1,0:T(8,128)(2,1)S(1)}, bf16[256,1152]{1,0:T(8,128)(2,1)S(1)}, bf16[256,1152]{1,0:T(8,128)(2,1)S(1)}) custom-call(bf16[128,1152]{1,0:T(8,128)(2,1)S(1)} %get-tuple-element.29.refs_0_, f32[8,256]{1,0:T(8,128)S(1)} %get-tuple-element.21.refs_0_.refs_1_.refs_2_, bf16[256,1152]{1,0:T(8,128)(2,1)S(1)} %collective-permute-done.12.refs_1_.refs_2_, ...), custom_call_target="tpu_custom_call" | custom-call | flops 56623104 | bytes 119872 | tf_op jit(solution)/shard_map/middle_rest/pallas_call | solution.py:45
  54.4 0.1 add_half.3.refs_1_
  54.5 0.6 collective-permute-start.23
  55.0 1.8 %collective-permute-start.20 = (bf16[256,1152]{1,0:T(8,128)(2,1)S(1)}, bf16[256,1152]{1,0:T(8,128)(2,1)S(1)}, u32[]{:S(2)}, u32[]{:S(2)}) collective-permute-start(bf16[256,1152]{1,0:T(8,128)(2,1)S(1)} %get-tuple-element.37), channel_id=1, source_target_pairs={{0,64},{8,73},{2,66},{10,75},{4,68},{12,77},{6,70},{14,79},{16,80}... | collective-permute-start | bytes 1769480 | tf_op jit(solution)/shard_map/ppermute | solution.py:29
  56.9 0.1 add_half.2.refs_0_
  57.0 0.3 collective-permute-start.19
  57.3 5.8 %near_rest.1 = (bf16[256,1152]{1,0:T(8,128)(2,1)S(1)}, bf16[256,1152]{1,0:T(8,128)(2,1)S(1)}, bf16[256,1152]{1,0:T(8,128)(2,1)S(1)}, bf16[256,1152]{1,0:T(8,128)(2,1)S(1)}) custom-call(bf16[256,1152]{1,0:T(8,128)(2,1)S(1)} %add_half.2.refs_0_, bf16[256,1152]{1,0:T(8,128)(2,1)S(1)} %add_half.3.refs_1_, ...), custom_call_target="tpu_custom_call" | custom-call | flops 75497472 | bytes 147520 | tf_op jit(solution)/shard_map/near_rest/pallas_call | solution.py:45
  63.1 2.7 %collective-permute-start.22 = (bf16[256,1152]{1,0:T(8,128)(2,1)S(1)}, bf16[256,1152]{1,0:T(8,128)(2,1)S(1)}, u32[]{:S(2)}, u32[]{:S(2)}) collective-permute-start(bf16[256,1152]{1,0:T(8,128)(2,1)S(1)} %get-tuple-element.38), channel_id=1, source_target_pairs={{0,48},{8,14},{2,50},{10,8},{4,52},{12,10},{6,54},{14,12},{16,0},{... | collective-permute-start | bytes 1769480 | tf_op jit(solution)/shard_map/ppermute | solution.py:29
  65.8 0.1 add.3
  66.0 0.9 %collective-permute-start.24 = (bf16[256,1152]{1,0:T(8,128)(2,1)S(1)}, bf16[256,1152]{1,0:T(8,128)(2,1)S(1)}, u32[]{:S(2)}, u32[]{:S(2)}) collective-permute-start(bf16[256,1152]{1,0:T(8,128)(2,1)S(1)} %add.3), channel_id=1, source_target_pairs={{0,64},{8,73},{2,66},{10,75},{4,68},{12,77},{6,70},{14,79},{16,80}... | collective-permute-start | bytes 1769480 | tf_op jit(solution)/shard_map/ppermute | solution.py:29
  66.9 0.3 collective-permute-done.19.refs_1_
  67.2 0.2 add.2
  67.4 0.1 collective-permute-start.21
  67.5 5.2 %collective-permute-done.22.refs_2_.refs_6_ = bf16[256,1152]{1,0:T(8,128)(2,1)S(1)} collective-permute-done((bf16[256,1152]{1,0:T(8,128)(2,1)S(1)}, bf16[256,1152]{1,0:T(8,128)(2,1)S(1)}, u32[]{:S(2)}, u32[]{:S(2)}) %collective-permute-start.22) | collective-permute-done | bytes 589856 | tf_op jit(solution)/shard_map/ppermute | solution.py:29
  72.7 3.6 %collective-permute-done.24.refs_3_.refs_7_ = bf16[256,1152]{1,0:T(8,128)(2,1)S(1)} collective-permute-done((bf16[256,1152]{1,0:T(8,128)(2,1)S(1)}, bf16[256,1152]{1,0:T(8,128)(2,1)S(1)}, u32[]{:S(2)}, u32[]{:S(2)}) %collective-permute-start.24) | collective-permute-done | bytes 589856 | tf_op jit(solution)/shard_map/ppermute | solution.py:29
  76.3 1.4 %collective-permute-done.21.refs_1_.refs_5_ = bf16[256,1152]{1,0:T(8,128)(2,1)S(1)} collective-permute-done((bf16[256,1152]{1,0:T(8,128)(2,1)S(1)}, bf16[256,1152]{1,0:T(8,128)(2,1)S(1)}, u32[]{:S(2)}, u32[]{:S(2)}) %collective-permute-start.21) | collective-permute-done | bytes 589856 | tf_op jit(solution)/shard_map/ppermute | solution.py:29
  77.7 0.1 give.1
  77.9 1.3 %collective-permute-start.25 = (bf16[128,1152]{1,0:T(8,128)(2,1)S(1)}, bf16[128,1152]{1,0:T(8,128)(2,1)S(1)}, u32[]{:S(2)}, u32[]{:S(2)}) collective-permute-start(bf16[128,1152]{1,0:T(8,128)(2,1)S(1)} %give.1), channel_id=1, source_target_pairs={{0,8},{8,0},{2,10},{10,2},{4,12},{12,4},{6,14},{14,6},{16,24},{24,... | collective-permute-start | bytes 884744 | tf_op jit(solution)/shard_map/ppermute | solution.py:29
  79.1 1.2 %collective-permute-done.25.refs_3_ = bf16[128,1152]{1,0:T(8,128)(2,1)S(1)} collective-permute-done((bf16[128,1152]{1,0:T(8,128)(2,1)S(1)}, bf16[128,1152]{1,0:T(8,128)(2,1)S(1)}, u32[]{:S(2)}, u32[]{:S(2)}) %collective-permute-start.25) | collective-permute-done | bytes 294944 | tf_op jit(solution)/shard_map/ppermute | solution.py:29
  80.3 1.4 %final.1 = (bf16[128,1152]{1,0:T(8,128)(2,1)}, bf16[128,1152]{1,0:T(8,128)(2,1)}) custom-call(s32[1]{0:T(128)} %bitcast.refs_0_, bf16[128,1152]{1,0:T(8,128)(2,1)S(1)} %copy-done.1, bf16[128,1152]{1,0:T(8,128)(2,1)S(1)} %copy-done.3, bf16[128,1152]{1,0:T(8,128)(2,1)S(1)} %collective-permute-done.25.refs_3_, ...), custom_call_target="tpu_custom_call" | custom-call | flops 46080 | bytes 59904 | tf_op jit(solution)/shard_map/final/pallas_call | solution.py:45
  (30 shorter events, 0.2 us)
Async XLA Ops:
  2.6 1.0 %copy-start = (bf16[128,1152]{1,0:T(8,128)(2,1)S(1)}, bf16[128,1152]{1,0:T(8,128)(2,1)}, u32[]{:S(2)}) copy-start(bf16[128,1152]{1,0:T(8,128)(2,1)} %refs_1_.1) | copy-start | bytes 884740
  3.5 1.0 %copy-start.2 = (bf16[128,1152]{1,0:T(8,128)(2,1)S(1)}, bf16[128,1152]{1,0:T(8,128)(2,1)}, u32[]{:S(2)}) copy-start(bf16[128,1152]{1,0:T(8,128)(2,1)} %refs_2_.1) | copy-start | bytes 884740
  4.7 2.7 %collective-permute-start = (bf16[128,1152]{1,0:T(8,128)(2,1)S(1)}, bf16[128,1152]{1,0:T(8,128)(2,1)S(1)}, u32[]{:S(2)}, u32[]{:S(2)}) collective-permute-start(bf16[128,1152]{1,0:T(8,128)(2,1)S(1)} %get-tuple-element.23), channel_id=1, source_target_pairs={{0,8},{8,0},{2,10},{10,2},{4,12},{12,4},{6,14},{14,6},{16,24},{24,... | collective-permute-start | bytes 884744 | tf_op jit(solution)/shard_map/ppermute | solution.py:29
  7.5 11.2 %collective-permute-start.5 = (bf16[256,1152]{1,0:T(8,128)(2,1)S(1)}, bf16[256,1152]{1,0:T(8,128)(2,1)S(1)}, u32[]{:S(2)}, u32[]{:S(2)}) collective-permute-start(bf16[256,1152]{1,0:T(8,128)(2,1)S(1)} %constant_dynamic-update-slice_fusion.refs_1_.refs_3_), channel_id=1, source_target_pairs={{0,16},{8,10},{2,18},{10,12},{4,20},{12,14},{6,22},{14,8},{16,32},... | collective-permute-start | bytes 1769480 | tf_op jit(solution)/shard_map/ppermute | solution.py:29
  9.3 9.9 %collective-permute-start.3 = (bf16[256,1152]{1,0:T(8,128)(2,1)S(1)}, bf16[256,1152]{1,0:T(8,128)(2,1)S(1)}, u32[]{:S(2)}, u32[]{:S(2)}) collective-permute-start(bf16[256,1152]{1,0:T(8,128)(2,1)S(1)} %constant_dynamic-update-slice_fusion.refs_1_.refs_3_), channel_id=1, source_target_pairs={{0,64},{8,73},{2,66},{10,75},{4,68},{12,77},{6,70},{14,79},{16,80}... | collective-permute-start | bytes 1769480 | tf_op jit(solution)/shard_map/ppermute | solution.py:29
  11.7 9.0 %collective-permute-start.1 = (bf16[256,1152]{1,0:T(8,128)(2,1)S(1)}, bf16[256,1152]{1,0:T(8,128)(2,1)S(1)}, u32[]{:S(2)}, u32[]{:S(2)}) collective-permute-start(bf16[256,1152]{1,0:T(8,128)(2,1)S(1)} %constant_dynamic-update-slice_fusion.refs_1_.refs_3_), channel_id=1, source_target_pairs={{0,48},{8,14},{2,50},{10,8},{4,52},{12,10},{6,54},{14,12},{16,0},{... | collective-permute-start | bytes 1769480 | tf_op jit(solution)/shard_map/ppermute | solution.py:29
  13.9 8.6 %collective-permute-start.6 = (bf16[256,1152]{1,0:T(8,128)(2,1)S(1)}, bf16[256,1152]{1,0:T(8,128)(2,1)S(1)}, u32[]{:S(2)}, u32[]{:S(2)}) collective-permute-start(bf16[256,1152]{1,0:T(8,128)(2,1)S(1)} %constant_dynamic-update-slice_fusion.refs_1_.refs_3_), channel_id=1, source_target_pairs={{0,8},{8,0},{2,10},{10,2},{4,12},{12,4},{6,14},{14,6},{16,24},{24,... | collective-permute-start | bytes 1769480 | tf_op jit(solution)/shard_map/ppermute | solution.py:29
  18.6 6.1 %collective-permute-start.9 = (bf16[256,1152]{1,0:T(8,128)(2,1)S(1)}, bf16[256,1152]{1,0:T(8,128)(2,1)S(1)}, u32[]{:S(2)}, u32[]{:S(2)}) collective-permute-start(bf16[256,1152]{1,0:T(8,128)(2,1)S(1)} %collective-permute-done.5.refs_4_.refs_6_), channel_id=1, source_target_pairs={{0,8},{8,0},{2,10},{10,2},{4,12},{12,4},{6,14},{14,6},{16,24},{24,... | collective-permute-start | bytes 1769480 | tf_op jit(solution)/shard_map/ppermute | solution.py:29
  19.2 7.3 %collective-permute-start.7 = (bf16[256,1152]{1,0:T(8,128)(2,1)S(1)}, bf16[256,1152]{1,0:T(8,128)(2,1)S(1)}, u32[]{:S(2)}, u32[]{:S(2)}) collective-permute-start(bf16[256,1152]{1,0:T(8,128)(2,1)S(1)} %collective-permute-done.3.refs_2_.refs_4_), channel_id=1, source_target_pairs={{0,8},{8,0},{2,10},{10,2},{4,12},{12,4},{6,14},{14,6},{16,24},{24,... | collective-permute-start | bytes 1769480 | tf_op jit(solution)/shard_map/ppermute | solution.py:29
  20.8 5.8 %collective-permute-start.8 = (bf16[256,1152]{1,0:T(8,128)(2,1)S(1)}, bf16[256,1152]{1,0:T(8,128)(2,1)S(1)}, u32[]{:S(2)}, u32[]{:S(2)}) collective-permute-start(bf16[256,1152]{1,0:T(8,128)(2,1)S(1)} %collective-permute-done.1.refs_3_.refs_5_), channel_id=1, source_target_pairs={{0,8},{8,0},{2,10},{10,2},{4,12},{12,4},{6,14},{14,6},{16,24},{24,... | collective-permute-start | bytes 1769480 | tf_op jit(solution)/shard_map/ppermute | solution.py:29
  20.9 11.4 %collective-permute-start.4 = (bf16[256,1152]{1,0:T(8,128)(2,1)S(1)}, bf16[256,1152]{1,0:T(8,128)(2,1)S(1)}, u32[]{:S(2)}, u32[]{:S(2)}) collective-permute-start(bf16[256,1152]{1,0:T(8,128)(2,1)S(1)} %collective-permute-done.3.refs_2_.refs_4_), channel_id=1, source_target_pairs={{0,16},{8,10},{2,18},{10,12},{4,20},{12,14},{6,22},{14,8},{16,32},... | collective-permute-start | bytes 1769480 | tf_op jit(solution)/shard_map/ppermute | solution.py:29
  22.6 9.7 %collective-permute-start.2 = (bf16[256,1152]{1,0:T(8,128)(2,1)S(1)}, bf16[256,1152]{1,0:T(8,128)(2,1)S(1)}, u32[]{:S(2)}, u32[]{:S(2)}) collective-permute-start(bf16[256,1152]{1,0:T(8,128)(2,1)S(1)} %collective-permute-done.1.refs_3_.refs_5_), channel_id=1, source_target_pairs={{0,48},{8,14},{2,50},{10,8},{4,52},{12,10},{6,54},{14,12},{16,0},{... | collective-permute-start | bytes 1769480 | tf_op jit(solution)/shard_map/ppermute | solution.py:29
  24.7 11.0 %collective-permute-start.12 = (bf16[256,1152]{1,0:T(8,128)(2,1)S(1)}, bf16[256,1152]{1,0:T(8,128)(2,1)S(1)}, u32[]{:S(2)}, u32[]{:S(2)}) collective-permute-start(bf16[256,1152]{1,0:T(8,128)(2,1)S(1)} %collective-permute-done.1.refs_3_.refs_5_), channel_id=1, source_target_pairs={{0,64},{8,73},{2,66},{10,75},{4,68},{12,77},{6,70},{14,79},{16,80}... | collective-permute-start | bytes 1769480 | tf_op jit(solution)/shard_map/ppermute | solution.py:29
  32.4 7.7 %collective-permute-start.11 = (bf16[128,1152]{1,0:T(8,128)(2,1)S(1)}, bf16[128,1152]{1,0:T(8,128)(2,1)S(1)}, u32[]{:S(2)}, u32[]{:S(2)}) collective-permute-start(bf16[128,1152]{1,0:T(8,128)(2,1)S(1)} %slice.7), channel_id=1, source_target_pairs={{0,16},{8,10},{2,18},{10,12},{4,20},{12,14},{6,22},{14,8},{16,32},... | collective-permute-start | bytes 884744 | tf_op jit(solution)/shard_map/ppermute | solution.py:29
  33.4 7.0 %collective-permute-start.10 = (bf16[128,1152]{1,0:T(8,128)(2,1)S(1)}, bf16[128,1152]{1,0:T(8,128)(2,1)S(1)}, u32[]{:S(2)}, u32[]{:S(2)}) collective-permute-start(bf16[128,1152]{1,0:T(8,128)(2,1)S(1)} %slice.6), channel_id=1, source_target_pairs={{0,64},{8,73},{2,66},{10,75},{4,68},{12,77},{6,70},{14,79},{16,80}... | collective-permute-start | bytes 884744 | tf_op jit(solution)/shard_map/ppermute | solution.py:29
  35.2 6.1 %collective-permute-start.16 = (bf16[256,1152]{1,0:T(8,128)(2,1)S(1)}, bf16[256,1152]{1,0:T(8,128)(2,1)S(1)}, u32[]{:S(2)}, u32[]{:S(2)}) collective-permute-start(bf16[256,1152]{1,0:T(8,128)(2,1)S(1)} %collective-permute-done.2.refs_3_.refs_4_), channel_id=1, source_target_pairs={{0,8},{8,0},{2,10},{10,2},{4,12},{12,4},{6,14},{14,6},{16,24},{24,... | collective-permute-start | bytes 1769480 | tf_op jit(solution)/shard_map/ppermute | solution.py:29
  35.2 6.1 %collective-permute-start.15 = (bf16[256,1152]{1,0:T(8,128)(2,1)S(1)}, bf16[256,1152]{1,0:T(8,128)(2,1)S(1)}, u32[]{:S(2)}, u32[]{:S(2)}) collective-permute-start(bf16[256,1152]{1,0:T(8,128)(2,1)S(1)} %collective-permute-done.4.refs_2_.refs_3_), channel_id=1, source_target_pairs={{0,8},{8,0},{2,10},{10,2},{4,12},{12,4},{6,14},{14,6},{16,24},{24,... | collective-permute-start | bytes 1769480 | tf_op jit(solution)/shard_map/ppermute | solution.py:29
  35.7 5.6 %collective-permute-start.14 = (bf16[256,1152]{1,0:T(8,128)(2,1)S(1)}, bf16[256,1152]{1,0:T(8,128)(2,1)S(1)}, u32[]{:S(2)}, u32[]{:S(2)}) collective-permute-start(bf16[256,1152]{1,0:T(8,128)(2,1)S(1)} %collective-permute-done.12.refs_1_.refs_2_), channel_id=1, source_target_pairs={{0,8},{8,0},{2,10},{10,2},{4,12},{12,4},{6,14},{14,6},{16,24},{24,... | collective-permute-start | bytes 1769480 | tf_op jit(solution)/shard_map/ppermute | solution.py:29
  40.5 3.5 %collective-permute-start.13 = (bf16[256,1152]{1,0:T(8,128)(2,1)S(1)}, bf16[256,1152]{1,0:T(8,128)(2,1)S(1)}, u32[]{:S(2)}, u32[]{:S(2)}) collective-permute-start(bf16[256,1152]{1,0:T(8,128)(2,1)S(1)} %pack.1.refs_1_), channel_id=1, source_target_pairs={{0,8},{8,0},{2,10},{10,2},{4,12},{12,4},{6,14},{14,6},{16,24},{24,... | collective-permute-start | bytes 1769480 | tf_op jit(solution)/shard_map/ppermute | solution.py:29
  44.9 9.5 %collective-permute-start.18 = (bf16[128,1152]{1,0:T(8,128)(2,1)S(1)}, bf16[128,1152]{1,0:T(8,128)(2,1)S(1)}, u32[]{:S(2)}, u32[]{:S(2)}) collective-permute-start(bf16[128,1152]{1,0:T(8,128)(2,1)S(1)} %get-tuple-element.33), channel_id=1, source_target_pairs={{0,48},{8,14},{2,50},{10,8},{4,52},{12,10},{6,54},{14,12},{16,0},{... | collective-permute-start | bytes 884744 | tf_op jit(solution)/shard_map/ppermute | solution.py:29
  48.1 8.8 %collective-permute-start.17 = (bf16[128,1152]{1,0:T(8,128)(2,1)S(1)}, bf16[128,1152]{1,0:T(8,128)(2,1)S(1)}, u32[]{:S(2)}, u32[]{:S(2)}) collective-permute-start(bf16[128,1152]{1,0:T(8,128)(2,1)S(1)} %get-tuple-element.29.refs_0_), channel_id=1, source_target_pairs={{0,64},{8,73},{2,66},{10,75},{4,68},{12,77},{6,70},{14,79},{16,80}... | collective-permute-start | bytes 884744 | tf_op jit(solution)/shard_map/ppermute | solution.py:29
  54.5 11.4 %collective-permute-start.23 = (bf16[256,1152]{1,0:T(8,128)(2,1)S(1)}, bf16[256,1152]{1,0:T(8,128)(2,1)S(1)}, u32[]{:S(2)}, u32[]{:S(2)}) collective-permute-start(bf16[256,1152]{1,0:T(8,128)(2,1)S(1)} %add_half.3.refs_1_), channel_id=1, source_target_pairs={{0,48},{8,14},{2,50},{10,8},{4,52},{12,10},{6,54},{14,12},{16,0},{... | collective-permute-start | bytes 1769480 | tf_op jit(solution)/shard_map/ppermute | solution.py:29
  55.0 11.9 %collective-permute-start.20 = (bf16[256,1152]{1,0:T(8,128)(2,1)S(1)}, bf16[256,1152]{1,0:T(8,128)(2,1)S(1)}, u32[]{:S(2)}, u32[]{:S(2)}) collective-permute-start(bf16[256,1152]{1,0:T(8,128)(2,1)S(1)} %get-tuple-element.37), channel_id=1, source_target_pairs={{0,64},{8,73},{2,66},{10,75},{4,68},{12,77},{6,70},{14,79},{16,80}... | collective-permute-start | bytes 1769480 | tf_op jit(solution)/shard_map/ppermute | solution.py:29
  57.0 10.2 %collective-permute-start.19 = (bf16[256,1152]{1,0:T(8,128)(2,1)S(1)}, bf16[256,1152]{1,0:T(8,128)(2,1)S(1)}, u32[]{:S(2)}, u32[]{:S(2)}) collective-permute-start(bf16[256,1152]{1,0:T(8,128)(2,1)S(1)} %add_half.2.refs_0_), channel_id=1, source_target_pairs={{0,16},{8,10},{2,18},{10,12},{4,20},{12,14},{6,22},{14,8},{16,32},... | collective-permute-start | bytes 1769480 | tf_op jit(solution)/shard_map/ppermute | solution.py:29
  63.1 17.3 %copy-start.1 = (bf16[128,1152]{1,0:T(8,128)(2,1)S(1)}, bf16[128,1152]{1,0:T(8,128)(2,1)}, u32[]{:S(2)}) copy-start(bf16[128,1152]{1,0:T(8,128)(2,1)} %refs_1_.1) | copy-start | bytes 884740
  63.1 17.2 %copy-start.3 = (bf16[128,1152]{1,0:T(8,128)(2,1)S(1)}, bf16[128,1152]{1,0:T(8,128)(2,1)}, u32[]{:S(2)}) copy-start(bf16[128,1152]{1,0:T(8,128)(2,1)} %refs_2_.1) | copy-start | bytes 884740
  63.1 9.6 %collective-permute-start.22 = (bf16[256,1152]{1,0:T(8,128)(2,1)S(1)}, bf16[256,1152]{1,0:T(8,128)(2,1)S(1)}, u32[]{:S(2)}, u32[]{:S(2)}) collective-permute-start(bf16[256,1152]{1,0:T(8,128)(2,1)S(1)} %get-tuple-element.38), channel_id=1, source_target_pairs={{0,48},{8,14},{2,50},{10,8},{4,52},{12,10},{6,54},{14,12},{16,0},{... | collective-permute-start | bytes 1769480 | tf_op jit(solution)/shard_map/ppermute | solution.py:29
  66.0 10.3 %collective-permute-start.24 = (bf16[256,1152]{1,0:T(8,128)(2,1)S(1)}, bf16[256,1152]{1,0:T(8,128)(2,1)S(1)}, u32[]{:S(2)}, u32[]{:S(2)}) collective-permute-start(bf16[256,1152]{1,0:T(8,128)(2,1)S(1)} %add.3), channel_id=1, source_target_pairs={{0,64},{8,73},{2,66},{10,75},{4,68},{12,77},{6,70},{14,79},{16,80}... | collective-permute-start | bytes 1769480 | tf_op jit(solution)/shard_map/ppermute | solution.py:29
  67.4 10.3 %collective-permute-start.21 = (bf16[256,1152]{1,0:T(8,128)(2,1)S(1)}, bf16[256,1152]{1,0:T(8,128)(2,1)S(1)}, u32[]{:S(2)}, u32[]{:S(2)}) collective-permute-start(bf16[256,1152]{1,0:T(8,128)(2,1)S(1)} %add.2), channel_id=1, source_target_pairs={{0,16},{8,10},{2,18},{10,12},{4,20},{12,14},{6,22},{14,8},{16,32},... | collective-permute-start | bytes 1769480 | tf_op jit(solution)/shard_map/ppermute | solution.py:29
  77.9 2.5 %collective-permute-start.25 = (bf16[128,1152]{1,0:T(8,128)(2,1)S(1)}, bf16[128,1152]{1,0:T(8,128)(2,1)S(1)}, u32[]{:S(2)}, u32[]{:S(2)}) collective-permute-start(bf16[128,1152]{1,0:T(8,128)(2,1)S(1)} %give.1), channel_id=1, source_target_pairs={{0,8},{8,0},{2,10},{10,2},{4,12},{12,4},{6,14},{14,6},{16,24},{24,... | collective-permute-start | bytes 884744 | tf_op jit(solution)/shard_map/ppermute | solution.py:29

commit v4 on v3

--- a/solution.py
+++ b/solution.py
@@ -10,6 +10,7 @@
 RING = 4
 CORES = 2
 TILE = 256
+SEND_FLOPS = 10**12
 VMEM_BYTES = 24 * 1024 * 1024
 
 
@@ -268,7 +269,8 @@
     partner_above, partner_below, far = sums(
         "middle_rest", constants, middle, rest, middle_held, rows_out=2 * rows, after=[last_0]
     )
-    far, partner_below = add_half(far, to_far, 0), add_half(partner_below, to_below, 1)
+    far = add_half(far, to_far, 0, flops=SEND_FLOPS)
+    partner_below = add_half(partner_below, to_below, 1, flops=SEND_FLOPS)
     to_above, to_partner, to_above_too = up(far), down(partner_below), cross(partner_above)
     own, partner, above, below = sums(
         "near_rest",
@@ -279,7 +281,8 @@
         rows_out=2 * rows,
         after=[far, partner_below],
     )
-    above, partner = add(above, to_above, to_above_too), add(partner, to_partner)
+    above = add(add(above, to_above_too, flops=SEND_FLOPS), to_above)
+    partner = add(partner, to_partner)
     terms = [own, up(above), down(below), cross(partner)]
     image_grad, text_grad = through_norms(core, picture_vectors, caption_vectors, terms)
     return image_grad, text_grad

time: 81.9 us -> 81.4 us (level)
  starting transfers between devices: 31.2 us -> 30.3 us
    ppermute x26, starting transfers between devices: 31.2 us -> 30.3 us  [sender(): return lambda value: lax.ppermute(value, ('blk', 'grp'), pairs)]
    pallas_call x14 -> x15, Pallas kernels: 26.3 us -> 26.4 us  [call(): pl.pallas_call(lambda *refs: body(*refs[len(after):]), name=name, out_sha...]
  transfers between devices with their start and end apart: 26 -> 26, of which waited for: 10 -> 11; matrix products, arithmetic and copies ran while one was open for 0% -> 0% of each run, Pallas kernels for 29% -> 29%
where the time goes in v4:
time: 81.4 us; the launch traced here: 81.2 us
  starting transfers between devices  30.3 us (37%)
  Pallas kernels  26.4 us (32%)
  waiting for transfers between devices  19.7 us (24%)
  between operations  2.77 us (3%)
  local copies, waits for them, and re-layouts  2.03 us (2%)
    ppermute x26, starting transfers between devices, sender(): return lambda value: lax.ppermute(value, ('blk', 'grp'), pairs)  30.3 us
    pallas_call x15, Pallas kernels, call(): pl.pallas_call(lambda *refs: body(*refs[len(after):]), name=name, out_sha...  26.4 us
    ppermute x26, waiting for transfers between devices, sender(): return lambda value: lax.ppermute(value, ('blk', 'grp'), pairs)  19.7 us
    unnamed x9, local copies, waits for them, and re-layouts  1.95 us
  transfers between devices with their start and end apart: 26, of which 11 were waited for; matrix products, arithmetic and copies ran while one was open for 0% of the time, Pallas kernels for 29%

profile of v4, /device:TPU:1, one launch (start us, length us, event | category | flops | bytes accessed | tf_op | source)
XLA Modules:
  0.0 81.2 jit_solution(15368087121303008306)
XLA Ops:
  2.6 1.0 %copy-done = bf16[128,1152]{1,0:T(8,128)(2,1)S(1)} copy-done((bf16[128,1152]{1,0:T(8,128)(2,1)S(1)}, bf16[128,1152]{1,0:T(8,128)(2,1)}, u32[]{:S(2)}) %copy-start) | copy-done | bytes 294936
  3.5 1.0 %copy-done.2 = bf16[128,1152]{1,0:T(8,128)(2,1)S(1)} copy-done((bf16[128,1152]{1,0:T(8,128)(2,1)S(1)}, bf16[128,1152]{1,0:T(8,128)(2,1)}, u32[]{:S(2)}) %copy-start.2) | copy-done | bytes 294936
  4.5 0.2 units.1
  4.7 1.5 %collective-permute-start = (bf16[128,1152]{1,0:T(8,128)(2,1)S(1)}, bf16[128,1152]{1,0:T(8,128)(2,1)S(1)}, u32[]{:S(2)}, u32[]{:S(2)}) collective-permute-start(bf16[128,1152]{1,0:T(8,128)(2,1)S(1)} %get-tuple-element.23), channel_id=1, source_target_pairs={{0,8},{8,0},{2,10},{10,2},{4,12},{12,4},{6,14},{14,6},{16,24},{24,... | collective-permute-start | bytes 884744 | tf_op jit(solution)/shard_map/ppermute | solution.py:30
  6.2 1.2 %collective-permute-done = bf16[128,1152]{1,0:T(8,128)(2,1)S(1)} collective-permute-done((bf16[128,1152]{1,0:T(8,128)(2,1)S(1)}, bf16[128,1152]{1,0:T(8,128)(2,1)S(1)}, u32[]{:S(2)}, u32[]{:S(2)}) %collective-permute-start) | collective-permute-done | bytes 294944 | tf_op jit(solution)/shard_map/ppermute | solution.py:30
  7.5 1.8 %collective-permute-start.5 = (bf16[256,1152]{1,0:T(8,128)(2,1)S(1)}, bf16[256,1152]{1,0:T(8,128)(2,1)S(1)}, u32[]{:S(2)}, u32[]{:S(2)}) collective-permute-start(bf16[256,1152]{1,0:T(8,128)(2,1)S(1)} %constant_dynamic-update-slice_fusion.refs_1_.refs_3_), channel_id=1, source_target_pairs={{0,16},{8,10},{2,18},{10,12},{4,20},{12,14},{6,22},{14,8},{16,32},... | collective-permute-start | bytes 1769480 | tf_op jit(solution)/shard_map/ppermute | solution.py:30
  9.3 2.5 %collective-permute-start.3 = (bf16[256,1152]{1,0:T(8,128)(2,1)S(1)}, bf16[256,1152]{1,0:T(8,128)(2,1)S(1)}, u32[]{:S(2)}, u32[]{:S(2)}) collective-permute-start(bf16[256,1152]{1,0:T(8,128)(2,1)S(1)} %constant_dynamic-update-slice_fusion.refs_1_.refs_3_), channel_id=1, source_target_pairs={{0,64},{8,73},{2,66},{10,75},{4,68},{12,77},{6,70},{14,79},{16,80}... | collective-permute-start | bytes 1769480 | tf_op jit(solution)/shard_map/ppermute | solution.py:30
  11.7 2.2 %collective-permute-start.1 = (bf16[256,1152]{1,0:T(8,128)(2,1)S(1)}, bf16[256,1152]{1,0:T(8,128)(2,1)S(1)}, u32[]{:S(2)}, u32[]{:S(2)}) collective-permute-start(bf16[256,1152]{1,0:T(8,128)(2,1)S(1)} %constant_dynamic-update-slice_fusion.refs_1_.refs_3_), channel_id=1, source_target_pairs={{0,48},{8,14},{2,50},{10,8},{4,52},{12,10},{6,54},{14,12},{16,0},{... | collective-permute-start | bytes 1769480 | tf_op jit(solution)/shard_map/ppermute | solution.py:30
  14.0 4.7 %collective-permute-done.5.refs_4_.refs_6_ = bf16[256,1152]{1,0:T(8,128)(2,1)S(1)} collective-permute-done((bf16[256,1152]{1,0:T(8,128)(2,1)S(1)}, bf16[256,1152]{1,0:T(8,128)(2,1)S(1)}, u32[]{:S(2)}, u32[]{:S(2)}) %collective-permute-start.5) | collective-permute-done | bytes 589856 | tf_op jit(solution)/shard_map/ppermute | solution.py:30
  18.6 0.4 collective-permute-start.9
  19.0 0.2 collective-permute-done.3.refs_2_.refs_4_
  19.2 0.3 collective-permute-start.7
  19.5 1.3 %collective-permute-done.1.refs_3_.refs_5_ = bf16[256,1152]{1,0:T(8,128)(2,1)S(1)} collective-permute-done((bf16[256,1152]{1,0:T(8,128)(2,1)S(1)}, bf16[256,1152]{1,0:T(8,128)(2,1)S(1)}, u32[]{:S(2)}, u32[]{:S(2)}) %collective-permute-start.1) | collective-permute-done | bytes 589856 | tf_op jit(solution)/shard_map/ppermute | solution.py:30
  20.8 0.2 collective-permute-start.8
  20.9 1.6 %collective-permute-start.4 = (bf16[256,1152]{1,0:T(8,128)(2,1)S(1)}, bf16[256,1152]{1,0:T(8,128)(2,1)S(1)}, u32[]{:S(2)}, u32[]{:S(2)}) collective-permute-start(bf16[256,1152]{1,0:T(8,128)(2,1)S(1)} %collective-permute-done.3.refs_2_.refs_4_), channel_id=1, source_target_pairs={{0,16},{8,10},{2,18},{10,12},{4,20},{12,14},{6,22},{14,8},{16,32},... | collective-permute-start | bytes 1769480 | tf_op jit(solution)/shard_map/ppermute | solution.py:30
  22.6 2.1 %collective-permute-start.2 = (bf16[256,1152]{1,0:T(8,128)(2,1)S(1)}, bf16[256,1152]{1,0:T(8,128)(2,1)S(1)}, u32[]{:S(2)}, u32[]{:S(2)}) collective-permute-start(bf16[256,1152]{1,0:T(8,128)(2,1)S(1)} %collective-permute-done.1.refs_3_.refs_5_), channel_id=1, source_target_pairs={{0,48},{8,14},{2,50},{10,8},{4,52},{12,10},{6,54},{14,12},{16,0},{... | collective-permute-start | bytes 1769480 | tf_op jit(solution)/shard_map/ppermute | solution.py:30
  24.7 1.8 %collective-permute-start.12 = (bf16[256,1152]{1,0:T(8,128)(2,1)S(1)}, bf16[256,1152]{1,0:T(8,128)(2,1)S(1)}, u32[]{:S(2)}, u32[]{:S(2)}) collective-permute-start(bf16[256,1152]{1,0:T(8,128)(2,1)S(1)} %collective-permute-done.1.refs_3_.refs_5_), channel_id=1, source_target_pairs={{0,64},{8,73},{2,66},{10,75},{4,68},{12,77},{6,70},{14,79},{16,80}... | collective-permute-start | bytes 1769480 | tf_op jit(solution)/shard_map/ppermute | solution.py:30
  26.5 5.8 %near.1.refs_11_ = f32[1024,1152]{1,0:T(8,128)S(1)} custom-call(f32[8,256]{1,0:T(8,128)S(1)} %get-tuple-element.21.refs_0_.refs_1_.refs_2_, bf16[256,1152]{1,0:T(8,128)(2,1)S(1)} %constant_dynamic-update-slice_fusion.refs_1_.refs_3_, bf16[256,1152]{1,0:T(8,128)(2,1)S(1)} %collective-permute-done.3.refs_2_.refs_4_, ...), custom_call_target="tpu_custom_call" | custom-call | flops 75497472 | bytes 110656 | tf_op jit(solution)/shard_map/near/pallas_call | solution.py:46
  32.4 1.0 %collective-permute-start.11 = (bf16[128,1152]{1,0:T(8,128)(2,1)S(1)}, bf16[128,1152]{1,0:T(8,128)(2,1)S(1)}, u32[]{:S(2)}, u32[]{:S(2)}) collective-permute-start(bf16[128,1152]{1,0:T(8,128)(2,1)S(1)} %slice.7), channel_id=1, source_target_pairs={{0,16},{8,10},{2,18},{10,12},{4,20},{12,14},{6,22},{14,8},{16,32},... | collective-permute-start | bytes 884744 | tf_op jit(solution)/shard_map/ppermute | solution.py:30
  33.4 1.8 %collective-permute-start.10 = (bf16[128,1152]{1,0:T(8,128)(2,1)S(1)}, bf16[128,1152]{1,0:T(8,128)(2,1)S(1)}, u32[]{:S(2)}, u32[]{:S(2)}) collective-permute-start(bf16[128,1152]{1,0:T(8,128)(2,1)S(1)} %slice.6), channel_id=1, source_target_pairs={{0,64},{8,73},{2,66},{10,75},{4,68},{12,77},{6,70},{14,79},{16,80}... | collective-permute-start | bytes 884744 | tf_op jit(solution)/shard_map/ppermute | solution.py:30
  35.2 0.5 collective-permute-start.15
  35.7 4.4 %middle.1.refs_9_ = f32[768,1152]{1,0:T(8,128)S(1)} custom-call(f32[8,256]{1,0:T(8,128)S(1)} %get-tuple-element.21.refs_0_.refs_1_.refs_2_, bf16[256,1152]{1,0:T(8,128)(2,1)S(1)} %collective-permute-done.12.refs_1_.refs_2_, bf16[256,1152]{1,0:T(8,128)(2,1)S(1)} %collective-permute-done.4.refs_2_.refs_3_, ...), custom_call_target="tpu_custom_call" | custom-call | flops 56623104 | bytes 92224 | tf_op jit(solution)/shard_map/middle/pallas_call | solution.py:46
  40.1 0.3 collective-permute-done.10.refs_0_
  40.5 0.8 %collective-permute-start.13 = (bf16[256,1152]{1,0:T(8,128)(2,1)S(1)}, bf16[256,1152]{1,0:T(8,128)(2,1)S(1)}, u32[]{:S(2)}, u32[]{:S(2)}) collective-permute-start(bf16[256,1152]{1,0:T(8,128)(2,1)S(1)} %pack.1.refs_1_), channel_id=1, source_target_pairs={{0,8},{8,0},{2,10},{10,2},{4,12},{12,4},{6,14},{14,6},{16,24},{24,... | collective-permute-start | bytes 1769480 | tf_op jit(solution)/shard_map/ppermute | solution.py:30
  41.3 2.6 %last.1.refs_3_ = f32[256,1152]{1,0:T(8,128)S(1)} custom-call(f32[8,256]{1,0:T(8,128)S(1)} %get-tuple-element.21.refs_0_.refs_1_.refs_2_, bf16[256,1152]{1,0:T(8,128)(2,1)S(1)} %pack.1.refs_1_, bf16[256,1152]{1,0:T(8,128)(2,1)S(1)} %collective-permute-done.6.refs_5_.refs_4_.refs_2_, bf16[256,1152]{1,0:T(8,128)(2,1)S(1)} %collective-permute-done.7.refs_6_.refs_5_.refs_3_, ...), custom_call_target="tpu_custom_call" | custom-call | flops 33030144 | bytes 83008 | tf_op jit(solution)/shard_map/last/pallas_call | solution.py:46
  44.0 0.9 %last_rest.1 = (bf16[128,1152]{1,0:T(8,128)(2,1)S(1)}, bf16[128,1152]{1,0:T(8,128)(2,1)S(1)}) custom-call(f32[8,256]{1,0:T(8,128)S(1)} %get-tuple-element.21.refs_0_.refs_1_.refs_2_, bf16[256,1152]{1,0:T(8,128)(2,1)S(1)} %pack.1.refs_1_, bf16[256,1152]{1,0:T(8,128)(2,1)S(1)} %collective-permute-done.13.refs_2_.refs_8_.refs_10_, f32[256,1152]{1,0:T(8,128)S(1)} %last.1.refs_3_), custom_call_target="tpu_custom_call" | custom-call | flops 4718592 | bytes 36928 | tf_op jit(solution)/shard_map/last_rest/pallas_call | solution.py:46
  44.9 1.3 %collective-permute-start.17 = (bf16[128,1152]{1,0:T(8,128)(2,1)S(1)}, bf16[128,1152]{1,0:T(8,128)(2,1)S(1)}, u32[]{:S(2)}, u32[]{:S(2)}) collective-permute-start(bf16[128,1152]{1,0:T(8,128)(2,1)S(1)} %get-tuple-element.29.refs_0_), channel_id=1, source_target_pairs={{0,64},{8,73},{2,66},{10,75},{4,68},{12,77},{6,70},{14,79},{16,80}... | collective-permute-start | bytes 884744 | tf_op jit(solution)/shard_map/ppermute | solution.py:30
  46.2 3.8 %collective-permute-start.18 = (bf16[128,1152]{1,0:T(8,128)(2,1)S(1)}, bf16[128,1152]{1,0:T(8,128)(2,1)S(1)}, u32[]{:S(2)}, u32[]{:S(2)}) collective-permute-start(bf16[128,1152]{1,0:T(8,128)(2,1)S(1)} %get-tuple-element.33), channel_id=1, source_target_pairs={{0,48},{8,14},{2,50},{10,8},{4,52},{12,10},{6,54},{14,12},{16,0},{... | collective-permute-start | bytes 884744 | tf_op jit(solution)/shard_map/ppermute | solution.py:30
  49.9 4.4 %middle_rest.1 = (bf16[256,1152]{1,0:T(8,128)(2,1)S(1)}, bf16[256,1152]{1,0:T(8,128)(2,1)S(1)}, bf16[256,1152]{1,0:T(8,128)(2,1)S(1)}) custom-call(bf16[128,1152]{1,0:T(8,128)(2,1)S(1)} %get-tuple-element.29.refs_0_, f32[8,256]{1,0:T(8,128)S(1)} %get-tuple-element.21.refs_0_.refs_1_.refs_2_, bf16[256,1152]{1,0:T(8,128)(2,1)S(1)} %collective-permute-done.12.refs_1_.refs_2_, ...), custom_call_target="tpu_custom_call" | custom-call | flops 56623104 | bytes 119872 | tf_op jit(solution)/shard_map/middle_rest/pallas_call | solution.py:46
  54.4 0.9 %collective-permute-start.19 = (bf16[256,1152]{1,0:T(8,128)(2,1)S(1)}, bf16[256,1152]{1,0:T(8,128)(2,1)S(1)}, u32[]{:S(2)}, u32[]{:S(2)}) collective-permute-start(bf16[256,1152]{1,0:T(8,128)(2,1)S(1)} %get-tuple-element.37), channel_id=1, source_target_pairs={{0,64},{8,73},{2,66},{10,75},{4,68},{12,77},{6,70},{14,79},{16,80}... | collective-permute-start | bytes 1769480 | tf_op jit(solution)/shard_map/ppermute | solution.py:30
  55.3 0.1 add_half.2.refs_0_
  55.5 0.1 add_half.3.refs_1_
  55.6 2.9 %collective-permute-start.23 = (bf16[256,1152]{1,0:T(8,128)(2,1)S(1)}, bf16[256,1152]{1,0:T(8,128)(2,1)S(1)}, u32[]{:S(2)}, u32[]{:S(2)}) collective-permute-start(bf16[256,1152]{1,0:T(8,128)(2,1)S(1)} %add_half.3.refs_1_), channel_id=1, source_target_pairs={{0,48},{8,14},{2,50},{10,8},{4,52},{12,10},{6,54},{14,12},{16,0},{... | collective-permute-start | bytes 1769480 | tf_op jit(solution)/shard_map/ppermute | solution.py:30
  58.5 5.8 %near_rest.1 = (bf16[256,1152]{1,0:T(8,128)(2,1)S(1)}, bf16[256,1152]{1,0:T(8,128)(2,1)S(1)}, bf16[256,1152]{1,0:T(8,128)(2,1)S(1)}, bf16[256,1152]{1,0:T(8,128)(2,1)S(1)}) custom-call(bf16[256,1152]{1,0:T(8,128)(2,1)S(1)} %add_half.2.refs_0_, bf16[256,1152]{1,0:T(8,128)(2,1)S(1)} %add_half.3.refs_1_, ...), custom_call_target="tpu_custom_call" | custom-call | flops 75497472 | bytes 147520 | tf_op jit(solution)/shard_map/near_rest/pallas_call | solution.py:46
  64.4 0.1 collective-permute-start.22
  64.5 0.2 collective-permute-done.19.refs_1_
  64.7 0.1 add.3.refs_0_
  64.9 0.5 collective-permute-done.23.refs_1_
  65.4 0.1 add.5
  65.5 1.9 %collective-permute-start.24 = (bf16[256,1152]{1,0:T(8,128)(2,1)S(1)}, bf16[256,1152]{1,0:T(8,128)(2,1)S(1)}, u32[]{:S(2)}, u32[]{:S(2)}) collective-permute-start(bf16[256,1152]{1,0:T(8,128)(2,1)S(1)} %add.5), channel_id=1, source_target_pairs={{0,64},{8,73},{2,66},{10,75},{4,68},{12,77},{6,70},{14,79},{16,80}... | collective-permute-start | bytes 1769480 | tf_op jit(solution)/shard_map/ppermute | solution.py:30
  67.4 0.1 add.4
  67.6 0.8 collective-permute-start.21
  68.3 5.1 %collective-permute-done.22.refs_2_.refs_6_ = bf16[256,1152]{1,0:T(8,128)(2,1)S(1)} collective-permute-done((bf16[256,1152]{1,0:T(8,128)(2,1)S(1)}, bf16[256,1152]{1,0:T(8,128)(2,1)S(1)}, u32[]{:S(2)}, u32[]{:S(2)}) %collective-permute-start.22) | collective-permute-done | bytes 589856 | tf_op jit(solution)/shard_map/ppermute | solution.py:30
  73.5 2.4 %collective-permute-done.24.refs_3_.refs_7_ = bf16[256,1152]{1,0:T(8,128)(2,1)S(1)} collective-permute-done((bf16[256,1152]{1,0:T(8,128)(2,1)S(1)}, bf16[256,1152]{1,0:T(8,128)(2,1)S(1)}, u32[]{:S(2)}, u32[]{:S(2)}) %collective-permute-start.24) | collective-permute-done | bytes 589856 | tf_op jit(solution)/shard_map/ppermute | solution.py:30
  75.8 2.2 %collective-permute-done.21.refs_1_.refs_5_ = bf16[256,1152]{1,0:T(8,128)(2,1)S(1)} collective-permute-done((bf16[256,1152]{1,0:T(8,128)(2,1)S(1)}, bf16[256,1152]{1,0:T(8,128)(2,1)S(1)}, u32[]{:S(2)}, u32[]{:S(2)}) %collective-permute-start.21) | collective-permute-done | bytes 589856 | tf_op jit(solution)/shard_map/ppermute | solution.py:30
  78.0 0.1 give.1
  78.3 1.6 %collective-permute-done.25.refs_3_ = bf16[128,1152]{1,0:T(8,128)(2,1)S(1)} collective-permute-done((bf16[128,1152]{1,0:T(8,128)(2,1)S(1)}, bf16[128,1152]{1,0:T(8,128)(2,1)S(1)}, u32[]{:S(2)}, u32[]{:S(2)}) %collective-permute-start.25) | collective-permute-done | bytes 294944 | tf_op jit(solution)/shard_map/ppermute | solution.py:30
  79.8 1.4 %final.1 = (bf16[128,1152]{1,0:T(8,128)(2,1)}, bf16[128,1152]{1,0:T(8,128)(2,1)}) custom-call(s32[1]{0:T(128)} %bitcast.refs_0_, bf16[128,1152]{1,0:T(8,128)(2,1)S(1)} %copy-done.1, bf16[128,1152]{1,0:T(8,128)(2,1)S(1)} %copy-done.3, bf16[128,1152]{1,0:T(8,128)(2,1)S(1)} %collective-permute-done.25.refs_3_, ...), custom_call_target="tpu_custom_call" | custom-call | flops 46080 | bytes 59904 | tf_op jit(solution)/shard_map/final/pallas_call | solution.py:46
  (31 shorter events, 0.4 us)
Async XLA Ops:
  2.6 1.0 %copy-start = (bf16[128,1152]{1,0:T(8,128)(2,1)S(1)}, bf16[128,1152]{1,0:T(8,128)(2,1)}, u32[]{:S(2)}) copy-start(bf16[128,1152]{1,0:T(8,128)(2,1)} %refs_1_.1) | copy-start | bytes 884740
  3.5 1.0 %copy-start.2 = (bf16[128,1152]{1,0:T(8,128)(2,1)S(1)}, bf16[128,1152]{1,0:T(8,128)(2,1)}, u32[]{:S(2)}) copy-start(bf16[128,1152]{1,0:T(8,128)(2,1)} %refs_2_.1) | copy-start | bytes 884740
  4.7 2.7 %collective-permute-start = (bf16[128,1152]{1,0:T(8,128)(2,1)S(1)}, bf16[128,1152]{1,0:T(8,128)(2,1)S(1)}, u32[]{:S(2)}, u32[]{:S(2)}) collective-permute-start(bf16[128,1152]{1,0:T(8,128)(2,1)S(1)} %get-tuple-element.23), channel_id=1, source_target_pairs={{0,8},{8,0},{2,10},{10,2},{4,12},{12,4},{6,14},{14,6},{16,24},{24,... | collective-permute-start | bytes 884744 | tf_op jit(solution)/shard_map/ppermute | solution.py:30
  7.5 11.2 %collective-permute-start.5 = (bf16[256,1152]{1,0:T(8,128)(2,1)S(1)}, bf16[256,1152]{1,0:T(8,128)(2,1)S(1)}, u32[]{:S(2)}, u32[]{:S(2)}) collective-permute-start(bf16[256,1152]{1,0:T(8,128)(2,1)S(1)} %constant_dynamic-update-slice_fusion.refs_1_.refs_3_), channel_id=1, source_target_pairs={{0,16},{8,10},{2,18},{10,12},{4,20},{12,14},{6,22},{14,8},{16,32},... | collective-permute-start | bytes 1769480 | tf_op jit(solution)/shard_map/ppermute | solution.py:30
  9.3 9.9 %collective-permute-start.3 = (bf16[256,1152]{1,0:T(8,128)(2,1)S(1)}, bf16[256,1152]{1,0:T(8,128)(2,1)S(1)}, u32[]{:S(2)}, u32[]{:S(2)}) collective-permute-start(bf16[256,1152]{1,0:T(8,128)(2,1)S(1)} %constant_dynamic-update-slice_fusion.refs_1_.refs_3_), channel_id=1, source_target_pairs={{0,64},{8,73},{2,66},{10,75},{4,68},{12,77},{6,70},{14,79},{16,80}... | collective-permute-start | bytes 1769480 | tf_op jit(solution)/shard_map/ppermute | solution.py:30
  11.7 9.0 %collective-permute-start.1 = (bf16[256,1152]{1,0:T(8,128)(2,1)S(1)}, bf16[256,1152]{1,0:T(8,128)(2,1)S(1)}, u32[]{:S(2)}, u32[]{:S(2)}) collective-permute-start(bf16[256,1152]{1,0:T(8,128)(2,1)S(1)} %constant_dynamic-update-slice_fusion.refs_1_.refs_3_), channel_id=1, source_target_pairs={{0,48},{8,14},{2,50},{10,8},{4,52},{12,10},{6,54},{14,12},{16,0},{... | collective-permute-start | bytes 1769480 | tf_op jit(solution)/shard_map/ppermute | solution.py:30
  13.9 8.6 %collective-permute-start.6 = (bf16[256,1152]{1,0:T(8,128)(2,1)S(1)}, bf16[256,1152]{1,0:T(8,128)(2,1)S(1)}, u32[]{:S(2)}, u32[]{:S(2)}) collective-permute-start(bf16[256,1152]{1,0:T(8,128)(2,1)S(1)} %constant_dynamic-update-slice_fusion.refs_1_.refs_3_), channel_id=1, source_target_pairs={{0,8},{8,0},{2,10},{10,2},{4,12},{12,4},{6,14},{14,6},{16,24},{24,... | collective-permute-start | bytes 1769480 | tf_op jit(solution)/shard_map/ppermute | solution.py:30
  18.6 6.1 %collective-permute-start.9 = (bf16[256,1152]{1,0:T(8,128)(2,1)S(1)}, bf16[256,1152]{1,0:T(8,128)(2,1)S(1)}, u32[]{:S(2)}, u32[]{:S(2)}) collective-permute-start(bf16[256,1152]{1,0:T(8,128)(2,1)S(1)} %collective-permute-done.5.refs_4_.refs_6_), channel_id=1, source_target_pairs={{0,8},{8,0},{2,10},{10,2},{4,12},{12,4},{6,14},{14,6},{16,24},{24,... | collective-permute-start | bytes 1769480 | tf_op jit(solution)/shard_map/ppermute | solution.py:30
  19.2 7.3 %collective-permute-start.7 = (bf16[256,1152]{1,0:T(8,128)(2,1)S(1)}, bf16[256,1152]{1,0:T(8,128)(2,1)S(1)}, u32[]{:S(2)}, u32[]{:S(2)}) collective-permute-start(bf16[256,1152]{1,0:T(8,128)(2,1)S(1)} %collective-permute-done.3.refs_2_.refs_4_), channel_id=1, source_target_pairs={{0,8},{8,0},{2,10},{10,2},{4,12},{12,4},{6,14},{14,6},{16,24},{24,... | collective-permute-start | bytes 1769480 | tf_op jit(solution)/shard_map/ppermute | solution.py:30
  20.8 5.8 %collective-permute-start.8 = (bf16[256,1152]{1,0:T(8,128)(2,1)S(1)}, bf16[256,1152]{1,0:T(8,128)(2,1)S(1)}, u32[]{:S(2)}, u32[]{:S(2)}) collective-permute-start(bf16[256,1152]{1,0:T(8,128)(2,1)S(1)} %collective-permute-done.1.refs_3_.refs_5_), channel_id=1, source_target_pairs={{0,8},{8,0},{2,10},{10,2},{4,12},{12,4},{6,14},{14,6},{16,24},{24,... | collective-permute-start | bytes 1769480 | tf_op jit(solution)/shard_map/ppermute | solution.py:30
  20.9 11.4 %collective-permute-start.4 = (bf16[256,1152]{1,0:T(8,128)(2,1)S(1)}, bf16[256,1152]{1,0:T(8,128)(2,1)S(1)}, u32[]{:S(2)}, u32[]{:S(2)}) collective-permute-start(bf16[256,1152]{1,0:T(8,128)(2,1)S(1)} %collective-permute-done.3.refs_2_.refs_4_), channel_id=1, source_target_pairs={{0,16},{8,10},{2,18},{10,12},{4,20},{12,14},{6,22},{14,8},{16,32},... | collective-permute-start | bytes 1769480 | tf_op jit(solution)/shard_map/ppermute | solution.py:30
  22.6 9.7 %collective-permute-start.2 = (bf16[256,1152]{1,0:T(8,128)(2,1)S(1)}, bf16[256,1152]{1,0:T(8,128)(2,1)S(1)}, u32[]{:S(2)}, u32[]{:S(2)}) collective-permute-start(bf16[256,1152]{1,0:T(8,128)(2,1)S(1)} %collective-permute-done.1.refs_3_.refs_5_), channel_id=1, source_target_pairs={{0,48},{8,14},{2,50},{10,8},{4,52},{12,10},{6,54},{14,12},{16,0},{... | collective-permute-start | bytes 1769480 | tf_op jit(solution)/shard_map/ppermute | solution.py:30
  24.7 11.0 %collective-permute-start.12 = (bf16[256,1152]{1,0:T(8,128)(2,1)S(1)}, bf16[256,1152]{1,0:T(8,128)(2,1)S(1)}, u32[]{:S(2)}, u32[]{:S(2)}) collective-permute-start(bf16[256,1152]{1,0:T(8,128)(2,1)S(1)} %collective-permute-done.1.refs_3_.refs_5_), channel_id=1, source_target_pairs={{0,64},{8,73},{2,66},{10,75},{4,68},{12,77},{6,70},{14,79},{16,80}... | collective-permute-start | bytes 1769480 | tf_op jit(solution)/shard_map/ppermute | solution.py:30
  32.4 7.7 %collective-permute-start.11 = (bf16[128,1152]{1,0:T(8,128)(2,1)S(1)}, bf16[128,1152]{1,0:T(8,128)(2,1)S(1)}, u32[]{:S(2)}, u32[]{:S(2)}) collective-permute-start(bf16[128,1152]{1,0:T(8,128)(2,1)S(1)} %slice.7), channel_id=1, source_target_pairs={{0,16},{8,10},{2,18},{10,12},{4,20},{12,14},{6,22},{14,8},{16,32},... | collective-permute-start | bytes 884744 | tf_op jit(solution)/shard_map/ppermute | solution.py:30
  33.4 7.0 %collective-permute-start.10 = (bf16[128,1152]{1,0:T(8,128)(2,1)S(1)}, bf16[128,1152]{1,0:T(8,128)(2,1)S(1)}, u32[]{:S(2)}, u32[]{:S(2)}) collective-permute-start(bf16[128,1152]{1,0:T(8,128)(2,1)S(1)} %slice.6), channel_id=1, source_target_pairs={{0,64},{8,73},{2,66},{10,75},{4,68},{12,77},{6,70},{14,79},{16,80}... | collective-permute-start | bytes 884744 | tf_op jit(solution)/shard_map/ppermute | solution.py:30
  35.2 6.1 %collective-permute-start.16 = (bf16[256,1152]{1,0:T(8,128)(2,1)S(1)}, bf16[256,1152]{1,0:T(8,128)(2,1)S(1)}, u32[]{:S(2)}, u32[]{:S(2)}) collective-permute-start(bf16[256,1152]{1,0:T(8,128)(2,1)S(1)} %collective-permute-done.2.refs_3_.refs_4_), channel_id=1, source_target_pairs={{0,8},{8,0},{2,10},{10,2},{4,12},{12,4},{6,14},{14,6},{16,24},{24,... | collective-permute-start | bytes 1769480 | tf_op jit(solution)/shard_map/ppermute | solution.py:30
  35.2 6.1 %collective-permute-start.15 = (bf16[256,1152]{1,0:T(8,128)(2,1)S(1)}, bf16[256,1152]{1,0:T(8,128)(2,1)S(1)}, u32[]{:S(2)}, u32[]{:S(2)}) collective-permute-start(bf16[256,1152]{1,0:T(8,128)(2,1)S(1)} %collective-permute-done.4.refs_2_.refs_3_), channel_id=1, source_target_pairs={{0,8},{8,0},{2,10},{10,2},{4,12},{12,4},{6,14},{14,6},{16,24},{24,... | collective-permute-start | bytes 1769480 | tf_op jit(solution)/shard_map/ppermute | solution.py:30
  35.7 5.6 %collective-permute-start.14 = (bf16[256,1152]{1,0:T(8,128)(2,1)S(1)}, bf16[256,1152]{1,0:T(8,128)(2,1)S(1)}, u32[]{:S(2)}, u32[]{:S(2)}) collective-permute-start(bf16[256,1152]{1,0:T(8,128)(2,1)S(1)} %collective-permute-done.12.refs_1_.refs_2_), channel_id=1, source_target_pairs={{0,8},{8,0},{2,10},{10,2},{4,12},{12,4},{6,14},{14,6},{16,24},{24,... | collective-permute-start | bytes 1769480 | tf_op jit(solution)/shard_map/ppermute | solution.py:30
  40.5 3.5 %collective-permute-start.13 = (bf16[256,1152]{1,0:T(8,128)(2,1)S(1)}, bf16[256,1152]{1,0:T(8,128)(2,1)S(1)}, u32[]{:S(2)}, u32[]{:S(2)}) collective-permute-start(bf16[256,1152]{1,0:T(8,128)(2,1)S(1)} %pack.1.refs_1_), channel_id=1, source_target_pairs={{0,8},{8,0},{2,10},{10,2},{4,12},{12,4},{6,14},{14,6},{16,24},{24,... | collective-permute-start | bytes 1769480 | tf_op jit(solution)/shard_map/ppermute | solution.py:30
  44.9 10.4 %collective-permute-start.17 = (bf16[128,1152]{1,0:T(8,128)(2,1)S(1)}, bf16[128,1152]{1,0:T(8,128)(2,1)S(1)}, u32[]{:S(2)}, u32[]{:S(2)}) collective-permute-start(bf16[128,1152]{1,0:T(8,128)(2,1)S(1)} %get-tuple-element.29.refs_0_), channel_id=1, source_target_pairs={{0,64},{8,73},{2,66},{10,75},{4,68},{12,77},{6,70},{14,79},{16,80}... | collective-permute-start | bytes 884744 | tf_op jit(solution)/shard_map/ppermute | solution.py:30
  46.2 9.3 %collective-permute-start.18 = (bf16[128,1152]{1,0:T(8,128)(2,1)S(1)}, bf16[128,1152]{1,0:T(8,128)(2,1)S(1)}, u32[]{:S(2)}, u32[]{:S(2)}) collective-permute-start(bf16[128,1152]{1,0:T(8,128)(2,1)S(1)} %get-tuple-element.33), channel_id=1, source_target_pairs={{0,48},{8,14},{2,50},{10,8},{4,52},{12,10},{6,54},{14,12},{16,0},{... | collective-permute-start | bytes 884744 | tf_op jit(solution)/shard_map/ppermute | solution.py:30
  54.4 10.3 %collective-permute-start.19 = (bf16[256,1152]{1,0:T(8,128)(2,1)S(1)}, bf16[256,1152]{1,0:T(8,128)(2,1)S(1)}, u32[]{:S(2)}, u32[]{:S(2)}) collective-permute-start(bf16[256,1152]{1,0:T(8,128)(2,1)S(1)} %get-tuple-element.37), channel_id=1, source_target_pairs={{0,64},{8,73},{2,66},{10,75},{4,68},{12,77},{6,70},{14,79},{16,80}... | collective-permute-start | bytes 1769480 | tf_op jit(solution)/shard_map/ppermute | solution.py:30
  55.4 12.0 %collective-permute-start.20 = (bf16[256,1152]{1,0:T(8,128)(2,1)S(1)}, bf16[256,1152]{1,0:T(8,128)(2,1)S(1)}, u32[]{:S(2)}, u32[]{:S(2)}) collective-permute-start(bf16[256,1152]{1,0:T(8,128)(2,1)S(1)} %add_half.2.refs_0_), channel_id=1, source_target_pairs={{0,16},{8,10},{2,18},{10,12},{4,20},{12,14},{6,22},{14,8},{16,32},... | collective-permute-start | bytes 1769480 | tf_op jit(solution)/shard_map/ppermute | solution.py:30
  55.6 9.8 %collective-permute-start.23 = (bf16[256,1152]{1,0:T(8,128)(2,1)S(1)}, bf16[256,1152]{1,0:T(8,128)(2,1)S(1)}, u32[]{:S(2)}, u32[]{:S(2)}) collective-permute-start(bf16[256,1152]{1,0:T(8,128)(2,1)S(1)} %add_half.3.refs_1_), channel_id=1, source_target_pairs={{0,48},{8,14},{2,50},{10,8},{4,52},{12,10},{6,54},{14,12},{16,0},{... | collective-permute-start | bytes 1769480 | tf_op jit(solution)/shard_map/ppermute | solution.py:30
  64.4 9.1 %collective-permute-start.22 = (bf16[256,1152]{1,0:T(8,128)(2,1)S(1)}, bf16[256,1152]{1,0:T(8,128)(2,1)S(1)}, u32[]{:S(2)}, u32[]{:S(2)}) collective-permute-start(bf16[256,1152]{1,0:T(8,128)(2,1)S(1)} %get-tuple-element.38), channel_id=1, source_target_pairs={{0,48},{8,14},{2,50},{10,8},{4,52},{12,10},{6,54},{14,12},{16,0},{... | collective-permute-start | bytes 1769480 | tf_op jit(solution)/shard_map/ppermute | solution.py:30
  64.8 15.0 %copy-start.1 = (bf16[128,1152]{1,0:T(8,128)(2,1)S(1)}, bf16[128,1152]{1,0:T(8,128)(2,1)}, u32[]{:S(2)}) copy-start(bf16[128,1152]{1,0:T(8,128)(2,1)} %refs_1_.1) | copy-start | bytes 884740
  64.8 15.0 %copy-start.3 = (bf16[128,1152]{1,0:T(8,128)(2,1)S(1)}, bf16[128,1152]{1,0:T(8,128)(2,1)}, u32[]{:S(2)}) copy-start(bf16[128,1152]{1,0:T(8,128)(2,1)} %refs_2_.1) | copy-start | bytes 884740
  65.5 10.3 %collective-permute-start.24 = (bf16[256,1152]{1,0:T(8,128)(2,1)S(1)}, bf16[256,1152]{1,0:T(8,128)(2,1)S(1)}, u32[]{:S(2)}, u32[]{:S(2)}) collective-permute-start(bf16[256,1152]{1,0:T(8,128)(2,1)S(1)} %add.5), channel_id=1, source_target_pairs={{0,64},{8,73},{2,66},{10,75},{4,68},{12,77},{6,70},{14,79},{16,80}... | collective-permute-start | bytes 1769480 | tf_op jit(solution)/shard_map/ppermute | solution.py:30
  67.6 10.5 %collective-permute-start.21 = (bf16[256,1152]{1,0:T(8,128)(2,1)S(1)}, bf16[256,1152]{1,0:T(8,128)(2,1)S(1)}, u32[]{:S(2)}, u32[]{:S(2)}) collective-permute-start(bf16[256,1152]{1,0:T(8,128)(2,1)S(1)} %add.4), channel_id=1, source_target_pairs={{0,16},{8,10},{2,18},{10,12},{4,20},{12,14},{6,22},{14,8},{16,32},... | collective-permute-start | bytes 1769480 | tf_op jit(solution)/shard_map/ppermute | solution.py:30
  78.2 1.7 %collective-permute-start.25 = (bf16[128,1152]{1,0:T(8,128)(2,1)S(1)}, bf16[128,1152]{1,0:T(8,128)(2,1)S(1)}, u32[]{:S(2)}, u32[]{:S(2)}) collective-permute-start(bf16[128,1152]{1,0:T(8,128)(2,1)S(1)} %give.1), channel_id=1, source_target_pairs={{0,8},{8,0},{2,10},{10,2},{4,12},{12,4},{6,14},{14,6},{16,24},{24,... | collective-permute-start | bytes 884744 | tf_op jit(solution)/shard_map/ppermute | solution.py:30

commit v5 on v4

--- a/solution.py
+++ b/solution.py
@@ -269,8 +269,8 @@
     partner_above, partner_below, far = sums(
         "middle_rest", constants, middle, rest, middle_held, rows_out=2 * rows, after=[last_0]
     )
-    far = add_half(far, to_far, 0, flops=SEND_FLOPS)
     partner_below = add_half(partner_below, to_below, 1, flops=SEND_FLOPS)
+    far = add_half(far, to_far, 0, flops=SEND_FLOPS, after=[partner_below])
     to_above, to_partner, to_above_too = up(far), down(partner_below), cross(partner_above)
     own, partner, above, below = sums(
         "near_rest",

time: 81.4 us -> 81.3 us (level)
  transfers between devices with their start and end apart: 26 -> 26, of which waited for: 11 -> 9; matrix products, arithmetic and copies ran while one was open for 0% -> 0% of each run, Pallas kernels for 29% -> 29%
where the time goes in v5:
time: 81.3 us; the launch traced here: 81.1 us
  starting transfers between devices  30.9 us (38%)
  Pallas kernels  26.4 us (32%)
  waiting for transfers between devices  19 us (23%)
  between operations  2.76 us (3%)
  local copies, waits for them, and re-layouts  2.03 us (2%)
    ppermute x26, starting transfers between devices, sender(): return lambda value: lax.ppermute(value, ('blk', 'grp'), pairs)  30.9 us
    pallas_call x15, Pallas kernels, call(): pl.pallas_call(lambda *refs: body(*refs[len(after):]), name=name, out_sha...  26.4 us
    ppermute x26, waiting for transfers between devices, sender(): return lambda value: lax.ppermute(value, ('blk', 'grp'), pairs)  19 us
    unnamed x9, local copies, waits for them, and re-layouts  1.95 us
  transfers between devices with their start and end apart: 26, of which 9 were waited for; matrix products, arithmetic and copies ran while one was open for 0% of the time, Pallas kernels for 29%

profile of v5, /device:TPU:1, one launch (start us, length us, event | category | flops | bytes accessed | tf_op | source)
XLA Modules:
  0.0 81.1 jit_solution(17195161508180950396)
XLA Ops:
  2.6 1.0 %copy-done = bf16[128,1152]{1,0:T(8,128)(2,1)S(1)} copy-done((bf16[128,1152]{1,0:T(8,128)(2,1)S(1)}, bf16[128,1152]{1,0:T(8,128)(2,1)}, u32[]{:S(2)}) %copy-start) | copy-done | bytes 294936
  3.5 1.0 %copy-done.2 = bf16[128,1152]{1,0:T(8,128)(2,1)S(1)} copy-done((bf16[128,1152]{1,0:T(8,128)(2,1)S(1)}, bf16[128,1152]{1,0:T(8,128)(2,1)}, u32[]{:S(2)}) %copy-start.2) | copy-done | bytes 294936
  4.5 0.2 units.1
  4.7 1.5 %collective-permute-start = (bf16[128,1152]{1,0:T(8,128)(2,1)S(1)}, bf16[128,1152]{1,0:T(8,128)(2,1)S(1)}, u32[]{:S(2)}, u32[]{:S(2)}) collective-permute-start(bf16[128,1152]{1,0:T(8,128)(2,1)S(1)} %get-tuple-element.23), channel_id=1, source_target_pairs={{0,8},{8,0},{2,10},{10,2},{4,12},{12,4},{6,14},{14,6},{16,24},{24,... | collective-permute-start | bytes 884744 | tf_op jit(solution)/shard_map/ppermute | solution.py:30
  6.2 1.2 %collective-permute-done = bf16[128,1152]{1,0:T(8,128)(2,1)S(1)} collective-permute-done((bf16[128,1152]{1,0:T(8,128)(2,1)S(1)}, bf16[128,1152]{1,0:T(8,128)(2,1)S(1)}, u32[]{:S(2)}, u32[]{:S(2)}) %collective-permute-start) | collective-permute-done | bytes 294944 | tf_op jit(solution)/shard_map/ppermute | solution.py:30
  7.5 1.8 %collective-permute-start.5 = (bf16[256,1152]{1,0:T(8,128)(2,1)S(1)}, bf16[256,1152]{1,0:T(8,128)(2,1)S(1)}, u32[]{:S(2)}, u32[]{:S(2)}) collective-permute-start(bf16[256,1152]{1,0:T(8,128)(2,1)S(1)} %constant_dynamic-update-slice_fusion.refs_1_.refs_3_), channel_id=1, source_target_pairs={{0,16},{8,10},{2,18},{10,12},{4,20},{12,14},{6,22},{14,8},{16,32},... | collective-permute-start | bytes 1769480 | tf_op jit(solution)/shard_map/ppermute | solution.py:30
  9.3 2.5 %collective-permute-start.3 = (bf16[256,1152]{1,0:T(8,128)(2,1)S(1)}, bf16[256,1152]{1,0:T(8,128)(2,1)S(1)}, u32[]{:S(2)}, u32[]{:S(2)}) collective-permute-start(bf16[256,1152]{1,0:T(8,128)(2,1)S(1)} %constant_dynamic-update-slice_fusion.refs_1_.refs_3_), channel_id=1, source_target_pairs={{0,64},{8,73},{2,66},{10,75},{4,68},{12,77},{6,70},{14,79},{16,80}... | collective-permute-start | bytes 1769480 | tf_op jit(solution)/shard_map/ppermute | solution.py:30
  11.7 2.2 %collective-permute-start.1 = (bf16[256,1152]{1,0:T(8,128)(2,1)S(1)}, bf16[256,1152]{1,0:T(8,128)(2,1)S(1)}, u32[]{:S(2)}, u32[]{:S(2)}) collective-permute-start(bf16[256,1152]{1,0:T(8,128)(2,1)S(1)} %constant_dynamic-update-slice_fusion.refs_1_.refs_3_), channel_id=1, source_target_pairs={{0,48},{8,14},{2,50},{10,8},{4,52},{12,10},{6,54},{14,12},{16,0},{... | collective-permute-start | bytes 1769480 | tf_op jit(solution)/shard_map/ppermute | solution.py:30
  14.0 4.7 %collective-permute-done.5.refs_4_.refs_6_ = bf16[256,1152]{1,0:T(8,128)(2,1)S(1)} collective-permute-done((bf16[256,1152]{1,0:T(8,128)(2,1)S(1)}, bf16[256,1152]{1,0:T(8,128)(2,1)S(1)}, u32[]{:S(2)}, u32[]{:S(2)}) %collective-permute-start.5) | collective-permute-done | bytes 589856 | tf_op jit(solution)/shard_map/ppermute | solution.py:30
  18.6 0.4 collective-permute-start.9
  19.0 0.2 collective-permute-done.3.refs_2_.refs_4_
  19.2 0.3 collective-permute-start.7
  19.5 1.3 %collective-permute-done.1.refs_3_.refs_5_ = bf16[256,1152]{1,0:T(8,128)(2,1)S(1)} collective-permute-done((bf16[256,1152]{1,0:T(8,128)(2,1)S(1)}, bf16[256,1152]{1,0:T(8,128)(2,1)S(1)}, u32[]{:S(2)}, u32[]{:S(2)}) %collective-permute-start.1) | collective-permute-done | bytes 589856 | tf_op jit(solution)/shard_map/ppermute | solution.py:30
  20.8 0.2 collective-permute-start.8
  20.9 1.6 %collective-permute-start.4 = (bf16[256,1152]{1,0:T(8,128)(2,1)S(1)}, bf16[256,1152]{1,0:T(8,128)(2,1)S(1)}, u32[]{:S(2)}, u32[]{:S(2)}) collective-permute-start(bf16[256,1152]{1,0:T(8,128)(2,1)S(1)} %collective-permute-done.3.refs_2_.refs_4_), channel_id=1, source_target_pairs={{0,16},{8,10},{2,18},{10,12},{4,20},{12,14},{6,22},{14,8},{16,32},... | collective-permute-start | bytes 1769480 | tf_op jit(solution)/shard_map/ppermute | solution.py:30
  22.6 2.1 %collective-permute-start.2 = (bf16[256,1152]{1,0:T(8,128)(2,1)S(1)}, bf16[256,1152]{1,0:T(8,128)(2,1)S(1)}, u32[]{:S(2)}, u32[]{:S(2)}) collective-permute-start(bf16[256,1152]{1,0:T(8,128)(2,1)S(1)} %collective-permute-done.1.refs_3_.refs_5_), channel_id=1, source_target_pairs={{0,48},{8,14},{2,50},{10,8},{4,52},{12,10},{6,54},{14,12},{16,0},{... | collective-permute-start | bytes 1769480 | tf_op jit(solution)/shard_map/ppermute | solution.py:30
  24.7 1.8 %collective-permute-start.12 = (bf16[256,1152]{1,0:T(8,128)(2,1)S(1)}, bf16[256,1152]{1,0:T(8,128)(2,1)S(1)}, u32[]{:S(2)}, u32[]{:S(2)}) collective-permute-start(bf16[256,1152]{1,0:T(8,128)(2,1)S(1)} %collective-permute-done.1.refs_3_.refs_5_), channel_id=1, source_target_pairs={{0,64},{8,73},{2,66},{10,75},{4,68},{12,77},{6,70},{14,79},{16,80}... | collective-permute-start | bytes 1769480 | tf_op jit(solution)/shard_map/ppermute | solution.py:30
  26.5 5.8 %near.1.refs_11_ = f32[1024,1152]{1,0:T(8,128)S(1)} custom-call(f32[8,256]{1,0:T(8,128)S(1)} %get-tuple-element.21.refs_0_.refs_1_.refs_2_, bf16[256,1152]{1,0:T(8,128)(2,1)S(1)} %constant_dynamic-update-slice_fusion.refs_1_.refs_3_, bf16[256,1152]{1,0:T(8,128)(2,1)S(1)} %collective-permute-done.3.refs_2_.refs_4_, ...), custom_call_target="tpu_custom_call" | custom-call | flops 75497472 | bytes 110656 | tf_op jit(solution)/shard_map/near/pallas_call | solution.py:46
  32.4 1.0 %collective-permute-start.11 = (bf16[128,1152]{1,0:T(8,128)(2,1)S(1)}, bf16[128,1152]{1,0:T(8,128)(2,1)S(1)}, u32[]{:S(2)}, u32[]{:S(2)}) collective-permute-start(bf16[128,1152]{1,0:T(8,128)(2,1)S(1)} %slice.7), channel_id=1, source_target_pairs={{0,16},{8,10},{2,18},{10,12},{4,20},{12,14},{6,22},{14,8},{16,32},... | collective-permute-start | bytes 884744 | tf_op jit(solution)/shard_map/ppermute | solution.py:30
  33.4 1.8 %collective-permute-start.10 = (bf16[128,1152]{1,0:T(8,128)(2,1)S(1)}, bf16[128,1152]{1,0:T(8,128)(2,1)S(1)}, u32[]{:S(2)}, u32[]{:S(2)}) collective-permute-start(bf16[128,1152]{1,0:T(8,128)(2,1)S(1)} %slice.6), channel_id=1, source_target_pairs={{0,64},{8,73},{2,66},{10,75},{4,68},{12,77},{6,70},{14,79},{16,80}... | collective-permute-start | bytes 884744 | tf_op jit(solution)/shard_map/ppermute | solution.py:30
  35.2 0.5 collective-permute-start.15
  35.7 4.4 %middle.1.refs_9_ = f32[768,1152]{1,0:T(8,128)S(1)} custom-call(f32[8,256]{1,0:T(8,128)S(1)} %get-tuple-element.21.refs_0_.refs_1_.refs_2_, bf16[256,1152]{1,0:T(8,128)(2,1)S(1)} %collective-permute-done.12.refs_1_.refs_2_, bf16[256,1152]{1,0:T(8,128)(2,1)S(1)} %collective-permute-done.4.refs_2_.refs_3_, ...), custom_call_target="tpu_custom_call" | custom-call | flops 56623104 | bytes 92224 | tf_op jit(solution)/shard_map/middle/pallas_call | solution.py:46
  40.1 0.3 collective-permute-done.10.refs_0_
  40.5 0.8 %collective-permute-start.13 = (bf16[256,1152]{1,0:T(8,128)(2,1)S(1)}, bf16[256,1152]{1,0:T(8,128)(2,1)S(1)}, u32[]{:S(2)}, u32[]{:S(2)}) collective-permute-start(bf16[256,1152]{1,0:T(8,128)(2,1)S(1)} %pack.1.refs_1_), channel_id=1, source_target_pairs={{0,8},{8,0},{2,10},{10,2},{4,12},{12,4},{6,14},{14,6},{16,24},{24,... | collective-permute-start | bytes 1769480 | tf_op jit(solution)/shard_map/ppermute | solution.py:30
  41.3 2.6 %last.1.refs_3_ = f32[256,1152]{1,0:T(8,128)S(1)} custom-call(f32[8,256]{1,0:T(8,128)S(1)} %get-tuple-element.21.refs_0_.refs_1_.refs_2_, bf16[256,1152]{1,0:T(8,128)(2,1)S(1)} %pack.1.refs_1_, bf16[256,1152]{1,0:T(8,128)(2,1)S(1)} %collective-permute-done.6.refs_5_.refs_4_.refs_2_, bf16[256,1152]{1,0:T(8,128)(2,1)S(1)} %collective-permute-done.7.refs_6_.refs_5_.refs_3_, ...), custom_call_target="tpu_custom_call" | custom-call | flops 33030144 | bytes 83008 | tf_op jit(solution)/shard_map/last/pallas_call | solution.py:46
  44.0 0.9 %last_rest.1 = (bf16[128,1152]{1,0:T(8,128)(2,1)S(1)}, bf16[128,1152]{1,0:T(8,128)(2,1)S(1)}) custom-call(f32[8,256]{1,0:T(8,128)S(1)} %get-tuple-element.21.refs_0_.refs_1_.refs_2_, bf16[256,1152]{1,0:T(8,128)(2,1)S(1)} %pack.1.refs_1_, bf16[256,1152]{1,0:T(8,128)(2,1)S(1)} %collective-permute-done.13.refs_2_.refs_8_.refs_10_, f32[256,1152]{1,0:T(8,128)S(1)} %last.1.refs_3_), custom_call_target="tpu_custom_call" | custom-call | flops 4718592 | bytes 36928 | tf_op jit(solution)/shard_map/last_rest/pallas_call | solution.py:46
  44.9 3.2 %collective-permute-start.17 = (bf16[128,1152]{1,0:T(8,128)(2,1)S(1)}, bf16[128,1152]{1,0:T(8,128)(2,1)S(1)}, u32[]{:S(2)}, u32[]{:S(2)}) collective-permute-start(bf16[128,1152]{1,0:T(8,128)(2,1)S(1)} %get-tuple-element.32), channel_id=1, source_target_pairs={{0,48},{8,14},{2,50},{10,8},{4,52},{12,10},{6,54},{14,12},{16,0},{... | collective-permute-start | bytes 884744 | tf_op jit(solution)/shard_map/ppermute | solution.py:30
  48.1 1.8 %collective-permute-start.18 = (bf16[128,1152]{1,0:T(8,128)(2,1)S(1)}, bf16[128,1152]{1,0:T(8,128)(2,1)S(1)}, u32[]{:S(2)}, u32[]{:S(2)}) collective-permute-start(bf16[128,1152]{1,0:T(8,128)(2,1)S(1)} %get-tuple-element.29.refs_0_), channel_id=1, source_target_pairs={{0,64},{8,73},{2,66},{10,75},{4,68},{12,77},{6,70},{14,79},{16,80}... | collective-permute-start | bytes 884744 | tf_op jit(solution)/shard_map/ppermute | solution.py:30
  49.9 4.4 %middle_rest.1 = (bf16[256,1152]{1,0:T(8,128)(2,1)S(1)}, bf16[256,1152]{1,0:T(8,128)(2,1)S(1)}, bf16[256,1152]{1,0:T(8,128)(2,1)S(1)}) custom-call(bf16[128,1152]{1,0:T(8,128)(2,1)S(1)} %get-tuple-element.29.refs_0_, f32[8,256]{1,0:T(8,128)S(1)} %get-tuple-element.21.refs_0_.refs_1_.refs_2_, bf16[256,1152]{1,0:T(8,128)(2,1)S(1)} %collective-permute-done.12.refs_1_.refs_2_, ...), custom_call_target="tpu_custom_call" | custom-call | flops 56623104 | bytes 119872 | tf_op jit(solution)/shard_map/middle_rest/pallas_call | solution.py:46
  54.4 0.9 %collective-permute-start.19 = (bf16[256,1152]{1,0:T(8,128)(2,1)S(1)}, bf16[256,1152]{1,0:T(8,128)(2,1)S(1)}, u32[]{:S(2)}, u32[]{:S(2)}) collective-permute-start(bf16[256,1152]{1,0:T(8,128)(2,1)S(1)} %get-tuple-element.37), channel_id=1, source_target_pairs={{0,64},{8,73},{2,66},{10,75},{4,68},{12,77},{6,70},{14,79},{16,80}... | collective-permute-start | bytes 1769480 | tf_op jit(solution)/shard_map/ppermute | solution.py:30
  55.3 0.1 add_half.2.refs_0_.refs_1_
  55.4 0.3 collective-permute-start.23
  55.7 0.1 add_half.3.refs_0_
  55.8 1.5 %collective-permute-start.20 = (bf16[256,1152]{1,0:T(8,128)(2,1)S(1)}, bf16[256,1152]{1,0:T(8,128)(2,1)S(1)}, u32[]{:S(2)}, u32[]{:S(2)}) collective-permute-start(bf16[256,1152]{1,0:T(8,128)(2,1)S(1)} %add_half.3.refs_0_), channel_id=1, source_target_pairs={{0,16},{8,10},{2,18},{10,12},{4,20},{12,14},{6,22},{14,8},{16,32},... | collective-permute-start | bytes 1769480 | tf_op jit(solution)/shard_map/ppermute | solution.py:30
  57.3 5.8 %near_rest.1 = (bf16[256,1152]{1,0:T(8,128)(2,1)S(1)}, bf16[256,1152]{1,0:T(8,128)(2,1)S(1)}, bf16[256,1152]{1,0:T(8,128)(2,1)S(1)}, bf16[256,1152]{1,0:T(8,128)(2,1)S(1)}) custom-call(bf16[256,1152]{1,0:T(8,128)(2,1)S(1)} %add_half.3.refs_0_, bf16[256,1152]{1,0:T(8,128)(2,1)S(1)} %add_half.2.refs_0_.refs_1_, ...), custom_call_target="tpu_custom_call" | custom-call | flops 75497472 | bytes 147520 | tf_op jit(solution)/shard_map/near_rest/pallas_call | solution.py:46
  63.1 1.5 %collective-permute-start.22 = (bf16[256,1152]{1,0:T(8,128)(2,1)S(1)}, bf16[256,1152]{1,0:T(8,128)(2,1)S(1)}, u32[]{:S(2)}, u32[]{:S(2)}) collective-permute-start(bf16[256,1152]{1,0:T(8,128)(2,1)S(1)} %get-tuple-element.38), channel_id=1, source_target_pairs={{0,48},{8,14},{2,50},{10,8},{4,52},{12,10},{6,54},{14,12},{16,0},{... | collective-permute-start | bytes 1769480 | tf_op jit(solution)/shard_map/ppermute | solution.py:30
  64.7 0.1 add.3.refs_0_
  64.9 0.1 add.5
  65.0 1.8 %collective-permute-start.24 = (bf16[256,1152]{1,0:T(8,128)(2,1)S(1)}, bf16[256,1152]{1,0:T(8,128)(2,1)S(1)}, u32[]{:S(2)}, u32[]{:S(2)}) collective-permute-start(bf16[256,1152]{1,0:T(8,128)(2,1)S(1)} %add.5), channel_id=1, source_target_pairs={{0,64},{8,73},{2,66},{10,75},{4,68},{12,77},{6,70},{14,79},{16,80}... | collective-permute-start | bytes 1769480 | tf_op jit(solution)/shard_map/ppermute | solution.py:30
  66.8 0.1 add.4
  66.9 0.2 collective-permute-start.21
  67.1 5.1 %collective-permute-done.22.refs_2_.refs_6_ = bf16[256,1152]{1,0:T(8,128)(2,1)S(1)} collective-permute-done((bf16[256,1152]{1,0:T(8,128)(2,1)S(1)}, bf16[256,1152]{1,0:T(8,128)(2,1)S(1)}, u32[]{:S(2)}, u32[]{:S(2)}) %collective-permute-start.22) | collective-permute-done | bytes 589856 | tf_op jit(solution)/shard_map/ppermute | solution.py:30
  72.2 3.1 %collective-permute-done.24.refs_3_.refs_7_ = bf16[256,1152]{1,0:T(8,128)(2,1)S(1)} collective-permute-done((bf16[256,1152]{1,0:T(8,128)(2,1)S(1)}, bf16[256,1152]{1,0:T(8,128)(2,1)S(1)}, u32[]{:S(2)}, u32[]{:S(2)}) %collective-permute-start.24) | collective-permute-done | bytes 589856 | tf_op jit(solution)/shard_map/ppermute | solution.py:30
  75.3 1.9 %collective-permute-done.21.refs_1_.refs_5_ = bf16[256,1152]{1,0:T(8,128)(2,1)S(1)} collective-permute-done((bf16[256,1152]{1,0:T(8,128)(2,1)S(1)}, bf16[256,1152]{1,0:T(8,128)(2,1)S(1)}, u32[]{:S(2)}, u32[]{:S(2)}) %collective-permute-start.21) | collective-permute-done | bytes 589856 | tf_op jit(solution)/shard_map/ppermute | solution.py:30
  77.2 0.1 give.1
  77.4 1.1 %collective-permute-start.25 = (bf16[128,1152]{1,0:T(8,128)(2,1)S(1)}, bf16[128,1152]{1,0:T(8,128)(2,1)S(1)}, u32[]{:S(2)}, u32[]{:S(2)}) collective-permute-start(bf16[128,1152]{1,0:T(8,128)(2,1)S(1)} %give.1), channel_id=1, source_target_pairs={{0,8},{8,0},{2,10},{10,2},{4,12},{12,4},{6,14},{14,6},{16,24},{24,... | collective-permute-start | bytes 884744 | tf_op jit(solution)/shard_map/ppermute | solution.py:30
  78.5 1.2 %collective-permute-done.25.refs_3_ = bf16[128,1152]{1,0:T(8,128)(2,1)S(1)} collective-permute-done((bf16[128,1152]{1,0:T(8,128)(2,1)S(1)}, bf16[128,1152]{1,0:T(8,128)(2,1)S(1)}, u32[]{:S(2)}, u32[]{:S(2)}) %collective-permute-start.25) | collective-permute-done | bytes 294944 | tf_op jit(solution)/shard_map/ppermute | solution.py:30
  79.7 1.4 %final.1 = (bf16[128,1152]{1,0:T(8,128)(2,1)}, bf16[128,1152]{1,0:T(8,128)(2,1)}) custom-call(s32[1]{0:T(128)} %bitcast.refs_0_, bf16[128,1152]{1,0:T(8,128)(2,1)S(1)} %copy-done.1, bf16[128,1152]{1,0:T(8,128)(2,1)S(1)} %copy-done.3, bf16[128,1152]{1,0:T(8,128)(2,1)S(1)} %collective-permute-done.25.refs_3_, ...), custom_call_target="tpu_custom_call" | custom-call | flops 46080 | bytes 59904 | tf_op jit(solution)/shard_map/final/pallas_call | solution.py:46
  (31 shorter events, 0.2 us)
Async XLA Ops:
  2.6 1.0 %copy-start = (bf16[128,1152]{1,0:T(8,128)(2,1)S(1)}, bf16[128,1152]{1,0:T(8,128)(2,1)}, u32[]{:S(2)}) copy-start(bf16[128,1152]{1,0:T(8,128)(2,1)} %refs_1_.1) | copy-start | bytes 884740
  3.5 1.0 %copy-start.2 = (bf16[128,1152]{1,0:T(8,128)(2,1)S(1)}, bf16[128,1152]{1,0:T(8,128)(2,1)}, u32[]{:S(2)}) copy-start(bf16[128,1152]{1,0:T(8,128)(2,1)} %refs_2_.1) | copy-start | bytes 884740
  4.7 2.7 %collective-permute-start = (bf16[128,1152]{1,0:T(8,128)(2,1)S(1)}, bf16[128,1152]{1,0:T(8,128)(2,1)S(1)}, u32[]{:S(2)}, u32[]{:S(2)}) collective-permute-start(bf16[128,1152]{1,0:T(8,128)(2,1)S(1)} %get-tuple-element.23), channel_id=1, source_target_pairs={{0,8},{8,0},{2,10},{10,2},{4,12},{12,4},{6,14},{14,6},{16,24},{24,... | collective-permute-start | bytes 884744 | tf_op jit(solution)/shard_map/ppermute | solution.py:30
  7.5 11.2 %collective-permute-start.5 = (bf16[256,1152]{1,0:T(8,128)(2,1)S(1)}, bf16[256,1152]{1,0:T(8,128)(2,1)S(1)}, u32[]{:S(2)}, u32[]{:S(2)}) collective-permute-start(bf16[256,1152]{1,0:T(8,128)(2,1)S(1)} %constant_dynamic-update-slice_fusion.refs_1_.refs_3_), channel_id=1, source_target_pairs={{0,16},{8,10},{2,18},{10,12},{4,20},{12,14},{6,22},{14,8},{16,32},... | collective-permute-start | bytes 1769480 | tf_op jit(solution)/shard_map/ppermute | solution.py:30
  9.3 9.9 %collective-permute-start.3 = (bf16[256,1152]{1,0:T(8,128)(2,1)S(1)}, bf16[256,1152]{1,0:T(8,128)(2,1)S(1)}, u32[]{:S(2)}, u32[]{:S(2)}) collective-permute-start(bf16[256,1152]{1,0:T(8,128)(2,1)S(1)} %constant_dynamic-update-slice_fusion.refs_1_.refs_3_), channel_id=1, source_target_pairs={{0,64},{8,73},{2,66},{10,75},{4,68},{12,77},{6,70},{14,79},{16,80}... | collective-permute-start | bytes 1769480 | tf_op jit(solution)/shard_map/ppermute | solution.py:30
  11.7 9.0 %collective-permute-start.1 = (bf16[256,1152]{1,0:T(8,128)(2,1)S(1)}, bf16[256,1152]{1,0:T(8,128)(2,1)S(1)}, u32[]{:S(2)}, u32[]{:S(2)}) collective-permute-start(bf16[256,1152]{1,0:T(8,128)(2,1)S(1)} %constant_dynamic-update-slice_fusion.refs_1_.refs_3_), channel_id=1, source_target_pairs={{0,48},{8,14},{2,50},{10,8},{4,52},{12,10},{6,54},{14,12},{16,0},{... | collective-permute-start | bytes 1769480 | tf_op jit(solution)/shard_map/ppermute | solution.py:30
  13.9 8.6 %collective-permute-start.6 = (bf16[256,1152]{1,0:T(8,128)(2,1)S(1)}, bf16[256,1152]{1,0:T(8,128)(2,1)S(1)}, u32[]{:S(2)}, u32[]{:S(2)}) collective-permute-start(bf16[256,1152]{1,0:T(8,128)(2,1)S(1)} %constant_dynamic-update-slice_fusion.refs_1_.refs_3_), channel_id=1, source_target_pairs={{0,8},{8,0},{2,10},{10,2},{4,12},{12,4},{6,14},{14,6},{16,24},{24,... | collective-permute-start | bytes 1769480 | tf_op jit(solution)/shard_map/ppermute | solution.py:30
  18.6 6.1 %collective-permute-start.9 = (bf16[256,1152]{1,0:T(8,128)(2,1)S(1)}, bf16[256,1152]{1,0:T(8,128)(2,1)S(1)}, u32[]{:S(2)}, u32[]{:S(2)}) collective-permute-start(bf16[256,1152]{1,0:T(8,128)(2,1)S(1)} %collective-permute-done.5.refs_4_.refs_6_), channel_id=1, source_target_pairs={{0,8},{8,0},{2,10},{10,2},{4,12},{12,4},{6,14},{14,6},{16,24},{24,... | collective-permute-start | bytes 1769480 | tf_op jit(solution)/shard_map/ppermute | solution.py:30
  19.2 7.3 %collective-permute-start.7 = (bf16[256,1152]{1,0:T(8,128)(2,1)S(1)}, bf16[256,1152]{1,0:T(8,128)(2,1)S(1)}, u32[]{:S(2)}, u32[]{:S(2)}) collective-permute-start(bf16[256,1152]{1,0:T(8,128)(2,1)S(1)} %collective-permute-done.3.refs_2_.refs_4_), channel_id=1, source_target_pairs={{0,8},{8,0},{2,10},{10,2},{4,12},{12,4},{6,14},{14,6},{16,24},{24,... | collective-permute-start | bytes 1769480 | tf_op jit(solution)/shard_map/ppermute | solution.py:30
  20.8 5.8 %collective-permute-start.8 = (bf16[256,1152]{1,0:T(8,128)(2,1)S(1)}, bf16[256,1152]{1,0:T(8,128)(2,1)S(1)}, u32[]{:S(2)}, u32[]{:S(2)}) collective-permute-start(bf16[256,1152]{1,0:T(8,128)(2,1)S(1)} %collective-permute-done.1.refs_3_.refs_5_), channel_id=1, source_target_pairs={{0,8},{8,0},{2,10},{10,2},{4,12},{12,4},{6,14},{14,6},{16,24},{24,... | collective-permute-start | bytes 1769480 | tf_op jit(solution)/shard_map/ppermute | solution.py:30
  20.9 11.4 %collective-permute-start.4 = (bf16[256,1152]{1,0:T(8,128)(2,1)S(1)}, bf16[256,1152]{1,0:T(8,128)(2,1)S(1)}, u32[]{:S(2)}, u32[]{:S(2)}) collective-permute-start(bf16[256,1152]{1,0:T(8,128)(2,1)S(1)} %collective-permute-done.3.refs_2_.refs_4_), channel_id=1, source_target_pairs={{0,16},{8,10},{2,18},{10,12},{4,20},{12,14},{6,22},{14,8},{16,32},... | collective-permute-start | bytes 1769480 | tf_op jit(solution)/shard_map/ppermute | solution.py:30
  22.6 9.7 %collective-permute-start.2 = (bf16[256,1152]{1,0:T(8,128)(2,1)S(1)}, bf16[256,1152]{1,0:T(8,128)(2,1)S(1)}, u32[]{:S(2)}, u32[]{:S(2)}) collective-permute-start(bf16[256,1152]{1,0:T(8,128)(2,1)S(1)} %collective-permute-done.1.refs_3_.refs_5_), channel_id=1, source_target_pairs={{0,48},{8,14},{2,50},{10,8},{4,52},{12,10},{6,54},{14,12},{16,0},{... | collective-permute-start | bytes 1769480 | tf_op jit(solution)/shard_map/ppermute | solution.py:30
  24.7 11.0 %collective-permute-start.12 = (bf16[256,1152]{1,0:T(8,128)(2,1)S(1)}, bf16[256,1152]{1,0:T(8,128)(2,1)S(1)}, u32[]{:S(2)}, u32[]{:S(2)}) collective-permute-start(bf16[256,1152]{1,0:T(8,128)(2,1)S(1)} %collective-permute-done.1.refs_3_.refs_5_), channel_id=1, source_target_pairs={{0,64},{8,73},{2,66},{10,75},{4,68},{12,77},{6,70},{14,79},{16,80}... | collective-permute-start | bytes 1769480 | tf_op jit(solution)/shard_map/ppermute | solution.py:30
  32.4 7.7 %collective-permute-start.11 = (bf16[128,1152]{1,0:T(8,128)(2,1)S(1)}, bf16[128,1152]{1,0:T(8,128)(2,1)S(1)}, u32[]{:S(2)}, u32[]{:S(2)}) collective-permute-start(bf16[128,1152]{1,0:T(8,128)(2,1)S(1)} %slice.7), channel_id=1, source_target_pairs={{0,16},{8,10},{2,18},{10,12},{4,20},{12,14},{6,22},{14,8},{16,32},... | collective-permute-start | bytes 884744 | tf_op jit(solution)/shard_map/ppermute | solution.py:30
  33.4 7.0 %collective-permute-start.10 = (bf16[128,1152]{1,0:T(8,128)(2,1)S(1)}, bf16[128,1152]{1,0:T(8,128)(2,1)S(1)}, u32[]{:S(2)}, u32[]{:S(2)}) collective-permute-start(bf16[128,1152]{1,0:T(8,128)(2,1)S(1)} %slice.6), channel_id=1, source_target_pairs={{0,64},{8,73},{2,66},{10,75},{4,68},{12,77},{6,70},{14,79},{16,80}... | collective-permute-start | bytes 884744 | tf_op jit(solution)/shard_map/ppermute | solution.py:30
  35.2 6.1 %collective-permute-start.16 = (bf16[256,1152]{1,0:T(8,128)(2,1)S(1)}, bf16[256,1152]{1,0:T(8,128)(2,1)S(1)}, u32[]{:S(2)}, u32[]{:S(2)}) collective-permute-start(bf16[256,1152]{1,0:T(8,128)(2,1)S(1)} %collective-permute-done.2.refs_3_.refs_4_), channel_id=1, source_target_pairs={{0,8},{8,0},{2,10},{10,2},{4,12},{12,4},{6,14},{14,6},{16,24},{24,... | collective-permute-start | bytes 1769480 | tf_op jit(solution)/shard_map/ppermute | solution.py:30
  35.2 6.1 %collective-permute-start.15 = (bf16[256,1152]{1,0:T(8,128)(2,1)S(1)}, bf16[256,1152]{1,0:T(8,128)(2,1)S(1)}, u32[]{:S(2)}, u32[]{:S(2)}) collective-permute-start(bf16[256,1152]{1,0:T(8,128)(2,1)S(1)} %collective-permute-done.4.refs_2_.refs_3_), channel_id=1, source_target_pairs={{0,8},{8,0},{2,10},{10,2},{4,12},{12,4},{6,14},{14,6},{16,24},{24,... | collective-permute-start | bytes 1769480 | tf_op jit(solution)/shard_map/ppermute | solution.py:30
  35.7 5.6 %collective-permute-start.14 = (bf16[256,1152]{1,0:T(8,128)(2,1)S(1)}, bf16[256,1152]{1,0:T(8,128)(2,1)S(1)}, u32[]{:S(2)}, u32[]{:S(2)}) collective-permute-start(bf16[256,1152]{1,0:T(8,128)(2,1)S(1)} %collective-permute-done.12.refs_1_.refs_2_), channel_id=1, source_target_pairs={{0,8},{8,0},{2,10},{10,2},{4,12},{12,4},{6,14},{14,6},{16,24},{24,... | collective-permute-start | bytes 1769480 | tf_op jit(solution)/shard_map/ppermute | solution.py:30
  40.5 3.5 %collective-permute-start.13 = (bf16[256,1152]{1,0:T(8,128)(2,1)S(1)}, bf16[256,1152]{1,0:T(8,128)(2,1)S(1)}, u32[]{:S(2)}, u32[]{:S(2)}) collective-permute-start(bf16[256,1152]{1,0:T(8,128)(2,1)S(1)} %pack.1.refs_1_), channel_id=1, source_target_pairs={{0,8},{8,0},{2,10},{10,2},{4,12},{12,4},{6,14},{14,6},{16,24},{24,... | collective-permute-start | bytes 1769480 | tf_op jit(solution)/shard_map/ppermute | solution.py:30
  44.9 10.4 %collective-permute-start.17 = (bf16[128,1152]{1,0:T(8,128)(2,1)S(1)}, bf16[128,1152]{1,0:T(8,128)(2,1)S(1)}, u32[]{:S(2)}, u32[]{:S(2)}) collective-permute-start(bf16[128,1152]{1,0:T(8,128)(2,1)S(1)} %get-tuple-element.32), channel_id=1, source_target_pairs={{0,48},{8,14},{2,50},{10,8},{4,52},{12,10},{6,54},{14,12},{16,0},{... | collective-permute-start | bytes 884744 | tf_op jit(solution)/shard_map/ppermute | solution.py:30
  48.1 7.6 %collective-permute-start.18 = (bf16[128,1152]{1,0:T(8,128)(2,1)S(1)}, bf16[128,1152]{1,0:T(8,128)(2,1)S(1)}, u32[]{:S(2)}, u32[]{:S(2)}) collective-permute-start(bf16[128,1152]{1,0:T(8,128)(2,1)S(1)} %get-tuple-element.29.refs_0_), channel_id=1, source_target_pairs={{0,64},{8,73},{2,66},{10,75},{4,68},{12,77},{6,70},{14,79},{16,80}... | collective-permute-start | bytes 884744 | tf_op jit(solution)/shard_map/ppermute | solution.py:30
  54.4 10.3 %collective-permute-start.19 = (bf16[256,1152]{1,0:T(8,128)(2,1)S(1)}, bf16[256,1152]{1,0:T(8,128)(2,1)S(1)}, u32[]{:S(2)}, u32[]{:S(2)}) collective-permute-start(bf16[256,1152]{1,0:T(8,128)(2,1)S(1)} %get-tuple-element.37), channel_id=1, source_target_pairs={{0,64},{8,73},{2,66},{10,75},{4,68},{12,77},{6,70},{14,79},{16,80}... | collective-permute-start | bytes 1769480 | tf_op jit(solution)/shard_map/ppermute | solution.py:30
  55.4 9.5 %collective-permute-start.23 = (bf16[256,1152]{1,0:T(8,128)(2,1)S(1)}, bf16[256,1152]{1,0:T(8,128)(2,1)S(1)}, u32[]{:S(2)}, u32[]{:S(2)}) collective-permute-start(bf16[256,1152]{1,0:T(8,128)(2,1)S(1)} %add_half.2.refs_0_.refs_1_), channel_id=1, source_target_pairs={{0,48},{8,14},{2,50},{10,8},{4,52},{12,10},{6,54},{14,12},{16,0},{... | collective-permute-start | bytes 1769480 | tf_op jit(solution)/shard_map/ppermute | solution.py:30
  55.8 11.0 %collective-permute-start.20 = (bf16[256,1152]{1,0:T(8,128)(2,1)S(1)}, bf16[256,1152]{1,0:T(8,128)(2,1)S(1)}, u32[]{:S(2)}, u32[]{:S(2)}) collective-permute-start(bf16[256,1152]{1,0:T(8,128)(2,1)S(1)} %add_half.3.refs_0_), channel_id=1, source_target_pairs={{0,16},{8,10},{2,18},{10,12},{4,20},{12,14},{6,22},{14,8},{16,32},... | collective-permute-start | bytes 1769480 | tf_op jit(solution)/shard_map/ppermute | solution.py:30
  63.1 9.1 %collective-permute-start.22 = (bf16[256,1152]{1,0:T(8,128)(2,1)S(1)}, bf16[256,1152]{1,0:T(8,128)(2,1)S(1)}, u32[]{:S(2)}, u32[]{:S(2)}) collective-permute-start(bf16[256,1152]{1,0:T(8,128)(2,1)S(1)} %get-tuple-element.38), channel_id=1, source_target_pairs={{0,48},{8,14},{2,50},{10,8},{4,52},{12,10},{6,54},{14,12},{16,0},{... | collective-permute-start | bytes 1769480 | tf_op jit(solution)/shard_map/ppermute | solution.py:30
  64.8 14.9 %copy-start.1 = (bf16[128,1152]{1,0:T(8,128)(2,1)S(1)}, bf16[128,1152]{1,0:T(8,128)(2,1)}, u32[]{:S(2)}) copy-start(bf16[128,1152]{1,0:T(8,128)(2,1)} %refs_1_.1) | copy-start | bytes 884740
  64.8 14.8 %copy-start.3 = (bf16[128,1152]{1,0:T(8,128)(2,1)S(1)}, bf16[128,1152]{1,0:T(8,128)(2,1)}, u32[]{:S(2)}) copy-start(bf16[128,1152]{1,0:T(8,128)(2,1)} %refs_2_.1) | copy-start | bytes 884740
  65.0 10.3 %collective-permute-start.24 = (bf16[256,1152]{1,0:T(8,128)(2,1)S(1)}, bf16[256,1152]{1,0:T(8,128)(2,1)S(1)}, u32[]{:S(2)}, u32[]{:S(2)}) collective-permute-start(bf16[256,1152]{1,0:T(8,128)(2,1)S(1)} %add.5), channel_id=1, source_target_pairs={{0,64},{8,73},{2,66},{10,75},{4,68},{12,77},{6,70},{14,79},{16,80}... | collective-permute-start | bytes 1769480 | tf_op jit(solution)/shard_map/ppermute | solution.py:30
  66.9 10.3 %collective-permute-start.21 = (bf16[256,1152]{1,0:T(8,128)(2,1)S(1)}, bf16[256,1152]{1,0:T(8,128)(2,1)S(1)}, u32[]{:S(2)}, u32[]{:S(2)}) collective-permute-start(bf16[256,1152]{1,0:T(8,128)(2,1)S(1)} %add.4), channel_id=1, source_target_pairs={{0,16},{8,10},{2,18},{10,12},{4,20},{12,14},{6,22},{14,8},{16,32},... | collective-permute-start | bytes 1769480 | tf_op jit(solution)/shard_map/ppermute | solution.py:30
  77.4 2.3 %collective-permute-start.25 = (bf16[128,1152]{1,0:T(8,128)(2,1)S(1)}, bf16[128,1152]{1,0:T(8,128)(2,1)S(1)}, u32[]{:S(2)}, u32[]{:S(2)}) collective-permute-start(bf16[128,1152]{1,0:T(8,128)(2,1)S(1)} %give.1), channel_id=1, source_target_pairs={{0,8},{8,0},{2,10},{10,2},{4,12},{12,4},{6,14},{14,6},{16,24},{24,... | collective-permute-start | bytes 884744 | tf_op jit(solution)/shard_map/ppermute | solution.py:30

commit v6 on v5

--- a/solution.py
+++ b/solution.py
@@ -248,9 +248,10 @@
     )
     own = jnp.concatenate([keep, to_core(give)], axis=0)
     partner, below, above = cross(own), up(own), down(own)
+    own_other, partner = lax.optimization_barrier((to_core(own), partner))
     partner_above, partner_below, far = cross(above), up(partner), down(above)
-    near = [own, partner, above, below]
-    near_other = [to_core(block) for block in near]
+    lines = pack(above, below)
+    near, near_other = [own, partner, lines], [own_other, to_core(partner), to_core(lines)]
     near_held = sums("near", constants, near, near_other, own=True)[0]
     partner_below, near_held = lax.optimization_barrier((partner_below, near_held))
     far, near_held = lax.optimization_barrier((far, near_held))

time: 81.3 us -> 81.5 us (level)
    ppermute x26 -> x25, waiting for transfers between devices: 19 us -> 19.3 us  [sender(): return lambda value: lax.ppermute(value, ('blk', 'grp'), pairs)]
    ppermute x26 -> x25, starting transfers between devices: 30.9 us -> 30.7 us  [sender(): return lambda value: lax.ppermute(value, ('blk', 'grp'), pairs)]
    pallas_call x15 -> x16, Pallas kernels: 26.4 us -> 26.5 us  [call(): pl.pallas_call(lambda *refs: body(*refs[len(after):]), name=name, out_sha...]
  transfers between devices with their start and end apart: 26 -> 25, of which waited for: 9 -> 8; matrix products, arithmetic and copies ran while one was open for 0% -> 0% of each run, Pallas kernels for 29% -> 29%
where the time goes in v6:
time: 81.5 us; the launch traced here: 81.3 us
  starting transfers between devices  30.7 us (38%)
  Pallas kernels  26.5 us (33%)
  waiting for transfers between devices  19.3 us (24%)
  between operations  2.76 us (3%)
  local copies, waits for them, and re-layouts  2.03 us (2%)
    ppermute x25, starting transfers between devices, sender(): return lambda value: lax.ppermute(value, ('blk', 'grp'), pairs)  30.7 us
    pallas_call x16, Pallas kernels, call(): pl.pallas_call(lambda *refs: body(*refs[len(after):]), name=name, out_sha...  26.5 us
    ppermute x25, waiting for transfers between devices, sender(): return lambda value: lax.ppermute(value, ('blk', 'grp'), pairs)  19.3 us
    unnamed x9, local copies, waits for them, and re-layouts  1.95 us
  transfers between devices with their start and end apart: 25, of which 8 were waited for; matrix products, arithmetic and copies ran while one was open for 0% of the time, Pallas kernels for 29%

profile of v6, /device:TPU:1, one launch (start us, length us, event | category | flops | bytes accessed | tf_op | source)
XLA Modules:
  0.0 81.3 jit_solution(10085774333629354497)
XLA Ops:
  2.6 0.0 copy-start
  2.6 1.0 %copy-done = bf16[128,1152]{1,0:T(8,128)(2,1)S(1)} copy-done((bf16[128,1152]{1,0:T(8,128)(2,1)S(1)}, bf16[128,1152]{1,0:T(8,128)(2,1)}, u32[]{:S(2)}) %copy-start) | copy-done | bytes 294936
  3.5 1.0 %copy-done.2 = bf16[128,1152]{1,0:T(8,128)(2,1)S(1)} copy-done((bf16[128,1152]{1,0:T(8,128)(2,1)S(1)}, bf16[128,1152]{1,0:T(8,128)(2,1)}, u32[]{:S(2)}) %copy-start.2) | copy-done | bytes 294936
  4.5 0.2 units.1
  4.7 1.5 %collective-permute-start = (bf16[128,1152]{1,0:T(8,128)(2,1)S(1)}, bf16[128,1152]{1,0:T(8,128)(2,1)S(1)}, u32[]{:S(2)}, u32[]{:S(2)}) collective-permute-start(bf16[128,1152]{1,0:T(8,128)(2,1)S(1)} %get-tuple-element.25), channel_id=1, source_target_pairs={{0,8},{8,0},{2,10},{10,2},{4,12},{12,4},{6,14},{14,6},{16,24},{24,... | collective-permute-start | bytes 884744 | tf_op jit(solution)/shard_map/ppermute | solution.py:30
  6.2 1.2 %collective-permute-done = bf16[128,1152]{1,0:T(8,128)(2,1)S(1)} collective-permute-done((bf16[128,1152]{1,0:T(8,128)(2,1)S(1)}, bf16[128,1152]{1,0:T(8,128)(2,1)S(1)}, u32[]{:S(2)}, u32[]{:S(2)}) %collective-permute-start) | collective-permute-done | bytes 294944 | tf_op jit(solution)/shard_map/ppermute | solution.py:30
  7.5 1.8 %collective-permute-start.6 = (bf16[256,1152]{1,0:T(8,128)(2,1)S(1)}, bf16[256,1152]{1,0:T(8,128)(2,1)S(1)}, u32[]{:S(2)}, u32[]{:S(2)}) collective-permute-start(bf16[256,1152]{1,0:T(8,128)(2,1)S(1)} %constant_dynamic-update-slice_fusion.refs_1_.refs_3_), channel_id=1, source_target_pairs={{0,16},{8,10},{2,18},{10,12},{4,20},{12,14},{6,22},{14,8},{16,32},... | collective-permute-start | bytes 1769480 | tf_op jit(solution)/shard_map/ppermute | solution.py:30
  9.3 2.2 %collective-permute-start.1 = (bf16[256,1152]{1,0:T(8,128)(2,1)S(1)}, bf16[256,1152]{1,0:T(8,128)(2,1)S(1)}, u32[]{:S(2)}, u32[]{:S(2)}) collective-permute-start(bf16[256,1152]{1,0:T(8,128)(2,1)S(1)} %constant_dynamic-update-slice_fusion.refs_1_.refs_3_), channel_id=1, source_target_pairs={{0,48},{8,14},{2,50},{10,8},{4,52},{12,10},{6,54},{14,12},{16,0},{... | collective-permute-start | bytes 1769480 | tf_op jit(solution)/shard_map/ppermute | solution.py:30
  11.5 2.5 %collective-permute-start.4 = (bf16[256,1152]{1,0:T(8,128)(2,1)S(1)}, bf16[256,1152]{1,0:T(8,128)(2,1)S(1)}, u32[]{:S(2)}, u32[]{:S(2)}) collective-permute-start(bf16[256,1152]{1,0:T(8,128)(2,1)S(1)} %constant_dynamic-update-slice_fusion.refs_1_.refs_3_), channel_id=1, source_target_pairs={{0,64},{8,73},{2,66},{10,75},{4,68},{12,77},{6,70},{14,79},{16,80}... | collective-permute-start | bytes 1769480 | tf_op jit(solution)/shard_map/ppermute | solution.py:30
  13.9 4.7 %collective-permute-done.6.refs_1_ = bf16[256,1152]{1,0:T(8,128)(2,1)S(1)} collective-permute-done((bf16[256,1152]{1,0:T(8,128)(2,1)S(1)}, bf16[256,1152]{1,0:T(8,128)(2,1)S(1)}, u32[]{:S(2)}, u32[]{:S(2)}) %collective-permute-start.6) | collective-permute-done | bytes 589856 | tf_op jit(solution)/shard_map/ppermute | solution.py:30
  18.7 0.1 pack.2.refs_3_.refs_5_
  18.7 0.9 %collective-permute-start.8 = (bf16[512,1152]{1,0:T(8,128)(2,1)S(1)}, bf16[512,1152]{1,0:T(8,128)(2,1)S(1)}, u32[]{:S(2)}, u32[]{:S(2)}) collective-permute-start(bf16[512,1152]{1,0:T(8,128)(2,1)S(1)} %pack.2.refs_3_.refs_5_), channel_id=1, source_target_pairs={{0,8},{8,0},{2,10},{10,2},{4,12},{12,4},{6,14},{14,6},{16,24},{24,... | collective-permute-start | bytes 3538952 | tf_op jit(solution)/shard_map/ppermute | solution.py:30
  19.6 1.8 %collective-permute-done.4.refs_2_.refs_4_ = bf16[256,1152]{1,0:T(8,128)(2,1)S(1)} collective-permute-done((bf16[256,1152]{1,0:T(8,128)(2,1)S(1)}, bf16[256,1152]{1,0:T(8,128)(2,1)S(1)}, u32[]{:S(2)}, u32[]{:S(2)}) %collective-permute-start.4) | collective-permute-done | bytes 589856 | tf_op jit(solution)/shard_map/ppermute | solution.py:30
  21.4 1.3 %collective-permute-start.5 = (bf16[256,1152]{1,0:T(8,128)(2,1)S(1)}, bf16[256,1152]{1,0:T(8,128)(2,1)S(1)}, u32[]{:S(2)}, u32[]{:S(2)}) collective-permute-start(bf16[256,1152]{1,0:T(8,128)(2,1)S(1)} %collective-permute-done.4.refs_2_.refs_4_), channel_id=1, source_target_pairs={{0,16},{8,10},{2,18},{10,12},{4,20},{12,14},{6,22},{14,8},{16,32},... | collective-permute-start | bytes 1769480 | tf_op jit(solution)/shard_map/ppermute | solution.py:30
  22.8 2.1 %collective-permute-start.2 = (bf16[256,1152]{1,0:T(8,128)(2,1)S(1)}, bf16[256,1152]{1,0:T(8,128)(2,1)S(1)}, u32[]{:S(2)}, u32[]{:S(2)}) collective-permute-start(bf16[256,1152]{1,0:T(8,128)(2,1)S(1)} %collective-permute-done.1.refs_0_), channel_id=1, source_target_pairs={{0,48},{8,14},{2,50},{10,8},{4,52},{12,10},{6,54},{14,12},{16,0},{... | collective-permute-start | bytes 1769480 | tf_op jit(solution)/shard_map/ppermute | solution.py:30
  24.9 2.5 %collective-permute-start.11 = (bf16[256,1152]{1,0:T(8,128)(2,1)S(1)}, bf16[256,1152]{1,0:T(8,128)(2,1)S(1)}, u32[]{:S(2)}, u32[]{:S(2)}) collective-permute-start(bf16[256,1152]{1,0:T(8,128)(2,1)S(1)} %collective-permute-done.1.refs_0_), channel_id=1, source_target_pairs={{0,64},{8,73},{2,66},{10,75},{4,68},{12,77},{6,70},{14,79},{16,80}... | collective-permute-start | bytes 1769480 | tf_op jit(solution)/shard_map/ppermute | solution.py:30
  27.4 5.8 %near.1.refs_10_ = f32[1024,1152]{1,0:T(8,128)S(1)} custom-call(f32[8,256]{1,0:T(8,128)S(1)} %get-tuple-element.23.refs_0_.refs_1_.refs_2_, bf16[256,1152]{1,0:T(8,128)(2,1)S(1)} %constant_dynamic-update-slice_fusion.refs_1_.refs_3_, bf16[256,1152]{1,0:T(8,128)(2,1)S(1)} %collective-permute-done.4.refs_2_.refs_4_, ...), custom_call_target="tpu_custom_call" | custom-call | flops 75497472 | bytes 110656 | tf_op jit(solution)/shard_map/near/pallas_call | solution.py:46
  33.2 0.3 collective-permute-start.10
  33.6 2.5 %collective-permute-start.9 = (bf16[128,1152]{1,0:T(8,128)(2,1)S(1)}, bf16[128,1152]{1,0:T(8,128)(2,1)S(1)}, u32[]{:S(2)}, u32[]{:S(2)}) collective-permute-start(bf16[128,1152]{1,0:T(8,128)(2,1)S(1)} %slice.6), channel_id=1, source_target_pairs={{0,64},{8,73},{2,66},{10,75},{4,68},{12,77},{6,70},{14,79},{16,80}... | collective-permute-start | bytes 884744 | tf_op jit(solution)/shard_map/ppermute | solution.py:30
  36.0 0.5 collective-permute-start.15
  36.5 0.0 collective-permute-start.14
  36.5 4.4 %middle.1.refs_9_ = f32[768,1152]{1,0:T(8,128)S(1)} custom-call(f32[8,256]{1,0:T(8,128)S(1)} %get-tuple-element.23.refs_0_.refs_1_.refs_2_, bf16[256,1152]{1,0:T(8,128)(2,1)S(1)} %collective-permute-done.11.refs_1_.refs_2_, bf16[256,1152]{1,0:T(8,128)(2,1)S(1)} %collective-permute-done.5.refs_2_.refs_3_, ...), custom_call_target="tpu_custom_call" | custom-call | flops 56623104 | bytes 92224 | tf_op jit(solution)/shard_map/middle/pallas_call | solution.py:46
  41.0 0.9 %collective-permute-start.12 = (bf16[256,1152]{1,0:T(8,128)(2,1)S(1)}, bf16[256,1152]{1,0:T(8,128)(2,1)S(1)}, u32[]{:S(2)}, u32[]{:S(2)}) collective-permute-start(bf16[256,1152]{1,0:T(8,128)(2,1)S(1)} %pack.3.refs_1_), channel_id=1, source_target_pairs={{0,8},{8,0},{2,10},{10,2},{4,12},{12,4},{6,14},{14,6},{16,24},{24,... | collective-permute-start | bytes 1769480 | tf_op jit(solution)/shard_map/ppermute | solution.py:30
  41.9 2.6 %last.1.refs_3_ = f32[256,1152]{1,0:T(8,128)S(1)} custom-call(f32[8,256]{1,0:T(8,128)S(1)} %get-tuple-element.23.refs_0_.refs_1_.refs_2_, bf16[256,1152]{1,0:T(8,128)(2,1)S(1)} %pack.3.refs_1_, bf16[256,1152]{1,0:T(8,128)(2,1)S(1)} %collective-permute-done.3.refs_4_.refs_2_, bf16[256,1152]{1,0:T(8,128)(2,1)S(1)} %collective-permute-done.7.refs_5_.refs_3_, ...), custom_call_target="tpu_custom_call" | custom-call | flops 33030144 | bytes 83008 | tf_op jit(solution)/shard_map/last/pallas_call | solution.py:46
  44.6 0.9 %last_rest.1 = (bf16[128,1152]{1,0:T(8,128)(2,1)S(1)}, bf16[128,1152]{1,0:T(8,128)(2,1)S(1)}) custom-call(f32[8,256]{1,0:T(8,128)S(1)} %get-tuple-element.23.refs_0_.refs_1_.refs_2_, bf16[256,1152]{1,0:T(8,128)(2,1)S(1)} %pack.3.refs_1_, bf16[256,1152]{1,0:T(8,128)(2,1)S(1)} %collective-permute-done.12.refs_2_.refs_8_.refs_9_, f32[256,1152]{1,0:T(8,128)S(1)} %last.1.refs_3_), custom_call_target="tpu_custom_call" | custom-call | flops 4718592 | bytes 36928 | tf_op jit(solution)/shard_map/last_rest/pallas_call | solution.py:46
  45.5 2.3 %collective-permute-start.16 = (bf16[128,1152]{1,0:T(8,128)(2,1)S(1)}, bf16[128,1152]{1,0:T(8,128)(2,1)S(1)}, u32[]{:S(2)}, u32[]{:S(2)}) collective-permute-start(bf16[128,1152]{1,0:T(8,128)(2,1)S(1)} %get-tuple-element.36), channel_id=1, source_target_pairs={{0,48},{8,14},{2,50},{10,8},{4,52},{12,10},{6,54},{14,12},{16,0},{... | collective-permute-start | bytes 884744 | tf_op jit(solution)/shard_map/ppermute | solution.py:30
  47.8 2.5 %collective-permute-start.17 = (bf16[128,1152]{1,0:T(8,128)(2,1)S(1)}, bf16[128,1152]{1,0:T(8,128)(2,1)S(1)}, u32[]{:S(2)}, u32[]{:S(2)}) collective-permute-start(bf16[128,1152]{1,0:T(8,128)(2,1)S(1)} %get-tuple-element.33.refs_0_), channel_id=1, source_target_pairs={{0,64},{8,73},{2,66},{10,75},{4,68},{12,77},{6,70},{14,79},{16,80}... | collective-permute-start | bytes 884744 | tf_op jit(solution)/shard_map/ppermute | solution.py:30
  50.3 4.4 %middle_rest.1 = (bf16[256,1152]{1,0:T(8,128)(2,1)S(1)}, bf16[256,1152]{1,0:T(8,128)(2,1)S(1)}, bf16[256,1152]{1,0:T(8,128)(2,1)S(1)}) custom-call(bf16[128,1152]{1,0:T(8,128)(2,1)S(1)} %get-tuple-element.33.refs_0_, f32[8,256]{1,0:T(8,128)S(1)} %get-tuple-element.23.refs_0_.refs_1_.refs_2_, bf16[256,1152]{1,0:T(8,128)(2,1)S(1)} %collective-permute-done.11.refs_1_.refs_2_, ...), custom_call_target="tpu_custom_call" | custom-call | flops 56623104 | bytes 119872 | tf_op jit(solution)/shard_map/middle_rest/pallas_call | solution.py:46
  54.8 0.3 collective-permute-start.18
  55.0 0.1 add_half.2.refs_0_.refs_1_
  55.1 0.7 collective-permute-start.22
  55.8 0.1 add_half.3.refs_0_
  55.9 1.2 %collective-permute-start.19 = (bf16[256,1152]{1,0:T(8,128)(2,1)S(1)}, bf16[256,1152]{1,0:T(8,128)(2,1)S(1)}, u32[]{:S(2)}, u32[]{:S(2)}) collective-permute-start(bf16[256,1152]{1,0:T(8,128)(2,1)S(1)} %add_half.3.refs_0_), channel_id=1, source_target_pairs={{0,16},{8,10},{2,18},{10,12},{4,20},{12,14},{6,22},{14,8},{16,32},... | collective-permute-start | bytes 1769480 | tf_op jit(solution)/shard_map/ppermute | solution.py:30
  57.1 5.8 %near_rest.1 = (bf16[256,1152]{1,0:T(8,128)(2,1)S(1)}, bf16[256,1152]{1,0:T(8,128)(2,1)S(1)}, bf16[256,1152]{1,0:T(8,128)(2,1)S(1)}, bf16[256,1152]{1,0:T(8,128)(2,1)S(1)}) custom-call(bf16[256,1152]{1,0:T(8,128)(2,1)S(1)} %add_half.3.refs_0_, bf16[256,1152]{1,0:T(8,128)(2,1)S(1)} %add_half.2.refs_0_.refs_1_, ...), custom_call_target="tpu_custom_call" | custom-call | flops 75497472 | bytes 147520 | tf_op jit(solution)/shard_map/near_rest/pallas_call | solution.py:46
  62.9 1.9 %collective-permute-start.21 = (bf16[256,1152]{1,0:T(8,128)(2,1)S(1)}, bf16[256,1152]{1,0:T(8,128)(2,1)S(1)}, u32[]{:S(2)}, u32[]{:S(2)}) collective-permute-start(bf16[256,1152]{1,0:T(8,128)(2,1)S(1)} %get-tuple-element.42), channel_id=1, source_target_pairs={{0,48},{8,14},{2,50},{10,8},{4,52},{12,10},{6,54},{14,12},{16,0},{... | collective-permute-start | bytes 1769480 | tf_op jit(solution)/shard_map/ppermute | solution.py:30
  64.8 0.3 collective-permute-done.18.refs_1_
  65.1 0.1 add.3.refs_0_
  65.2 0.1 add.5
  65.4 1.8 %collective-permute-start.23 = (bf16[256,1152]{1,0:T(8,128)(2,1)S(1)}, bf16[256,1152]{1,0:T(8,128)(2,1)S(1)}, u32[]{:S(2)}, u32[]{:S(2)}) collective-permute-start(bf16[256,1152]{1,0:T(8,128)(2,1)S(1)} %add.5), channel_id=1, source_target_pairs={{0,64},{8,73},{2,66},{10,75},{4,68},{12,77},{6,70},{14,79},{16,80}... | collective-permute-start | bytes 1769480 | tf_op jit(solution)/shard_map/ppermute | solution.py:30
  67.2 0.1 add.4
  67.3 0.2 collective-permute-start.20
  67.5 4.5 %collective-permute-done.21.refs_2_.refs_6_ = bf16[256,1152]{1,0:T(8,128)(2,1)S(1)} collective-permute-done((bf16[256,1152]{1,0:T(8,128)(2,1)S(1)}, bf16[256,1152]{1,0:T(8,128)(2,1)S(1)}, u32[]{:S(2)}, u32[]{:S(2)}) %collective-permute-start.21) | collective-permute-done | bytes 589856 | tf_op jit(solution)/shard_map/ppermute | solution.py:30
  72.0 3.7 %collective-permute-done.23.refs_3_.refs_7_ = bf16[256,1152]{1,0:T(8,128)(2,1)S(1)} collective-permute-done((bf16[256,1152]{1,0:T(8,128)(2,1)S(1)}, bf16[256,1152]{1,0:T(8,128)(2,1)S(1)}, u32[]{:S(2)}, u32[]{:S(2)}) %collective-permute-start.23) | collective-permute-done | bytes 589856 | tf_op jit(solution)/shard_map/ppermute | solution.py:30
  75.7 1.9 %collective-permute-done.20.refs_1_.refs_5_ = bf16[256,1152]{1,0:T(8,128)(2,1)S(1)} collective-permute-done((bf16[256,1152]{1,0:T(8,128)(2,1)S(1)}, bf16[256,1152]{1,0:T(8,128)(2,1)S(1)}, u32[]{:S(2)}, u32[]{:S(2)}) %collective-permute-start.20) | collective-permute-done | bytes 589856 | tf_op jit(solution)/shard_map/ppermute | solution.py:30
  77.6 0.2 give.1
  77.8 0.9 %collective-permute-start.24 = (bf16[128,1152]{1,0:T(8,128)(2,1)S(1)}, bf16[128,1152]{1,0:T(8,128)(2,1)S(1)}, u32[]{:S(2)}, u32[]{:S(2)}) collective-permute-start(bf16[128,1152]{1,0:T(8,128)(2,1)S(1)} %give.1), channel_id=1, source_target_pairs={{0,8},{8,0},{2,10},{10,2},{4,12},{12,4},{6,14},{14,6},{16,24},{24,... | collective-permute-start | bytes 884744 | tf_op jit(solution)/shard_map/ppermute | solution.py:30
  78.7 1.2 %collective-permute-done.24.refs_3_ = bf16[128,1152]{1,0:T(8,128)(2,1)S(1)} collective-permute-done((bf16[128,1152]{1,0:T(8,128)(2,1)S(1)}, bf16[128,1152]{1,0:T(8,128)(2,1)S(1)}, u32[]{:S(2)}, u32[]{:S(2)}) %collective-permute-start.24) | collective-permute-done | bytes 294944 | tf_op jit(solution)/shard_map/ppermute | solution.py:30
  79.9 1.4 %final.1 = (bf16[128,1152]{1,0:T(8,128)(2,1)}, bf16[128,1152]{1,0:T(8,128)(2,1)}) custom-call(s32[1]{0:T(128)} %bitcast.refs_0_, bf16[128,1152]{1,0:T(8,128)(2,1)S(1)} %copy-done.1, bf16[128,1152]{1,0:T(8,128)(2,1)S(1)} %copy-done.3, bf16[128,1152]{1,0:T(8,128)(2,1)S(1)} %collective-permute-done.24.refs_3_, ...), custom_call_target="tpu_custom_call" | custom-call | flops 46080 | bytes 59904 | tf_op jit(solution)/shard_map/final/pallas_call | solution.py:46
  (30 shorter events, 0.2 us)
Async XLA Ops:
  2.6 1.0 %copy-start = (bf16[128,1152]{1,0:T(8,128)(2,1)S(1)}, bf16[128,1152]{1,0:T(8,128)(2,1)}, u32[]{:S(2)}) copy-start(bf16[128,1152]{1,0:T(8,128)(2,1)} %refs_1_.1) | copy-start | bytes 884740
  3.5 1.0 %copy-start.2 = (bf16[128,1152]{1,0:T(8,128)(2,1)S(1)}, bf16[128,1152]{1,0:T(8,128)(2,1)}, u32[]{:S(2)}) copy-start(bf16[128,1152]{1,0:T(8,128)(2,1)} %refs_2_.1) | copy-start | bytes 884740
  4.7 2.7 %collective-permute-start = (bf16[128,1152]{1,0:T(8,128)(2,1)S(1)}, bf16[128,1152]{1,0:T(8,128)(2,1)S(1)}, u32[]{:S(2)}, u32[]{:S(2)}) collective-permute-start(bf16[128,1152]{1,0:T(8,128)(2,1)S(1)} %get-tuple-element.25), channel_id=1, source_target_pairs={{0,8},{8,0},{2,10},{10,2},{4,12},{12,4},{6,14},{14,6},{16,24},{24,... | collective-permute-start | bytes 884744 | tf_op jit(solution)/shard_map/ppermute | solution.py:30
  7.5 11.2 %collective-permute-start.6 = (bf16[256,1152]{1,0:T(8,128)(2,1)S(1)}, bf16[256,1152]{1,0:T(8,128)(2,1)S(1)}, u32[]{:S(2)}, u32[]{:S(2)}) collective-permute-start(bf16[256,1152]{1,0:T(8,128)(2,1)S(1)} %constant_dynamic-update-slice_fusion.refs_1_.refs_3_), channel_id=1, source_target_pairs={{0,16},{8,10},{2,18},{10,12},{4,20},{12,14},{6,22},{14,8},{16,32},... | collective-permute-start | bytes 1769480 | tf_op jit(solution)/shard_map/ppermute | solution.py:30
  9.3 9.4 %collective-permute-start.1 = (bf16[256,1152]{1,0:T(8,128)(2,1)S(1)}, bf16[256,1152]{1,0:T(8,128)(2,1)S(1)}, u32[]{:S(2)}, u32[]{:S(2)}) collective-permute-start(bf16[256,1152]{1,0:T(8,128)(2,1)S(1)} %constant_dynamic-update-slice_fusion.refs_1_.refs_3_), channel_id=1, source_target_pairs={{0,48},{8,14},{2,50},{10,8},{4,52},{12,10},{6,54},{14,12},{16,0},{... | collective-permute-start | bytes 1769480 | tf_op jit(solution)/shard_map/ppermute | solution.py:30
  11.5 9.9 %collective-permute-start.4 = (bf16[256,1152]{1,0:T(8,128)(2,1)S(1)}, bf16[256,1152]{1,0:T(8,128)(2,1)S(1)}, u32[]{:S(2)}, u32[]{:S(2)}) collective-permute-start(bf16[256,1152]{1,0:T(8,128)(2,1)S(1)} %constant_dynamic-update-slice_fusion.refs_1_.refs_3_), channel_id=1, source_target_pairs={{0,64},{8,73},{2,66},{10,75},{4,68},{12,77},{6,70},{14,79},{16,80}... | collective-permute-start | bytes 1769480 | tf_op jit(solution)/shard_map/ppermute | solution.py:30
  13.9 7.5 %collective-permute-start.3 = (bf16[256,1152]{1,0:T(8,128)(2,1)S(1)}, bf16[256,1152]{1,0:T(8,128)(2,1)S(1)}, u32[]{:S(2)}, u32[]{:S(2)}) collective-permute-start(bf16[256,1152]{1,0:T(8,128)(2,1)S(1)} %constant_dynamic-update-slice_fusion.refs_1_.refs_3_), channel_id=1, source_target_pairs={{0,8},{8,0},{2,10},{10,2},{4,12},{12,4},{6,14},{14,6},{16,24},{24,... | collective-permute-start | bytes 1769480 | tf_op jit(solution)/shard_map/ppermute | solution.py:30
  18.7 8.6 %collective-permute-start.8 = (bf16[512,1152]{1,0:T(8,128)(2,1)S(1)}, bf16[512,1152]{1,0:T(8,128)(2,1)S(1)}, u32[]{:S(2)}, u32[]{:S(2)}) collective-permute-start(bf16[512,1152]{1,0:T(8,128)(2,1)S(1)} %pack.2.refs_3_.refs_5_), channel_id=1, source_target_pairs={{0,8},{8,0},{2,10},{10,2},{4,12},{12,4},{6,14},{14,6},{16,24},{24,... | collective-permute-start | bytes 3538952 | tf_op jit(solution)/shard_map/ppermute | solution.py:30
  21.4 6.0 %collective-permute-start.7 = (bf16[256,1152]{1,0:T(8,128)(2,1)S(1)}, bf16[256,1152]{1,0:T(8,128)(2,1)S(1)}, u32[]{:S(2)}, u32[]{:S(2)}) collective-permute-start(bf16[256,1152]{1,0:T(8,128)(2,1)S(1)} %collective-permute-done.4.refs_2_.refs_4_), channel_id=1, source_target_pairs={{0,8},{8,0},{2,10},{10,2},{4,12},{12,4},{6,14},{14,6},{16,24},{24,... | collective-permute-start | bytes 1769480 | tf_op jit(solution)/shard_map/ppermute | solution.py:30
  21.4 11.7 %collective-permute-start.5 = (bf16[256,1152]{1,0:T(8,128)(2,1)S(1)}, bf16[256,1152]{1,0:T(8,128)(2,1)S(1)}, u32[]{:S(2)}, u32[]{:S(2)}) collective-permute-start(bf16[256,1152]{1,0:T(8,128)(2,1)S(1)} %collective-permute-done.4.refs_2_.refs_4_), channel_id=1, source_target_pairs={{0,16},{8,10},{2,18},{10,12},{4,20},{12,14},{6,22},{14,8},{16,32},... | collective-permute-start | bytes 1769480 | tf_op jit(solution)/shard_map/ppermute | solution.py:30
  22.8 10.4 %collective-permute-start.2 = (bf16[256,1152]{1,0:T(8,128)(2,1)S(1)}, bf16[256,1152]{1,0:T(8,128)(2,1)S(1)}, u32[]{:S(2)}, u32[]{:S(2)}) collective-permute-start(bf16[256,1152]{1,0:T(8,128)(2,1)S(1)} %collective-permute-done.1.refs_0_), channel_id=1, source_target_pairs={{0,48},{8,14},{2,50},{10,8},{4,52},{12,10},{6,54},{14,12},{16,0},{... | collective-permute-start | bytes 1769480 | tf_op jit(solution)/shard_map/ppermute | solution.py:30
  24.9 11.2 %collective-permute-start.11 = (bf16[256,1152]{1,0:T(8,128)(2,1)S(1)}, bf16[256,1152]{1,0:T(8,128)(2,1)S(1)}, u32[]{:S(2)}, u32[]{:S(2)}) collective-permute-start(bf16[256,1152]{1,0:T(8,128)(2,1)S(1)} %collective-permute-done.1.refs_0_), channel_id=1, source_target_pairs={{0,64},{8,73},{2,66},{10,75},{4,68},{12,77},{6,70},{14,79},{16,80}... | collective-permute-start | bytes 1769480 | tf_op jit(solution)/shard_map/ppermute | solution.py:30
  33.2 7.7 %collective-permute-start.10 = (bf16[128,1152]{1,0:T(8,128)(2,1)S(1)}, bf16[128,1152]{1,0:T(8,128)(2,1)S(1)}, u32[]{:S(2)}, u32[]{:S(2)}) collective-permute-start(bf16[128,1152]{1,0:T(8,128)(2,1)S(1)} %slice.7), channel_id=1, source_target_pairs={{0,16},{8,10},{2,18},{10,12},{4,20},{12,14},{6,22},{14,8},{16,32},... | collective-permute-start | bytes 884744 | tf_op jit(solution)/shard_map/ppermute | solution.py:30
  33.6 7.4 %collective-permute-start.9 = (bf16[128,1152]{1,0:T(8,128)(2,1)S(1)}, bf16[128,1152]{1,0:T(8,128)(2,1)S(1)}, u32[]{:S(2)}, u32[]{:S(2)}) collective-permute-start(bf16[128,1152]{1,0:T(8,128)(2,1)S(1)} %slice.6), channel_id=1, source_target_pairs={{0,64},{8,73},{2,66},{10,75},{4,68},{12,77},{6,70},{14,79},{16,80}... | collective-permute-start | bytes 884744 | tf_op jit(solution)/shard_map/ppermute | solution.py:30
  36.0 5.9 %collective-permute-start.13 = (bf16[256,1152]{1,0:T(8,128)(2,1)S(1)}, bf16[256,1152]{1,0:T(8,128)(2,1)S(1)}, u32[]{:S(2)}, u32[]{:S(2)}) collective-permute-start(bf16[256,1152]{1,0:T(8,128)(2,1)S(1)} %collective-permute-done.11.refs_1_.refs_2_), channel_id=1, source_target_pairs={{0,8},{8,0},{2,10},{10,2},{4,12},{12,4},{6,14},{14,6},{16,24},{24,... | collective-permute-start | bytes 1769480 | tf_op jit(solution)/shard_map/ppermute | solution.py:30
  36.0 5.9 %collective-permute-start.15 = (bf16[256,1152]{1,0:T(8,128)(2,1)S(1)}, bf16[256,1152]{1,0:T(8,128)(2,1)S(1)}, u32[]{:S(2)}, u32[]{:S(2)}) collective-permute-start(bf16[256,1152]{1,0:T(8,128)(2,1)S(1)} %collective-permute-done.2.refs_3_.refs_4_), channel_id=1, source_target_pairs={{0,8},{8,0},{2,10},{10,2},{4,12},{12,4},{6,14},{14,6},{16,24},{24,... | collective-permute-start | bytes 1769480 | tf_op jit(solution)/shard_map/ppermute | solution.py:30
  36.5 5.4 %collective-permute-start.14 = (bf16[256,1152]{1,0:T(8,128)(2,1)S(1)}, bf16[256,1152]{1,0:T(8,128)(2,1)S(1)}, u32[]{:S(2)}, u32[]{:S(2)}) collective-permute-start(bf16[256,1152]{1,0:T(8,128)(2,1)S(1)} %collective-permute-done.5.refs_2_.refs_3_), channel_id=1, source_target_pairs={{0,8},{8,0},{2,10},{10,2},{4,12},{12,4},{6,14},{14,6},{16,24},{24,... | collective-permute-start | bytes 1769480 | tf_op jit(solution)/shard_map/ppermute | solution.py:30
  41.0 3.5 %collective-permute-start.12 = (bf16[256,1152]{1,0:T(8,128)(2,1)S(1)}, bf16[256,1152]{1,0:T(8,128)(2,1)S(1)}, u32[]{:S(2)}, u32[]{:S(2)}) collective-permute-start(bf16[256,1152]{1,0:T(8,128)(2,1)S(1)} %pack.3.refs_1_), channel_id=1, source_target_pairs={{0,8},{8,0},{2,10},{10,2},{4,12},{12,4},{6,14},{14,6},{16,24},{24,... | collective-permute-start | bytes 1769480 | tf_op jit(solution)/shard_map/ppermute | solution.py:30
  45.5 9.5 %collective-permute-start.16 = (bf16[128,1152]{1,0:T(8,128)(2,1)S(1)}, bf16[128,1152]{1,0:T(8,128)(2,1)S(1)}, u32[]{:S(2)}, u32[]{:S(2)}) collective-permute-start(bf16[128,1152]{1,0:T(8,128)(2,1)S(1)} %get-tuple-element.36), channel_id=1, source_target_pairs={{0,48},{8,14},{2,50},{10,8},{4,52},{12,10},{6,54},{14,12},{16,0},{... | collective-permute-start | bytes 884744 | tf_op jit(solution)/shard_map/ppermute | solution.py:30
  47.8 8.0 %collective-permute-start.17 = (bf16[128,1152]{1,0:T(8,128)(2,1)S(1)}, bf16[128,1152]{1,0:T(8,128)(2,1)S(1)}, u32[]{:S(2)}, u32[]{:S(2)}) collective-permute-start(bf16[128,1152]{1,0:T(8,128)(2,1)S(1)} %get-tuple-element.33.refs_0_), channel_id=1, source_target_pairs={{0,64},{8,73},{2,66},{10,75},{4,68},{12,77},{6,70},{14,79},{16,80}... | collective-permute-start | bytes 884744 | tf_op jit(solution)/shard_map/ppermute | solution.py:30
  54.8 10.3 %collective-permute-start.18 = (bf16[256,1152]{1,0:T(8,128)(2,1)S(1)}, bf16[256,1152]{1,0:T(8,128)(2,1)S(1)}, u32[]{:S(2)}, u32[]{:S(2)}) collective-permute-start(bf16[256,1152]{1,0:T(8,128)(2,1)S(1)} %get-tuple-element.41), channel_id=1, source_target_pairs={{0,64},{8,73},{2,66},{10,75},{4,68},{12,77},{6,70},{14,79},{16,80}... | collective-permute-start | bytes 1769480 | tf_op jit(solution)/shard_map/ppermute | solution.py:30
  55.1 10.1 %collective-permute-start.22 = (bf16[256,1152]{1,0:T(8,128)(2,1)S(1)}, bf16[256,1152]{1,0:T(8,128)(2,1)S(1)}, u32[]{:S(2)}, u32[]{:S(2)}) collective-permute-start(bf16[256,1152]{1,0:T(8,128)(2,1)S(1)} %add_half.2.refs_0_.refs_1_), channel_id=1, source_target_pairs={{0,48},{8,14},{2,50},{10,8},{4,52},{12,10},{6,54},{14,12},{16,0},{... | collective-permute-start | bytes 1769480 | tf_op jit(solution)/shard_map/ppermute | solution.py:30
  55.9 11.2 %collective-permute-start.19 = (bf16[256,1152]{1,0:T(8,128)(2,1)S(1)}, bf16[256,1152]{1,0:T(8,128)(2,1)S(1)}, u32[]{:S(2)}, u32[]{:S(2)}) collective-permute-start(bf16[256,1152]{1,0:T(8,128)(2,1)S(1)} %add_half.3.refs_0_), channel_id=1, source_target_pairs={{0,16},{8,10},{2,18},{10,12},{4,20},{12,14},{6,22},{14,8},{16,32},... | collective-permute-start | bytes 1769480 | tf_op jit(solution)/shard_map/ppermute | solution.py:30
  62.9 9.1 %collective-permute-start.21 = (bf16[256,1152]{1,0:T(8,128)(2,1)S(1)}, bf16[256,1152]{1,0:T(8,128)(2,1)S(1)}, u32[]{:S(2)}, u32[]{:S(2)}) collective-permute-start(bf16[256,1152]{1,0:T(8,128)(2,1)S(1)} %get-tuple-element.42), channel_id=1, source_target_pairs={{0,48},{8,14},{2,50},{10,8},{4,52},{12,10},{6,54},{14,12},{16,0},{... | collective-permute-start | bytes 1769480 | tf_op jit(solution)/shard_map/ppermute | solution.py:30
  65.4 10.3 %collective-permute-start.23 = (bf16[256,1152]{1,0:T(8,128)(2,1)S(1)}, bf16[256,1152]{1,0:T(8,128)(2,1)S(1)}, u32[]{:S(2)}, u32[]{:S(2)}) collective-permute-start(bf16[256,1152]{1,0:T(8,128)(2,1)S(1)} %add.5), channel_id=1, source_target_pairs={{0,64},{8,73},{2,66},{10,75},{4,68},{12,77},{6,70},{14,79},{16,80}... | collective-permute-start | bytes 1769480 | tf_op jit(solution)/shard_map/ppermute | solution.py:30
  67.3 10.3 %collective-permute-start.20 = (bf16[256,1152]{1,0:T(8,128)(2,1)S(1)}, bf16[256,1152]{1,0:T(8,128)(2,1)S(1)}, u32[]{:S(2)}, u32[]{:S(2)}) collective-permute-start(bf16[256,1152]{1,0:T(8,128)(2,1)S(1)} %add.4), channel_id=1, source_target_pairs={{0,16},{8,10},{2,18},{10,12},{4,20},{12,14},{6,22},{14,8},{16,32},... | collective-permute-start | bytes 1769480 | tf_op jit(solution)/shard_map/ppermute | solution.py:30
  77.6 2.3 %copy-start.1 = (bf16[128,1152]{1,0:T(8,128)(2,1)S(1)}, bf16[128,1152]{1,0:T(8,128)(2,1)}, u32[]{:S(2)}) copy-start(bf16[128,1152]{1,0:T(8,128)(2,1)} %refs_1_.1) | copy-start | bytes 884740
  77.6 2.3 %copy-start.3 = (bf16[128,1152]{1,0:T(8,128)(2,1)S(1)}, bf16[128,1152]{1,0:T(8,128)(2,1)}, u32[]{:S(2)}) copy-start(bf16[128,1152]{1,0:T(8,128)(2,1)} %refs_2_.1) | copy-start | bytes 884740
  77.8 2.1 %collective-permute-start.24 = (bf16[128,1152]{1,0:T(8,128)(2,1)S(1)}, bf16[128,1152]{1,0:T(8,128)(2,1)S(1)}, u32[]{:S(2)}, u32[]{:S(2)}) collective-permute-start(bf16[128,1152]{1,0:T(8,128)(2,1)S(1)} %give.1), channel_id=1, source_target_pairs={{0,8},{8,0},{2,10},{10,2},{4,12},{12,4},{6,14},{14,6},{16,24},{24,... | collective-permute-start | bytes 884744 | tf_op jit(solution)/shard_map/ppermute | solution.py:30

commit v7 on v5

--- a/solution.py
+++ b/solution.py
@@ -203,35 +203,62 @@
 
     got = to_core(call("give", give_body, [array(rows, feature)], terms, 4 * rows * feature)[0])
 
-    def body(core, picture, caption, got, *refs):
-        kept, (image_out, text_out) = refs[:-2], refs[-2:]
-
-        def finish(raw, direct, out):
-            unit, inverse = unit_of(raw[...].astype(jnp.float32))
-            along = jnp.sum(unit * direct, axis=1, keepdims=True)
-            out[...] = (inverse * (direct - unit * along)).astype(jnp.bfloat16)
-
-        def direct_kept():
-            return total_of([ref[pl.ds(0, rows), :] for ref in kept])
+    def gradient(raw, direct):
+        unit, inverse = unit_of(raw[...].astype(jnp.float32))
+        along = jnp.sum(unit * direct, axis=1, keepdims=True)
+        return (inverse * (direct - unit * along)).astype(jnp.bfloat16)
+
+    def carried_body(core, picture, caption, *refs):
+        direct = total_of([ref[pl.ds(0, rows), :] for ref in refs[:-1]])
 
         @pl.when(core[0] == 0)
         def _():
-            finish(picture, got[...].astype(jnp.float32), image_out)
-            finish(caption, direct_kept(), text_out)
+            refs[-1][...] = gradient(caption, direct)
 
         @pl.when(core[0] != 0)
         def _():
-            finish(picture, direct_kept(), image_out)
-            finish(caption, got[...].astype(jnp.float32), text_out)
-
-    return call(
-        "final",
+            refs[-1][...] = gradient(picture, direct)
+
+    carried = call(
+        "carried",
+        carried_body,
+        [array(rows, feature)],
+        [picture, caption, *terms],
+        10 * rows * feature,
+        [core],
+    )[0]
+
+    def body(core, picture, caption, got, carried, image_out, text_out, other, sems):
+        def finish(raw, carried_out, other_out):
+            carried_copy = pltpu.make_async_copy(carried, carried_out, sems.at[0])
+            carried_copy.start()
+            other[...] = gradient(raw, got[...].astype(jnp.float32))
+            other_copy = pltpu.make_async_copy(other, other_out, sems.at[1])
+            other_copy.start()
+            carried_copy.wait()
+            other_copy.wait()
+
+        @pl.when(core[0] == 0)
+        def _():
+            finish(picture, text_out, image_out)
+
+        @pl.when(core[0] != 0)
+        def _():
+            finish(caption, image_out, text_out)
+
+    return pl.pallas_call(
         body,
-        [array(rows, feature)] * 2,
-        [picture, caption, got, *terms],
-        20 * rows * feature,
-        [core],
-    )
+        name="final",
+        out_shape=[array(rows, feature)] * 2,
+        in_specs=[pl.BlockSpec(memory_space=pltpu.SMEM)]
+        + [pl.BlockSpec(memory_space=pltpu.VMEM)] * 4,
+        out_specs=[pl.BlockSpec(memory_space=pl.ANY)] * 2,
+        scratch_shapes=[
+            pltpu.VMEM((rows, feature), jnp.bfloat16),
+            pltpu.SemaphoreType.DMA((2,)),
+        ],
+        compiler_params=pltpu.CompilerParams(vmem_limit_bytes=VMEM_BYTES),
+    )(core, picture, caption, got, carried)
 
 
 def on_device(

time: 81.3 us -> 81.1 us (level)
    pallas_call x0 -> x1, Pallas kernels: none -> 1 us  [through_norms(): pl.pallas_call(body, name='final', out_shape=[array(rows, feature)] * 2,...]
    pallas_call x15, Pallas kernels: 26.4 us -> 25.5 us  [call(): pl.pallas_call(lambda *refs: body(*refs[len(after):]), name=name, out_sha...]
  transfers between devices with their start and end apart: 26 -> 26, of which waited for: 9 -> 9; matrix products, arithmetic and copies ran while one was open for 0% -> 0% of each run, Pallas kernels for 29% -> 30%
where the time goes in v7:
time: 81.1 us; the launch traced here: 80.9 us
  starting transfers between devices  30.9 us (38%)
  Pallas kernels  26.5 us (33%)
  waiting for transfers between devices  18.5 us (23%)
  between operations  2.94 us (4%)
  local copies, waits for them, and re-layouts  2.03 us (3%)
    ppermute x26, starting transfers between devices, sender(): return lambda value: lax.ppermute(value, ('blk', 'grp'), pairs)  30.9 us
    pallas_call x15, Pallas kernels, call(): pl.pallas_call(lambda *refs: body(*refs[len(after):]), name=name, out_sha...  25.5 us
    ppermute x26, waiting for transfers between devices, sender(): return lambda value: lax.ppermute(value, ('blk', 'grp'), pairs)  18.5 us
    unnamed x9, local copies, waits for them, and re-layouts  1.95 us
  transfers between devices with their start and end apart: 26, of which 9 were waited for; matrix products, arithmetic and copies ran while one was open for 0% of the time, Pallas kernels for 30%

profile of v7, /device:TPU:1, one launch (start us, length us, event | category | flops | bytes accessed | tf_op | source)
XLA Modules:
  0.0 80.9 jit_solution(11960944367088158525)
XLA Ops:
  2.6 1.0 %copy-done = bf16[128,1152]{1,0:T(8,128)(2,1)S(1)} copy-done((bf16[128,1152]{1,0:T(8,128)(2,1)S(1)}, bf16[128,1152]{1,0:T(8,128)(2,1)}, u32[]{:S(2)}) %copy-start) | copy-done | bytes 294936
  3.5 1.0 %copy-done.2 = bf16[128,1152]{1,0:T(8,128)(2,1)S(1)} copy-done((bf16[128,1152]{1,0:T(8,128)(2,1)S(1)}, bf16[128,1152]{1,0:T(8,128)(2,1)}, u32[]{:S(2)}) %copy-start.2) | copy-done | bytes 294936
  4.5 0.2 units.1
  4.7 1.5 %collective-permute-start = (bf16[128,1152]{1,0:T(8,128)(2,1)S(1)}, bf16[128,1152]{1,0:T(8,128)(2,1)S(1)}, u32[]{:S(2)}, u32[]{:S(2)}) collective-permute-start(bf16[128,1152]{1,0:T(8,128)(2,1)S(1)} %get-tuple-element.23), channel_id=1, source_target_pairs={{0,8},{8,0},{2,10},{10,2},{4,12},{12,4},{6,14},{14,6},{16,24},{24,... | collective-permute-start | bytes 884744 | tf_op jit(solution)/shard_map/ppermute | solution.py:30
  6.2 1.2 %collective-permute-done = bf16[128,1152]{1,0:T(8,128)(2,1)S(1)} collective-permute-done((bf16[128,1152]{1,0:T(8,128)(2,1)S(1)}, bf16[128,1152]{1,0:T(8,128)(2,1)S(1)}, u32[]{:S(2)}, u32[]{:S(2)}) %collective-permute-start) | collective-permute-done | bytes 294944 | tf_op jit(solution)/shard_map/ppermute | solution.py:30
  7.5 1.8 %collective-permute-start.5 = (bf16[256,1152]{1,0:T(8,128)(2,1)S(1)}, bf16[256,1152]{1,0:T(8,128)(2,1)S(1)}, u32[]{:S(2)}, u32[]{:S(2)}) collective-permute-start(bf16[256,1152]{1,0:T(8,128)(2,1)S(1)} %constant_dynamic-update-slice_fusion.refs_1_.refs_3_), channel_id=1, source_target_pairs={{0,16},{8,10},{2,18},{10,12},{4,20},{12,14},{6,22},{14,8},{16,32},... | collective-permute-start | bytes 1769480 | tf_op jit(solution)/shard_map/ppermute | solution.py:30
  9.3 2.5 %collective-permute-start.3 = (bf16[256,1152]{1,0:T(8,128)(2,1)S(1)}, bf16[256,1152]{1,0:T(8,128)(2,1)S(1)}, u32[]{:S(2)}, u32[]{:S(2)}) collective-permute-start(bf16[256,1152]{1,0:T(8,128)(2,1)S(1)} %constant_dynamic-update-slice_fusion.refs_1_.refs_3_), channel_id=1, source_target_pairs={{0,64},{8,73},{2,66},{10,75},{4,68},{12,77},{6,70},{14,79},{16,80}... | collective-permute-start | bytes 1769480 | tf_op jit(solution)/shard_map/ppermute | solution.py:30
  11.7 2.2 %collective-permute-start.1 = (bf16[256,1152]{1,0:T(8,128)(2,1)S(1)}, bf16[256,1152]{1,0:T(8,128)(2,1)S(1)}, u32[]{:S(2)}, u32[]{:S(2)}) collective-permute-start(bf16[256,1152]{1,0:T(8,128)(2,1)S(1)} %constant_dynamic-update-slice_fusion.refs_1_.refs_3_), channel_id=1, source_target_pairs={{0,48},{8,14},{2,50},{10,8},{4,52},{12,10},{6,54},{14,12},{16,0},{... | collective-permute-start | bytes 1769480 | tf_op jit(solution)/shard_map/ppermute | solution.py:30
  14.0 4.7 %collective-permute-done.5.refs_4_.refs_6_ = bf16[256,1152]{1,0:T(8,128)(2,1)S(1)} collective-permute-done((bf16[256,1152]{1,0:T(8,128)(2,1)S(1)}, bf16[256,1152]{1,0:T(8,128)(2,1)S(1)}, u32[]{:S(2)}, u32[]{:S(2)}) %collective-permute-start.5) | collective-permute-done | bytes 589856 | tf_op jit(solution)/shard_map/ppermute | solution.py:30
  18.6 0.4 collective-permute-start.9
  19.0 0.2 collective-permute-done.3.refs_2_.refs_4_
  19.2 0.3 collective-permute-start.7
  19.5 1.3 %collective-permute-done.1.refs_3_.refs_5_ = bf16[256,1152]{1,0:T(8,128)(2,1)S(1)} collective-permute-done((bf16[256,1152]{1,0:T(8,128)(2,1)S(1)}, bf16[256,1152]{1,0:T(8,128)(2,1)S(1)}, u32[]{:S(2)}, u32[]{:S(2)}) %collective-permute-start.1) | collective-permute-done | bytes 589856 | tf_op jit(solution)/shard_map/ppermute | solution.py:30
  20.8 0.2 collective-permute-start.8
  20.9 1.6 %collective-permute-start.4 = (bf16[256,1152]{1,0:T(8,128)(2,1)S(1)}, bf16[256,1152]{1,0:T(8,128)(2,1)S(1)}, u32[]{:S(2)}, u32[]{:S(2)}) collective-permute-start(bf16[256,1152]{1,0:T(8,128)(2,1)S(1)} %collective-permute-done.3.refs_2_.refs_4_), channel_id=1, source_target_pairs={{0,16},{8,10},{2,18},{10,12},{4,20},{12,14},{6,22},{14,8},{16,32},... | collective-permute-start | bytes 1769480 | tf_op jit(solution)/shard_map/ppermute | solution.py:30
  22.6 2.1 %collective-permute-start.2 = (bf16[256,1152]{1,0:T(8,128)(2,1)S(1)}, bf16[256,1152]{1,0:T(8,128)(2,1)S(1)}, u32[]{:S(2)}, u32[]{:S(2)}) collective-permute-start(bf16[256,1152]{1,0:T(8,128)(2,1)S(1)} %collective-permute-done.1.refs_3_.refs_5_), channel_id=1, source_target_pairs={{0,48},{8,14},{2,50},{10,8},{4,52},{12,10},{6,54},{14,12},{16,0},{... | collective-permute-start | bytes 1769480 | tf_op jit(solution)/shard_map/ppermute | solution.py:30
  24.7 1.8 %collective-permute-start.12 = (bf16[256,1152]{1,0:T(8,128)(2,1)S(1)}, bf16[256,1152]{1,0:T(8,128)(2,1)S(1)}, u32[]{:S(2)}, u32[]{:S(2)}) collective-permute-start(bf16[256,1152]{1,0:T(8,128)(2,1)S(1)} %collective-permute-done.1.refs_3_.refs_5_), channel_id=1, source_target_pairs={{0,64},{8,73},{2,66},{10,75},{4,68},{12,77},{6,70},{14,79},{16,80}... | collective-permute-start | bytes 1769480 | tf_op jit(solution)/shard_map/ppermute | solution.py:30
  26.5 5.8 %near.1.refs_11_ = f32[1024,1152]{1,0:T(8,128)S(1)} custom-call(f32[8,256]{1,0:T(8,128)S(1)} %get-tuple-element.21.refs_0_.refs_1_.refs_2_, bf16[256,1152]{1,0:T(8,128)(2,1)S(1)} %constant_dynamic-update-slice_fusion.refs_1_.refs_3_, bf16[256,1152]{1,0:T(8,128)(2,1)S(1)} %collective-permute-done.3.refs_2_.refs_4_, ...), custom_call_target="tpu_custom_call" | custom-call | flops 75497472 | bytes 110656 | tf_op jit(solution)/shard_map/near/pallas_call | solution.py:46
  32.4 1.0 %collective-permute-start.11 = (bf16[128,1152]{1,0:T(8,128)(2,1)S(1)}, bf16[128,1152]{1,0:T(8,128)(2,1)S(1)}, u32[]{:S(2)}, u32[]{:S(2)}) collective-permute-start(bf16[128,1152]{1,0:T(8,128)(2,1)S(1)} %slice.7), channel_id=1, source_target_pairs={{0,16},{8,10},{2,18},{10,12},{4,20},{12,14},{6,22},{14,8},{16,32},... | collective-permute-start | bytes 884744 | tf_op jit(solution)/shard_map/ppermute | solution.py:30
  33.4 1.8 %collective-permute-start.10 = (bf16[128,1152]{1,0:T(8,128)(2,1)S(1)}, bf16[128,1152]{1,0:T(8,128)(2,1)S(1)}, u32[]{:S(2)}, u32[]{:S(2)}) collective-permute-start(bf16[128,1152]{1,0:T(8,128)(2,1)S(1)} %slice.6), channel_id=1, source_target_pairs={{0,64},{8,73},{2,66},{10,75},{4,68},{12,77},{6,70},{14,79},{16,80}... | collective-permute-start | bytes 884744 | tf_op jit(solution)/shard_map/ppermute | solution.py:30
  35.2 0.5 collective-permute-start.15
  35.7 4.4 %middle.1.refs_9_ = f32[768,1152]{1,0:T(8,128)S(1)} custom-call(f32[8,256]{1,0:T(8,128)S(1)} %get-tuple-element.21.refs_0_.refs_1_.refs_2_, bf16[256,1152]{1,0:T(8,128)(2,1)S(1)} %collective-permute-done.12.refs_1_.refs_2_, bf16[256,1152]{1,0:T(8,128)(2,1)S(1)} %collective-permute-done.4.refs_2_.refs_3_, ...), custom_call_target="tpu_custom_call" | custom-call | flops 56623104 | bytes 92224 | tf_op jit(solution)/shard_map/middle/pallas_call | solution.py:46
  40.1 0.3 collective-permute-done.10.refs_0_
  40.5 0.8 %collective-permute-start.13 = (bf16[256,1152]{1,0:T(8,128)(2,1)S(1)}, bf16[256,1152]{1,0:T(8,128)(2,1)S(1)}, u32[]{:S(2)}, u32[]{:S(2)}) collective-permute-start(bf16[256,1152]{1,0:T(8,128)(2,1)S(1)} %pack.1.refs_1_), channel_id=1, source_target_pairs={{0,8},{8,0},{2,10},{10,2},{4,12},{12,4},{6,14},{14,6},{16,24},{24,... | collective-permute-start | bytes 1769480 | tf_op jit(solution)/shard_map/ppermute | solution.py:30
  41.3 2.6 %last.1.refs_3_ = f32[256,1152]{1,0:T(8,128)S(1)} custom-call(f32[8,256]{1,0:T(8,128)S(1)} %get-tuple-element.21.refs_0_.refs_1_.refs_2_, bf16[256,1152]{1,0:T(8,128)(2,1)S(1)} %pack.1.refs_1_, bf16[256,1152]{1,0:T(8,128)(2,1)S(1)} %collective-permute-done.6.refs_5_.refs_4_.refs_2_, bf16[256,1152]{1,0:T(8,128)(2,1)S(1)} %collective-permute-done.7.refs_6_.refs_5_.refs_3_, ...), custom_call_target="tpu_custom_call" | custom-call | flops 33030144 | bytes 83008 | tf_op jit(solution)/shard_map/last/pallas_call | solution.py:46
  44.0 0.9 %last_rest.1 = (bf16[128,1152]{1,0:T(8,128)(2,1)S(1)}, bf16[128,1152]{1,0:T(8,128)(2,1)S(1)}) custom-call(f32[8,256]{1,0:T(8,128)S(1)} %get-tuple-element.21.refs_0_.refs_1_.refs_2_, bf16[256,1152]{1,0:T(8,128)(2,1)S(1)} %pack.1.refs_1_, bf16[256,1152]{1,0:T(8,128)(2,1)S(1)} %collective-permute-done.13.refs_2_.refs_8_.refs_10_, f32[256,1152]{1,0:T(8,128)S(1)} %last.1.refs_3_), custom_call_target="tpu_custom_call" | custom-call | flops 4718592 | bytes 36928 | tf_op jit(solution)/shard_map/last_rest/pallas_call | solution.py:46
  44.9 3.2 %collective-permute-start.17 = (bf16[128,1152]{1,0:T(8,128)(2,1)S(1)}, bf16[128,1152]{1,0:T(8,128)(2,1)S(1)}, u32[]{:S(2)}, u32[]{:S(2)}) collective-permute-start(bf16[128,1152]{1,0:T(8,128)(2,1)S(1)} %get-tuple-element.32), channel_id=1, source_target_pairs={{0,48},{8,14},{2,50},{10,8},{4,52},{12,10},{6,54},{14,12},{16,0},{... | collective-permute-start | bytes 884744 | tf_op jit(solution)/shard_map/ppermute | solution.py:30
  48.1 1.8 %collective-permute-start.18 = (bf16[128,1152]{1,0:T(8,128)(2,1)S(1)}, bf16[128,1152]{1,0:T(8,128)(2,1)S(1)}, u32[]{:S(2)}, u32[]{:S(2)}) collective-permute-start(bf16[128,1152]{1,0:T(8,128)(2,1)S(1)} %get-tuple-element.29.refs_0_), channel_id=1, source_target_pairs={{0,64},{8,73},{2,66},{10,75},{4,68},{12,77},{6,70},{14,79},{16,80}... | collective-permute-start | bytes 884744 | tf_op jit(solution)/shard_map/ppermute | solution.py:30
  49.9 4.4 %middle_rest.1 = (bf16[256,1152]{1,0:T(8,128)(2,1)S(1)}, bf16[256,1152]{1,0:T(8,128)(2,1)S(1)}, bf16[256,1152]{1,0:T(8,128)(2,1)S(1)}) custom-call(bf16[128,1152]{1,0:T(8,128)(2,1)S(1)} %get-tuple-element.29.refs_0_, f32[8,256]{1,0:T(8,128)S(1)} %get-tuple-element.21.refs_0_.refs_1_.refs_2_, bf16[256,1152]{1,0:T(8,128)(2,1)S(1)} %collective-permute-done.12.refs_1_.refs_2_, ...), custom_call_target="tpu_custom_call" | custom-call | flops 56623104 | bytes 119872 | tf_op jit(solution)/shard_map/middle_rest/pallas_call | solution.py:46
  54.4 0.9 %collective-permute-start.19 = (bf16[256,1152]{1,0:T(8,128)(2,1)S(1)}, bf16[256,1152]{1,0:T(8,128)(2,1)S(1)}, u32[]{:S(2)}, u32[]{:S(2)}) collective-permute-start(bf16[256,1152]{1,0:T(8,128)(2,1)S(1)} %get-tuple-element.37), channel_id=1, source_target_pairs={{0,64},{8,73},{2,66},{10,75},{4,68},{12,77},{6,70},{14,79},{16,80}... | collective-permute-start | bytes 1769480 | tf_op jit(solution)/shard_map/ppermute | solution.py:30
  55.3 0.1 add_half.2.refs_0_.refs_1_
  55.4 0.3 collective-permute-start.23
  55.8 1.5 %collective-permute-start.20 = (bf16[256,1152]{1,0:T(8,128)(2,1)S(1)}, bf16[256,1152]{1,0:T(8,128)(2,1)S(1)}, u32[]{:S(2)}, u32[]{:S(2)}) collective-permute-start(bf16[256,1152]{1,0:T(8,128)(2,1)S(1)} %add_half.3.refs_0_), channel_id=1, source_target_pairs={{0,16},{8,10},{2,18},{10,12},{4,20},{12,14},{6,22},{14,8},{16,32},... | collective-permute-start | bytes 1769480 | tf_op jit(solution)/shard_map/ppermute | solution.py:30
  57.3 5.8 %near_rest.1 = (bf16[256,1152]{1,0:T(8,128)(2,1)S(1)}, bf16[256,1152]{1,0:T(8,128)(2,1)S(1)}, bf16[256,1152]{1,0:T(8,128)(2,1)S(1)}, bf16[256,1152]{1,0:T(8,128)(2,1)S(1)}) custom-call(bf16[256,1152]{1,0:T(8,128)(2,1)S(1)} %add_half.3.refs_0_, bf16[256,1152]{1,0:T(8,128)(2,1)S(1)} %add_half.2.refs_0_.refs_1_, ...), custom_call_target="tpu_custom_call" | custom-call | flops 75497472 | bytes 147520 | tf_op jit(solution)/shard_map/near_rest/pallas_call | solution.py:46
  63.1 1.5 %collective-permute-start.22 = (bf16[256,1152]{1,0:T(8,128)(2,1)S(1)}, bf16[256,1152]{1,0:T(8,128)(2,1)S(1)}, u32[]{:S(2)}, u32[]{:S(2)}) collective-permute-start(bf16[256,1152]{1,0:T(8,128)(2,1)S(1)} %get-tuple-element.38), channel_id=1, source_target_pairs={{0,48},{8,14},{2,50},{10,8},{4,52},{12,10},{6,54},{14,12},{16,0},{... | collective-permute-start | bytes 1769480 | tf_op jit(solution)/shard_map/ppermute | solution.py:30
  64.7 0.1 add.3.refs_0_
  64.9 0.1 add.5
  65.0 1.8 %collective-permute-start.24 = (bf16[256,1152]{1,0:T(8,128)(2,1)S(1)}, bf16[256,1152]{1,0:T(8,128)(2,1)S(1)}, u32[]{:S(2)}, u32[]{:S(2)}) collective-permute-start(bf16[256,1152]{1,0:T(8,128)(2,1)S(1)} %add.5), channel_id=1, source_target_pairs={{0,64},{8,73},{2,66},{10,75},{4,68},{12,77},{6,70},{14,79},{16,80}... | collective-permute-start | bytes 1769480 | tf_op jit(solution)/shard_map/ppermute | solution.py:30
  66.8 0.1 add.4
  66.9 0.2 collective-permute-start.21
  67.1 5.1 %collective-permute-done.22.refs_2_.refs_5_ = bf16[256,1152]{1,0:T(8,128)(2,1)S(1)} collective-permute-done((bf16[256,1152]{1,0:T(8,128)(2,1)S(1)}, bf16[256,1152]{1,0:T(8,128)(2,1)S(1)}, u32[]{:S(2)}, u32[]{:S(2)}) %collective-permute-start.22) | collective-permute-done | bytes 589856 | tf_op jit(solution)/shard_map/ppermute | solution.py:30
  72.2 3.1 %collective-permute-done.24.refs_3_.refs_6_ = bf16[256,1152]{1,0:T(8,128)(2,1)S(1)} collective-permute-done((bf16[256,1152]{1,0:T(8,128)(2,1)S(1)}, bf16[256,1152]{1,0:T(8,128)(2,1)S(1)}, u32[]{:S(2)}, u32[]{:S(2)}) %collective-permute-start.24) | collective-permute-done | bytes 589856 | tf_op jit(solution)/shard_map/ppermute | solution.py:30
  75.3 1.9 %collective-permute-done.21.refs_1_.refs_4_ = bf16[256,1152]{1,0:T(8,128)(2,1)S(1)} collective-permute-done((bf16[256,1152]{1,0:T(8,128)(2,1)S(1)}, bf16[256,1152]{1,0:T(8,128)(2,1)S(1)}, u32[]{:S(2)}, u32[]{:S(2)}) %collective-permute-start.21) | collective-permute-done | bytes 589856 | tf_op jit(solution)/shard_map/ppermute | solution.py:30
  77.2 0.2 give.1
  77.4 1.1 %collective-permute-start.25 = (bf16[128,1152]{1,0:T(8,128)(2,1)S(1)}, bf16[128,1152]{1,0:T(8,128)(2,1)S(1)}, u32[]{:S(2)}, u32[]{:S(2)}) collective-permute-start(bf16[128,1152]{1,0:T(8,128)(2,1)S(1)} %give.1), channel_id=1, source_target_pairs={{0,8},{8,0},{2,10},{10,2},{4,12},{12,4},{6,14},{14,6},{16,24},{24,... | collective-permute-start | bytes 884744 | tf_op jit(solution)/shard_map/ppermute | solution.py:30
  78.5 0.5 carried.1
  79.0 0.7 collective-permute-done.25.got
  79.7 1.0 %final.1 = (bf16[128,1152]{1,0:T(8,128)(2,1)}, bf16[128,1152]{1,0:T(8,128)(2,1)}) custom-call(s32[1]{0:T(128)} %bitcast.refs_0_.core, bf16[128,1152]{1,0:T(8,128)(2,1)S(1)} %copy-done.1, bf16[128,1152]{1,0:T(8,128)(2,1)S(1)} %copy-done.3, bf16[128,1152]{1,0:T(8,128)(2,1)S(1)} %collective-permute-done.25.got, bf16[128,1152]{1,0:T(8,128)(2,1)S(1)} %carried.1), custom_call_target="tpu_custom_call" | custom-call | tf_op jit(solution)/shard_map/final/pallas_call | solution.py:249
  (32 shorter events, 0.3 us)
Async XLA Ops:
  2.6 1.0 %copy-start = (bf16[128,1152]{1,0:T(8,128)(2,1)S(1)}, bf16[128,1152]{1,0:T(8,128)(2,1)}, u32[]{:S(2)}) copy-start(bf16[128,1152]{1,0:T(8,128)(2,1)} %picture.1) | copy-start | bytes 884740
  3.5 1.0 %copy-start.2 = (bf16[128,1152]{1,0:T(8,128)(2,1)S(1)}, bf16[128,1152]{1,0:T(8,128)(2,1)}, u32[]{:S(2)}) copy-start(bf16[128,1152]{1,0:T(8,128)(2,1)} %caption.1) | copy-start | bytes 884740
  4.7 2.7 %collective-permute-start = (bf16[128,1152]{1,0:T(8,128)(2,1)S(1)}, bf16[128,1152]{1,0:T(8,128)(2,1)S(1)}, u32[]{:S(2)}, u32[]{:S(2)}) collective-permute-start(bf16[128,1152]{1,0:T(8,128)(2,1)S(1)} %get-tuple-element.23), channel_id=1, source_target_pairs={{0,8},{8,0},{2,10},{10,2},{4,12},{12,4},{6,14},{14,6},{16,24},{24,... | collective-permute-start | bytes 884744 | tf_op jit(solution)/shard_map/ppermute | solution.py:30
  7.5 11.2 %collective-permute-start.5 = (bf16[256,1152]{1,0:T(8,128)(2,1)S(1)}, bf16[256,1152]{1,0:T(8,128)(2,1)S(1)}, u32[]{:S(2)}, u32[]{:S(2)}) collective-permute-start(bf16[256,1152]{1,0:T(8,128)(2,1)S(1)} %constant_dynamic-update-slice_fusion.refs_1_.refs_3_), channel_id=1, source_target_pairs={{0,16},{8,10},{2,18},{10,12},{4,20},{12,14},{6,22},{14,8},{16,32},... | collective-permute-start | bytes 1769480 | tf_op jit(solution)/shard_map/ppermute | solution.py:30
  9.3 9.9 %collective-permute-start.3 = (bf16[256,1152]{1,0:T(8,128)(2,1)S(1)}, bf16[256,1152]{1,0:T(8,128)(2,1)S(1)}, u32[]{:S(2)}, u32[]{:S(2)}) collective-permute-start(bf16[256,1152]{1,0:T(8,128)(2,1)S(1)} %constant_dynamic-update-slice_fusion.refs_1_.refs_3_), channel_id=1, source_target_pairs={{0,64},{8,73},{2,66},{10,75},{4,68},{12,77},{6,70},{14,79},{16,80}... | collective-permute-start | bytes 1769480 | tf_op jit(solution)/shard_map/ppermute | solution.py:30
  11.7 9.0 %collective-permute-start.1 = (bf16[256,1152]{1,0:T(8,128)(2,1)S(1)}, bf16[256,1152]{1,0:T(8,128)(2,1)S(1)}, u32[]{:S(2)}, u32[]{:S(2)}) collective-permute-start(bf16[256,1152]{1,0:T(8,128)(2,1)S(1)} %constant_dynamic-update-slice_fusion.refs_1_.refs_3_), channel_id=1, source_target_pairs={{0,48},{8,14},{2,50},{10,8},{4,52},{12,10},{6,54},{14,12},{16,0},{... | collective-permute-start | bytes 1769480 | tf_op jit(solution)/shard_map/ppermute | solution.py:30
  13.9 8.6 %collective-permute-start.6 = (bf16[256,1152]{1,0:T(8,128)(2,1)S(1)}, bf16[256,1152]{1,0:T(8,128)(2,1)S(1)}, u32[]{:S(2)}, u32[]{:S(2)}) collective-permute-start(bf16[256,1152]{1,0:T(8,128)(2,1)S(1)} %constant_dynamic-update-slice_fusion.refs_1_.refs_3_), channel_id=1, source_target_pairs={{0,8},{8,0},{2,10},{10,2},{4,12},{12,4},{6,14},{14,6},{16,24},{24,... | collective-permute-start | bytes 1769480 | tf_op jit(solution)/shard_map/ppermute | solution.py:30
  18.6 6.1 %collective-permute-start.9 = (bf16[256,1152]{1,0:T(8,128)(2,1)S(1)}, bf16[256,1152]{1,0:T(8,128)(2,1)S(1)}, u32[]{:S(2)}, u32[]{:S(2)}) collective-permute-start(bf16[256,1152]{1,0:T(8,128)(2,1)S(1)} %collective-permute-done.5.refs_4_.refs_6_), channel_id=1, source_target_pairs={{0,8},{8,0},{2,10},{10,2},{4,12},{12,4},{6,14},{14,6},{16,24},{24,... | collective-permute-start | bytes 1769480 | tf_op jit(solution)/shard_map/ppermute | solution.py:30
  19.2 7.3 %collective-permute-start.7 = (bf16[256,1152]{1,0:T(8,128)(2,1)S(1)}, bf16[256,1152]{1,0:T(8,128)(2,1)S(1)}, u32[]{:S(2)}, u32[]{:S(2)}) collective-permute-start(bf16[256,1152]{1,0:T(8,128)(2,1)S(1)} %collective-permute-done.3.refs_2_.refs_4_), channel_id=1, source_target_pairs={{0,8},{8,0},{2,10},{10,2},{4,12},{12,4},{6,14},{14,6},{16,24},{24,... | collective-permute-start | bytes 1769480 | tf_op jit(solution)/shard_map/ppermute | solution.py:30
  20.8 5.8 %collective-permute-start.8 = (bf16[256,1152]{1,0:T(8,128)(2,1)S(1)}, bf16[256,1152]{1,0:T(8,128)(2,1)S(1)}, u32[]{:S(2)}, u32[]{:S(2)}) collective-permute-start(bf16[256,1152]{1,0:T(8,128)(2,1)S(1)} %collective-permute-done.1.refs_3_.refs_5_), channel_id=1, source_target_pairs={{0,8},{8,0},{2,10},{10,2},{4,12},{12,4},{6,14},{14,6},{16,24},{24,... | collective-permute-start | bytes 1769480 | tf_op jit(solution)/shard_map/ppermute | solution.py:30
  20.9 11.4 %collective-permute-start.4 = (bf16[256,1152]{1,0:T(8,128)(2,1)S(1)}, bf16[256,1152]{1,0:T(8,128)(2,1)S(1)}, u32[]{:S(2)}, u32[]{:S(2)}) collective-permute-start(bf16[256,1152]{1,0:T(8,128)(2,1)S(1)} %collective-permute-done.3.refs_2_.refs_4_), channel_id=1, source_target_pairs={{0,16},{8,10},{2,18},{10,12},{4,20},{12,14},{6,22},{14,8},{16,32},... | collective-permute-start | bytes 1769480 | tf_op jit(solution)/shard_map/ppermute | solution.py:30
  22.6 9.7 %collective-permute-start.2 = (bf16[256,1152]{1,0:T(8,128)(2,1)S(1)}, bf16[256,1152]{1,0:T(8,128)(2,1)S(1)}, u32[]{:S(2)}, u32[]{:S(2)}) collective-permute-start(bf16[256,1152]{1,0:T(8,128)(2,1)S(1)} %collective-permute-done.1.refs_3_.refs_5_), channel_id=1, source_target_pairs={{0,48},{8,14},{2,50},{10,8},{4,52},{12,10},{6,54},{14,12},{16,0},{... | collective-permute-start | bytes 1769480 | tf_op jit(solution)/shard_map/ppermute | solution.py:30
  24.7 11.0 %collective-permute-start.12 = (bf16[256,1152]{1,0:T(8,128)(2,1)S(1)}, bf16[256,1152]{1,0:T(8,128)(2,1)S(1)}, u32[]{:S(2)}, u32[]{:S(2)}) collective-permute-start(bf16[256,1152]{1,0:T(8,128)(2,1)S(1)} %collective-permute-done.1.refs_3_.refs_5_), channel_id=1, source_target_pairs={{0,64},{8,73},{2,66},{10,75},{4,68},{12,77},{6,70},{14,79},{16,80}... | collective-permute-start | bytes 1769480 | tf_op jit(solution)/shard_map/ppermute | solution.py:30
  32.4 7.7 %collective-permute-start.11 = (bf16[128,1152]{1,0:T(8,128)(2,1)S(1)}, bf16[128,1152]{1,0:T(8,128)(2,1)S(1)}, u32[]{:S(2)}, u32[]{:S(2)}) collective-permute-start(bf16[128,1152]{1,0:T(8,128)(2,1)S(1)} %slice.7), channel_id=1, source_target_pairs={{0,16},{8,10},{2,18},{10,12},{4,20},{12,14},{6,22},{14,8},{16,32},... | collective-permute-start | bytes 884744 | tf_op jit(solution)/shard_map/ppermute | solution.py:30
  33.4 7.0 %collective-permute-start.10 = (bf16[128,1152]{1,0:T(8,128)(2,1)S(1)}, bf16[128,1152]{1,0:T(8,128)(2,1)S(1)}, u32[]{:S(2)}, u32[]{:S(2)}) collective-permute-start(bf16[128,1152]{1,0:T(8,128)(2,1)S(1)} %slice.6), channel_id=1, source_target_pairs={{0,64},{8,73},{2,66},{10,75},{4,68},{12,77},{6,70},{14,79},{16,80}... | collective-permute-start | bytes 884744 | tf_op jit(solution)/shard_map/ppermute | solution.py:30
  35.2 6.1 %collective-permute-start.16 = (bf16[256,1152]{1,0:T(8,128)(2,1)S(1)}, bf16[256,1152]{1,0:T(8,128)(2,1)S(1)}, u32[]{:S(2)}, u32[]{:S(2)}) collective-permute-start(bf16[256,1152]{1,0:T(8,128)(2,1)S(1)} %collective-permute-done.2.refs_3_.refs_4_), channel_id=1, source_target_pairs={{0,8},{8,0},{2,10},{10,2},{4,12},{12,4},{6,14},{14,6},{16,24},{24,... | collective-permute-start | bytes 1769480 | tf_op jit(solution)/shard_map/ppermute | solution.py:30
  35.2 6.1 %collective-permute-start.15 = (bf16[256,1152]{1,0:T(8,128)(2,1)S(1)}, bf16[256,1152]{1,0:T(8,128)(2,1)S(1)}, u32[]{:S(2)}, u32[]{:S(2)}) collective-permute-start(bf16[256,1152]{1,0:T(8,128)(2,1)S(1)} %collective-permute-done.4.refs_2_.refs_3_), channel_id=1, source_target_pairs={{0,8},{8,0},{2,10},{10,2},{4,12},{12,4},{6,14},{14,6},{16,24},{24,... | collective-permute-start | bytes 1769480 | tf_op jit(solution)/shard_map/ppermute | solution.py:30
  35.7 5.6 %collective-permute-start.14 = (bf16[256,1152]{1,0:T(8,128)(2,1)S(1)}, bf16[256,1152]{1,0:T(8,128)(2,1)S(1)}, u32[]{:S(2)}, u32[]{:S(2)}) collective-permute-start(bf16[256,1152]{1,0:T(8,128)(2,1)S(1)} %collective-permute-done.12.refs_1_.refs_2_), channel_id=1, source_target_pairs={{0,8},{8,0},{2,10},{10,2},{4,12},{12,4},{6,14},{14,6},{16,24},{24,... | collective-permute-start | bytes 1769480 | tf_op jit(solution)/shard_map/ppermute | solution.py:30
  40.5 3.5 %collective-permute-start.13 = (bf16[256,1152]{1,0:T(8,128)(2,1)S(1)}, bf16[256,1152]{1,0:T(8,128)(2,1)S(1)}, u32[]{:S(2)}, u32[]{:S(2)}) collective-permute-start(bf16[256,1152]{1,0:T(8,128)(2,1)S(1)} %pack.1.refs_1_), channel_id=1, source_target_pairs={{0,8},{8,0},{2,10},{10,2},{4,12},{12,4},{6,14},{14,6},{16,24},{24,... | collective-permute-start | bytes 1769480 | tf_op jit(solution)/shard_map/ppermute | solution.py:30
  44.9 10.4 %collective-permute-start.17 = (bf16[128,1152]{1,0:T(8,128)(2,1)S(1)}, bf16[128,1152]{1,0:T(8,128)(2,1)S(1)}, u32[]{:S(2)}, u32[]{:S(2)}) collective-permute-start(bf16[128,1152]{1,0:T(8,128)(2,1)S(1)} %get-tuple-element.32), channel_id=1, source_target_pairs={{0,48},{8,14},{2,50},{10,8},{4,52},{12,10},{6,54},{14,12},{16,0},{... | collective-permute-start | bytes 884744 | tf_op jit(solution)/shard_map/ppermute | solution.py:30
  48.1 7.6 %collective-permute-start.18 = (bf16[128,1152]{1,0:T(8,128)(2,1)S(1)}, bf16[128,1152]{1,0:T(8,128)(2,1)S(1)}, u32[]{:S(2)}, u32[]{:S(2)}) collective-permute-start(bf16[128,1152]{1,0:T(8,128)(2,1)S(1)} %get-tuple-element.29.refs_0_), channel_id=1, source_target_pairs={{0,64},{8,73},{2,66},{10,75},{4,68},{12,77},{6,70},{14,79},{16,80}... | collective-permute-start | bytes 884744 | tf_op jit(solution)/shard_map/ppermute | solution.py:30
  54.4 10.3 %collective-permute-start.19 = (bf16[256,1152]{1,0:T(8,128)(2,1)S(1)}, bf16[256,1152]{1,0:T(8,128)(2,1)S(1)}, u32[]{:S(2)}, u32[]{:S(2)}) collective-permute-start(bf16[256,1152]{1,0:T(8,128)(2,1)S(1)} %get-tuple-element.37), channel_id=1, source_target_pairs={{0,64},{8,73},{2,66},{10,75},{4,68},{12,77},{6,70},{14,79},{16,80}... | collective-permute-start | bytes 1769480 | tf_op jit(solution)/shard_map/ppermute | solution.py:30
  55.4 9.5 %collective-permute-start.23 = (bf16[256,1152]{1,0:T(8,128)(2,1)S(1)}, bf16[256,1152]{1,0:T(8,128)(2,1)S(1)}, u32[]{:S(2)}, u32[]{:S(2)}) collective-permute-start(bf16[256,1152]{1,0:T(8,128)(2,1)S(1)} %add_half.2.refs_0_.refs_1_), channel_id=1, source_target_pairs={{0,48},{8,14},{2,50},{10,8},{4,52},{12,10},{6,54},{14,12},{16,0},{... | collective-permute-start | bytes 1769480 | tf_op jit(solution)/shard_map/ppermute | solution.py:30
  55.8 11.0 %collective-permute-start.20 = (bf16[256,1152]{1,0:T(8,128)(2,1)S(1)}, bf16[256,1152]{1,0:T(8,128)(2,1)S(1)}, u32[]{:S(2)}, u32[]{:S(2)}) collective-permute-start(bf16[256,1152]{1,0:T(8,128)(2,1)S(1)} %add_half.3.refs_0_), channel_id=1, source_target_pairs={{0,16},{8,10},{2,18},{10,12},{4,20},{12,14},{6,22},{14,8},{16,32},... | collective-permute-start | bytes 1769480 | tf_op jit(solution)/shard_map/ppermute | solution.py:30
  63.1 9.1 %collective-permute-start.22 = (bf16[256,1152]{1,0:T(8,128)(2,1)S(1)}, bf16[256,1152]{1,0:T(8,128)(2,1)S(1)}, u32[]{:S(2)}, u32[]{:S(2)}) collective-permute-start(bf16[256,1152]{1,0:T(8,128)(2,1)S(1)} %get-tuple-element.38), channel_id=1, source_target_pairs={{0,48},{8,14},{2,50},{10,8},{4,52},{12,10},{6,54},{14,12},{16,0},{... | collective-permute-start | bytes 1769480 | tf_op jit(solution)/shard_map/ppermute | solution.py:30
  64.8 13.6 %copy-start.1 = (bf16[128,1152]{1,0:T(8,128)(2,1)S(1)}, bf16[128,1152]{1,0:T(8,128)(2,1)}, u32[]{:S(2)}) copy-start(bf16[128,1152]{1,0:T(8,128)(2,1)} %picture.1) | copy-start | bytes 884740
  64.8 13.6 %copy-start.3 = (bf16[128,1152]{1,0:T(8,128)(2,1)S(1)}, bf16[128,1152]{1,0:T(8,128)(2,1)}, u32[]{:S(2)}) copy-start(bf16[128,1152]{1,0:T(8,128)(2,1)} %caption.1) | copy-start | bytes 884740
  65.0 10.3 %collective-permute-start.24 = (bf16[256,1152]{1,0:T(8,128)(2,1)S(1)}, bf16[256,1152]{1,0:T(8,128)(2,1)S(1)}, u32[]{:S(2)}, u32[]{:S(2)}) collective-permute-start(bf16[256,1152]{1,0:T(8,128)(2,1)S(1)} %add.5), channel_id=1, source_target_pairs={{0,64},{8,73},{2,66},{10,75},{4,68},{12,77},{6,70},{14,79},{16,80}... | collective-permute-start | bytes 1769480 | tf_op jit(solution)/shard_map/ppermute | solution.py:30
  66.9 10.3 %collective-permute-start.21 = (bf16[256,1152]{1,0:T(8,128)(2,1)S(1)}, bf16[256,1152]{1,0:T(8,128)(2,1)S(1)}, u32[]{:S(2)}, u32[]{:S(2)}) collective-permute-start(bf16[256,1152]{1,0:T(8,128)(2,1)S(1)} %add.4), channel_id=1, source_target_pairs={{0,16},{8,10},{2,18},{10,12},{4,20},{12,14},{6,22},{14,8},{16,32},... | collective-permute-start | bytes 1769480 | tf_op jit(solution)/shard_map/ppermute | solution.py:30
  77.4 2.3 %collective-permute-start.25 = (bf16[128,1152]{1,0:T(8,128)(2,1)S(1)}, bf16[128,1152]{1,0:T(8,128)(2,1)S(1)}, u32[]{:S(2)}, u32[]{:S(2)}) collective-permute-start(bf16[128,1152]{1,0:T(8,128)(2,1)S(1)} %give.1), channel_id=1, source_target_pairs={{0,8},{8,0},{2,10},{10,2},{4,12},{12,4},{6,14},{14,6},{16,24},{24,... | collective-permute-start | bytes 884744 | tf_op jit(solution)/shard_map/ppermute | solution.py:30
